TPU v7x, 32 devices: a whole 2x2x4 slice. The times are simulated.
32 devices in a mesh: section: 4 (over y, core), ctx: 2 (over x), mp: 4 (over z).
Axes of the slice: x: 2, y: 2, z: 4, core: 2. Of those that a mesh axis runs over, the one named last changes fastest.
Arguments:
- query_rows: bfloat16 [4, 512, 4096], P('section', 'ctx', 'mp'), may hold values from -6 to 6
- key_rows: bfloat16 [4, 512, 4096], P('section', 'ctx', 'mp'), may hold values from -6 to 6
- value_rows: bfloat16 [4, 512, 4096], P('section', 'ctx', 'mp'), may hold values from -6 to 6
- long_filter: bfloat16 [4, 512, 4096], P('section', 'ctx', 'mp'), may hold values from -1.1 to 1.1, as said below
- short_filter: float32 [4, 3, 3, 4096], P('section', None, None, 'mp'), may hold values from -3 to 3
- next_weight: bfloat16 [4, 4096, 4096], P('section', 'mp', 'ctx'), may hold values from -0.09375 to 0.09375
Outputs:
- projected: bfloat16 [4, 512, 4096], P('section', 'ctx', 'mp')
Inputs may be any that keep to these rules, and one draw needn't show every extreme that they name: `long_filter`: the filter's entries shrink with the lag at a per-channel rate.
All inputs are finite; a program needn't handle non-finite values.
Results may differ from a plain program's by a relative error of at most 0.0051.
Values may be sent and summed in bfloat16 or wider, within the bound.
No kernel may reach another device: no remote copies, remote signals or barrier semaphores. Data moves between devices by JAX's collectives and lax.ppermute only.
A program may use at most 128 MiB of HBM per device.

v0:
```python
import math

import jax
import jax.numpy as jnp
from jax import lax
from jax.sharding import PartitionSpec as P


def from_behind(value, axis, by):
    count = lax.axis_size(axis)
    pairs = [(i, i + by) for i in range(count) if 0 <= i + by < count]
    return lax.ppermute(value, axis, pairs)


def from_behind_2(value, axis, by):
    count = lax.axis_size(axis)
    return lax.ppermute(value, axis, [(i, (i + by) % count) for i in range(count)])


def phase_table(left, right, modulus):
    product = left[:, None] * right[None, :] % modulus
    angle = product.astype(jnp.float32) * (2.0 * math.pi / modulus)
    return (jnp.cos(angle), jnp.sin(angle))


def contract(pattern, table, data):
    return jnp.einsum(pattern, table, data, precision=lax.Precision.HIGHEST)


def rotate(cos_tab, sin_tab, orient, pattern, real_part, imag_part):
    new_real = contract(pattern, cos_tab, real_part) - orient * contract(
        pattern, sin_tab, imag_part
    )
    new_imag = contract(pattern, cos_tab, imag_part) + orient * contract(
        pattern, sin_tab, real_part
    )
    return (new_real, new_imag)


def transform(real_part, imag_part, orient):
    length = real_part.shape[-2]
    outer_len = math.gcd(length, 2 ** ((length.bit_length() - 1) // 2))
    inner_len = length // outer_len
    leading = real_part.shape[:-2]
    channels = real_part.shape[-1]
    real_part = real_part.reshape(leading + (outer_len, inner_len, channels))
    imag_part = imag_part.reshape(leading + (outer_len, inner_len, channels))
    outer_ids = jnp.arange(outer_len, dtype=jnp.int32)
    inner_ids = jnp.arange(inner_len, dtype=jnp.int32)
    cos_outer, sin_outer = phase_table(outer_ids, outer_ids, outer_len)
    real_part, imag_part = rotate(
        cos_outer, sin_outer, orient, "kn,...nbc->...kbc", real_part, imag_part
    )
    cos_twist, sin_twist = phase_table(outer_ids, inner_ids, length)
    cos_twist = cos_twist[:, :, None]
    sin_twist = sin_twist[:, :, None]
    real_part, imag_part = (
        real_part * cos_twist - orient * imag_part * sin_twist,
        imag_part * cos_twist + orient * real_part * sin_twist,
    )
    cos_inner, sin_inner = phase_table(inner_ids, inner_ids, inner_len)
    real_part, imag_part = rotate(
        cos_inner, sin_inner, orient, "qb,...kbc->...qkc", real_part, imag_part
    )
    return (
        real_part.reshape(leading + (length, channels)),
        imag_part.reshape(leading + (length, channels)),
    )


def on_device(query_rows, key_rows, value_rows, long_filter, short_filter, next_weight):
    blocks = lax.axis_size("ctx")
    query_local = query_rows[0]
    key_local = key_rows[0]
    value_local = value_rows[0]
    tok_dev = query_local.shape[0]
    total = 2 * tok_dev * blocks
    stacked = jnp.stack([query_local[-2:], key_local[-2:], value_local[-2:]])
    carried = from_behind(stacked, "ctx", 1)
    taps = short_filter[0]

    def featurize(branch, current):
        extended = jnp.concatenate([carried[branch], current], axis=0).astype(jnp.float32)
        return (
            taps[branch, 0] * extended[2:]
            + taps[branch, 1] * extended[1:-1]
            + taps[branch, 2] * extended[:-2]
        )

    query_feat = featurize(0, query_local)
    mixed_input = featurize(1, key_local) * featurize(2, value_local)
    pair = jnp.stack([mixed_input, long_filter[0].astype(jnp.float32)])
    whole = lax.all_to_all(pair, "ctx", split_axis=2, concat_axis=1, tiled=True)
    padded = jnp.concatenate([whole, jnp.zeros_like(whole)], axis=1)
    spec_real, spec_imag = transform(padded, jnp.zeros_like(padded), -1.0)
    prod_real = spec_real[0] * spec_real[1] - spec_imag[0] * spec_imag[1]
    prod_imag = spec_real[0] * spec_imag[1] + spec_imag[0] * spec_real[1]
    conv_real, conv_imag = transform(prod_real, prod_imag, 1.0)
    values_out = conv_real[: tok_dev * blocks] / total
    convolved = lax.all_to_all(values_out, "ctx", split_axis=0, concat_axis=1, tiled=True)
    hyena_out = (query_feat * convolved).astype(jnp.bfloat16)
    incoming = from_behind_2(hyena_out, "section", 1)
    weight_local = next_weight[0]
    partial_value = jnp.dot(
        incoming,
        lax.all_gather(weight_local, "ctx", axis=1, tiled=True),
        preferred_element_type=jnp.float32,
    )
    summed = lax.psum_scatter(partial_value, "mp", scatter_dimension=1, tiled=True)
    return summed.astype(jnp.bfloat16)[None]


def solution(mesh):
    in_specs = (
        P("section", "ctx", "mp"),
        P("section", "ctx", "mp"),
        P("section", "ctx", "mp"),
        P("section", "ctx", "mp"),
        P("section", None, None, "mp"),
        P("section", "mp", "ctx"),
    )
    out_specs = P("section", "ctx", "mp")
    return jax.shard_map(
        on_device, mesh=mesh, in_specs=in_specs, out_specs=out_specs, check_vma=False
    )
```

profile of v0, /device:TPU:2, one launch (start us, length us, event | category | flops | bytes accessed | tf_op | source)
XLA Modules:
  0.0 253.9 jit_solution(2815715257579456883)
XLA Ops:
  6.5 0.8 slice.100
  7.4 0.7 slice.101
  8.1 0.7 slice.102
  8.8 1.3 collective-permute-start
  10.1 0.8 copy.119
  11.0 1.1 convert_element_type.87
  12.1 2.3 collective-permute-done
  14.4 0.3 maximum_convert_fusion.1
  14.8 0.7 fusion.43
  15.4 0.1 pad_maximum_fusion
  15.6 2.4 copy.77
  18.0 4.1 %all-to-all-start = ((f32[2,256,1024]{1,0,2:T(2,128)}), f32[2,256,1024]{1,0,2:T(2,128)S(1)}, u32[]{:S(2)}, u32[]{:S(2)}) async-start(f32[2,256,1024]{1,0,2:T(2,128)} %copy.77), calls=%async_computation | async-start | bytes 4194304 | tf_op jit(solution)/shard_map/all_to_all | solution.py:93
  22.1 0.7 all-gather.3.cloned.1.call-update
  22.8 0.1 fusion.77
  22.9 0.1 broadcast_multiply_fusion
  23.1 0.1 fusion.76
  23.3 29.6 %all-to-all-done = f32[2,256,1024]{1,0,2:T(2,128)S(1)} async-done(((f32[2,256,1024]{1,0,2:T(2,128)}), f32[2,256,1024]{1,0,2:T(2,128)S(1)}, u32[]{:S(2)}, u32[]{:S(2)}) %all-to-all-start) | async-done | bytes 2097184 | tf_op jit(solution)/shard_map/all_to_all | solution.py:93
  52.9 1.6 copy.78
  54.5 2.2 copy.79
  56.7 0.5 concatenate.15
  57.2 7.2 %fusion.14 = f32[2,32,512,32]{2,3,1,0:T(8,128)S(1)} fusion(f32[2,32,32,512]{3,2,1,0:T(8,128)S(1)} %bitcast.111), kind=kOutput, calls=%fused_computation.22 | convolution fusion | flops 402667520 | bytes 8388608 | tf_op jit(solution)/shard_map/kn,...nbc->...kbc/dot_general | solution.py:27
  64.4 7.6 %fusion.12 = f32[2,32,512,32]{2,3,1,0:T(8,128)S(1)} fusion(f32[2,32,32,512]{3,2,1,0:T(8,128)S(1)} %bitcast.112), kind=kOutput, calls=%fused_computation.20 | convolution fusion | flops 402667520 | bytes 8388608 | tf_op jit(solution)/shard_map/kn,...nbc->...kbc/dot_general | solution.py:27
  72.0 2.2 multiply_subtract_fusion
  74.2 3.1 %fusion.2 = (f32[2,32,32,512]{3,1,2,0:T(8,128)S(1)}, f32[2,32,32,512]{3,1,2,0:T(8,128)S(1)}) fusion(f32[2,32,512,32]{2,3,1,0:T(8,128)S(1)} %multiply_subtract_fusion, f32[32,32]{0,1:T(8,128)S(1)} %copy.83, f32[32,32]{0,1:T(8,128)S(1)} %copy.81, f32[2,32,512,32]{2,3,1,0:T(8,128)S(1)} %fusion.12), kind=kOutput, calls=%fused_computation.4 | convolution fusion | flops 411056128 | bytes 16785408 | tf_op jit(solution)/shard_map/kn,...nbc->...kbc/dot_general | solution.py:27
  77.3 7.3 %fusion.6 = f32[2,32,512,32]{2,3,1,0:T(8,128)S(1)} fusion(f32[2,32,32,512]{3,1,2,0:T(8,128)S(1)} %get-tuple-element.6), kind=kOutput, calls=%fused_computation.14 | convolution fusion | flops 402667520 | bytes 8388608 | tf_op jit(solution)/shard_map/qb,...kbc->...qkc/dot_general | solution.py:27
  84.6 7.1 %fusion.4 = f32[2,32,512,32]{2,3,1,0:T(8,128)S(1)} fusion(f32[2,32,32,512]{3,1,2,0:T(8,128)S(1)} %get-tuple-element.6), kind=kOutput, calls=%fused_computation.12 | convolution fusion | flops 402667520 | bytes 8388608 | tf_op jit(solution)/shard_map/qb,...kbc->...qkc/dot_general | solution.py:27
  91.7 7.8 %subtract_bitcast_fusion = f32[2,32,32,512]{3,1,2,0:T(8,128)S(1)} fusion(f32[2,32,512,32]{2,3,1,0:T(8,128)S(1)} %fusion.6, f32[2,32,32,512]{3,1,2,0:T(8,128)S(1)} %get-tuple-element.5), kind=kOutput, calls=%fused_computation.9 | convolution fusion | flops 404764672 | bytes 12582912 | tf_op jit(solution)/shard_map/qb,...kbc->...qkc/dot_general | solution.py:27
  99.5 7.5 %add_bitcast_fusion = f32[2,32,32,512]{3,1,2,0:T(8,128)S(1)} fusion(f32[2,32,512,32]{2,3,1,0:T(8,128)S(1)} %fusion.4, f32[2,32,32,512]{3,1,2,0:T(8,128)S(1)} %get-tuple-element.5), kind=kOutput, calls=%fused_computation.8 | convolution fusion | flops 404764672 | bytes 12582912 | tf_op jit(solution)/shard_map/qb,...kbc->...qkc/dot_general | solution.py:27
  107.0 1.0 multiply_subtract_fusion.2
  108.0 2.4 fusion.22
  110.4 2.0 fusion.20
  112.4 2.0 fusion.34
  114.4 2.5 multiply_subtract_fusion.1
  116.9 3.0 %fusion.28 = f32[32,32,512]{2,0,1:T(8,128)S(1)} fusion(f32[32,32,512]{2,0,1:T(8,128)S(1)} %get-tuple-element.10), kind=kOutput, calls=%fused_computation.33 | convolution fusion | flops 201340928 | bytes 4194304 | tf_op jit(solution)/shard_map/qb,...kbc->...qkc/dot_general | solution.py:27
  119.9 3.2 %fusion.30 = f32[32,32,512]{2,0,1:T(8,128)S(1)} fusion(f32[32,32,512]{2,0,1:T(8,128)S(1)} %get-tuple-element.9), kind=kOutput, calls=%fused_computation.35 | convolution fusion | flops 201340928 | bytes 4194304 | tf_op jit(solution)/shard_map/qb,...kbc->...qkc/dot_general | solution.py:27
  123.2 0.3 fusion.40
  123.5 1.7 copy.92
  125.1 5.7 %all-to-all-start.1 = ((f32[2,256,512]{2,1,0:T(8,128)}), f32[2,256,512]{2,1,0:T(8,128)S(1)}, u32[]{:S(2)}, u32[]{:S(2)}) async-start(f32[2,256,512]{2,1,0:T(8,128)} %bitcast.34), calls=%async_computation.1 | async-start | bytes 2097152 | tf_op jit(solution)/shard_map/all_to_all | solution.py:100
  130.8 0.2 copy.76
  131.0 0.2 copy.97
  131.2 0.3 maximum_convert_fusion
  131.5 14.7 %all-to-all-done.1 = f32[2,256,512]{2,1,0:T(8,128)S(1)} async-done(((f32[2,256,512]{2,1,0:T(8,128)}), f32[2,256,512]{2,1,0:T(8,128)S(1)}, u32[]{:S(2)}, u32[]{:S(2)}) %all-to-all-start.1) | async-done | bytes 1048608 | tf_op jit(solution)/shard_map/all_to_all | solution.py:100
  146.3 1.4 copy.93
  147.7 2.3 fusion.49
  150.0 8.6 %collective-permute-done.1 = bf16[256,1024]{0,1:T(8,128)(2,1)S(1)} collective-permute-done((bf16[256,1024]{0,1:T(8,128)(2,1)S(1)}, bf16[256,1024]{0,1:T(8,128)(2,1)S(1)}, u32[]{:S(2)}, u32[]{:S(2)}) %collective-permute-start.1) | collective-permute-done | bytes 524320 | tf_op jit(solution)/shard_map/ppermute | solution.py:17
  158.6 7.7 %fusion = f32[256,4096]{1,0:T(8,128)} fusion(bf16[256,1024]{0,1:T(8,128)(2,1)S(1)} %collective-permute-done.1, bf16[1,1024,4096]{2,1,0:T(8,128)(2,1)} %all-gather.3.cloned.1.call-done), kind=kOutput, calls=%fused_computation | convolution fusion | flops 2147483648 | bytes 13107200 | tf_op jit(solution)/shard_map/dot_general | solution.py:104
  166.3 78.4 %reduce-scatter.2.cloned.1.call-done = f32[256,1024]{1,0:T(8,128)} async-done(((f32[256,4096]{1,0:T(8,128)}), f32[256,1024]{1,0:T(8,128)}) %reduce-scatter.2.cloned.1.call-update) | async-done | bytes 1048592 | tf_op jit(solution)/shard_map/reduce_scatter | solution.py:109
  244.7 2.1 convert_bitcast_fusion
  (17 shorter events, 0.4 us)
Async XLA Ops:
  6.5 7.9 %copy-start.1 = (bf16[1,256,1024]{2,1,0:T(8,128)(2,1)S(1)}, bf16[1,256,1024]{2,1,0:T(8,128)(2,1)}, u32[]{:S(2)}) copy-start(bf16[1,256,1024]{2,1,0:T(8,128)(2,1)} %param.7) | copy-start | bytes 1572868
  6.5 7.9 %copy-start = (bf16[1,256,1024]{2,1,0:T(8,128)(2,1)S(1)}, bf16[1,256,1024]{2,1,0:T(8,128)(2,1)}, u32[]{:S(2)}) copy-start(bf16[1,256,1024]{2,1,0:T(8,128)(2,1)} %param.8) | copy-start | bytes 1572868
  8.8 5.6 %collective-permute-start = (bf16[3,2,1024]{2,1,0:T(2,128)(2,1)S(1)}, bf16[3,2,1024]{2,1,0:T(2,128)(2,1)S(1)}, u32[]{:S(2)}, u32[]{:S(2)}) collective-permute-start(bf16[3,2,1024]{2,1,0:T(2,128)(2,1)S(1)} %pad_maximum_fusion.1), channel_id=1, source_target_pairs={{0,4},{1,5},{2,6},{3,7},{8,12},{9,13},{10,14},{11,15},{16,20},{17,... | collective-permute-start | bytes 36872 | tf_op jit(solution)/shard_map/ppermute | solution.py:12
  18.0 34.9 %all-to-all-start = ((f32[2,256,1024]{1,0,2:T(2,128)}), f32[2,256,1024]{1,0,2:T(2,128)S(1)}, u32[]{:S(2)}, u32[]{:S(2)}) async-start(f32[2,256,1024]{1,0,2:T(2,128)} %copy.77), calls=%async_computation | async-start | bytes 4194304 | tf_op jit(solution)/shard_map/all_to_all | solution.py:93
  22.1 136.5 %all-gather.3.cloned.1.call-start = ((), (), s32[]{:S(2)}) async-start(), calls=%async_computation.4 | async-start | bytes 12582912 | tf_op jit(solution)/shard_map/all_gather | solution.py:106
  123.5 7.3 %copy-start.2 = (bf16[1,256,1024]{2,1,0:T(8,128)(2,1)S(1)}, bf16[1,256,1024]{2,1,0:T(8,128)(2,1)}, u32[]{:S(2)}) copy-start(bf16[1,256,1024]{2,1,0:T(8,128)(2,1)} %param.6) | copy-start | bytes 1572868
  125.1 21.2 %all-to-all-start.1 = ((f32[2,256,512]{2,1,0:T(8,128)}), f32[2,256,512]{2,1,0:T(8,128)S(1)}, u32[]{:S(2)}, u32[]{:S(2)}) async-start(f32[2,256,512]{2,1,0:T(8,128)} %bitcast.34), calls=%async_computation.1 | async-start | bytes 2097152 | tf_op jit(solution)/shard_map/all_to_all | solution.py:100
  130.8 114.0 %reduce-scatter.2.cloned.1.call-start = ((), (), s32[]{:S(2)}) async-start(), calls=%async_computation.3 | async-start | bytes 5242880 | tf_op jit(solution)/shard_map/reduce_scatter | solution.py:109
  149.9 8.7 %collective-permute-start.1 = (bf16[256,1024]{0,1:T(8,128)(2,1)S(1)}, bf16[256,1024]{0,1:T(8,128)(2,1)S(1)}, u32[]{:S(2)}, u32[]{:S(2)}) collective-permute-start(bf16[256,1024]{0,1:T(8,128)(2,1)S(1)} %fusion.49), channel_id=1, source_target_pairs={{0,8},{8,16},{16,24},{24,0},{1,9},{9,17},{17,25},{25,1},{2,10},{10... | collective-permute-start | bytes 1572872 | tf_op jit(solution)/shard_map/ppermute | solution.py:17
Sparse Core Ops, SparseCore 0:
  24.4 116.6 all-gather.2
  166.5 78.2 reduce-scatter.1
where the time goes:
time: 258 us; the launch traced here: 254 us
  waiting for transfers between devices  134 us (52%)
  matrix products  72.6 us (28%)
  between operations  13.8 us (5%)
  local copies, waits for them, and re-layouts  13.4 us (5%)
  starting transfers between devices  11.1 us (4%)
  other arithmetic  8.55 us (3%)
    reduce_scatter x1, waiting for transfers between devices, on_device(): lax.psum_scatter(partial_value, 'mp', scatter_dimension=1, tiled=True)  78.4 us
    dot_general x14, matrix products, contract(): return jnp.einsum(pattern, table, data, precision=lax.Precision.HIGHEST)  64.8 us
    all_to_all x1, waiting for transfers between devices, on_device(): whole = lax.all_to_all(pair, 'ctx', split_axis=2, concat_axis=1, tiled=True)  29.6 us
    all_to_all x1, waiting for transfers between devices, on_device(): lax.all_to_all(values_out, 'ctx', split_axis=0, concat_axis=1, tiled=True)  14.7 us
    ppermute x1, waiting for transfers between devices, from_behind_2(): lax.ppermute(value, axis, [(i, (i + by) % count) for i in range(count)])  8.59 us
    dot_general x1, matrix products, on_device(): jnp.dot(incoming, lax.all_gather(weight_local, 'ctx', axis=1, tiled=True)...  7.73 us
    all_to_all x1, starting transfers between devices, on_device(): lax.all_to_all(values_out, 'ctx', split_axis=0, concat_axis=1, tiled=True)  5.65 us
  transfers between devices with their start and end apart: 6, of which 5 were waited for; matrix products, arithmetic and copies ran while one was open for 31% of the time, Pallas kernels for 0%

commit v1 on v0

--- a/solution.py
+++ b/solution.py
@@ -1,9 +1,286 @@
+import functools
 import math
 
 import jax
 import jax.numpy as jnp
+import ml_dtypes
+import numpy as np
 from jax import lax
+from jax.experimental import pallas as pl
+from jax.experimental.pallas import tpu as pltpu
 from jax.sharding import PartitionSpec as P
+
+F32 = jnp.float32
+BF16 = jnp.bfloat16
+EXTRA = 16
+VMEM_LIMIT = 56 * 2**20
+
+
+def odd_tables(length):
+    k = np.arange(length, dtype=np.int64)[:, None]
+    n = np.arange(length, dtype=np.int64)[None, :]
+    turn = ((2 * k + 1) * n) % (4 * length)
+    angle = turn.astype(np.float64) * (math.pi / (2 * length))
+    forward = np.concatenate([np.cos(angle), np.sin(angle)], axis=0)
+    high = forward.astype(ml_dtypes.bfloat16)
+    low = (forward - high.astype(np.float64)).astype(ml_dtypes.bfloat16)
+    scale = np.float64(1.0 / length)
+    back = forward.T * scale
+    back_high = back.astype(ml_dtypes.bfloat16)
+    back_low = (back - back_high.astype(np.float64)).astype(ml_dtypes.bfloat16)
+    return high, low, back_high, back_low
+
+
+def down(rows, by):
+    index = lax.broadcasted_iota(jnp.int32, rows.shape, 0)
+    return jnp.where(index >= by, pltpu.roll(rows, by, 0), 0.0)
+
+
+def short_filtered(rows, taps):
+    return taps[0:1] * rows + taps[1:2] * down(rows, 1) + taps[2:3] * down(rows, 2)
+
+
+def mix_kernel(place, key_ref, value_ref, taps_ref, send_ref, own_ref):
+    rows, width = own_ref.shape[0] - EXTRA, own_ref.shape[1]
+    for out_ref, half in ((send_ref, 1 - place[0]), (own_ref, place[0])):
+        lanes = pl.ds(pl.multiple_of(half * width, width), width)
+        key = key_ref[:, lanes].astype(F32)
+        value = value_ref[:, lanes].astype(F32)
+        mixed = short_filtered(key, taps_ref[1, :, lanes]) * short_filtered(value, taps_ref[2, :, lanes])
+        out_ref[:rows, :] = mixed.astype(BF16)
+        edges = [key[:2], key[rows - 2 :], value[:2], value[rows - 2 :], jnp.zeros((EXTRA - 8, width), F32)]
+        out_ref[rows:, :] = jnp.concatenate(edges, axis=0).astype(BF16)
+
+
+def filter_kernel(place, own_ref, come_ref, high_ref, low_ref, spec_ref, whole):
+    rows = own_ref.shape[0]
+    whole[pl.ds(pl.multiple_of(place[0] * rows, rows), rows), :] = own_ref[...]
+    whole[pl.ds(pl.multiple_of((1 - place[0]) * rows, rows), rows), :] = come_ref[...]
+    data = whole[...]
+    spec_ref[...] = jnp.dot(high_ref[...], data, preferred_element_type=F32) + jnp.dot(
+        low_ref[...], data, preferred_element_type=F32
+    )
+
+
+def conv_kernel(
+    place, own_ref, come_ref, taps_ref, spec_ref, high_ref, low_ref, back_high_ref, back_low_ref, out_ref, whole
+):
+    rows = own_ref.shape[0] - EXTRA
+    first = place[0] == 0
+    whole[pl.ds(pl.multiple_of(place[0] * rows, rows), rows), :] = own_ref[:rows, :]
+    whole[pl.ds(pl.multiple_of((1 - place[0]) * rows, rows), rows), :] = come_ref[:rows, :]
+    own_edge = own_ref[rows:, :].astype(F32)
+    come_edge = come_ref[rows:, :].astype(F32)
+    before = jnp.where(first, own_edge, come_edge)
+    after = jnp.where(first, come_edge, own_edge)
+
+    def edge_features(branch, base):
+        taps = taps_ref[branch]
+        older, old = before[base + 2 : base + 3], before[base + 3 : base + 4]
+        new, newer = after[base : base + 1], after[base + 1 : base + 2]
+        return (
+            taps[0:1] * new + taps[1:2] * old + taps[2:3] * older,
+            taps[0:1] * newer + taps[1:2] * new + taps[2:3] * old,
+        )
+
+    key_0, key_1 = edge_features(1, 0)
+    value_0, value_1 = edge_features(2, 4)
+    tile = whole[rows : rows + EXTRA, :].astype(F32)
+    index = lax.broadcasted_iota(jnp.int32, tile.shape, 0)
+    tile = jnp.where(index == 0, key_0 * value_0, jnp.where(index == 1, key_1 * value_1, tile))
+    whole[rows : rows + EXTRA, :] = tile.astype(BF16)
+
+    data = whole[...]
+    half = high_ref.shape[0] // 2
+    spec = jnp.dot(high_ref[...], data, preferred_element_type=F32) + jnp.dot(
+        low_ref[...], data, preferred_element_type=F32
+    )
+    cos_a, sin_a = spec[:half], spec[half:]
+    cos_b, sin_b = spec_ref[:half, :], spec_ref[half:, :]
+    product = jnp.concatenate([cos_a * cos_b - sin_a * sin_b, cos_a * sin_b + sin_a * cos_b], axis=0)
+    product_high = product.astype(BF16)
+    product_low = (product - product_high.astype(F32)).astype(BF16)
+    out_ref[...] = (
+        jnp.dot(back_high_ref[...], product_high, preferred_element_type=F32)
+        + jnp.dot(back_low_ref[...], product_high, preferred_element_type=F32)
+        + jnp.dot(back_high_ref[...], product_low, preferred_element_type=F32)
+    )
+
+
+def gate_kernel(place, own_ref, come_ref, taps_ref, conv_ref, out_ref, whole):
+    rows = own_ref.shape[0]
+    whole[pl.ds(pl.multiple_of(place[0] * rows, rows), rows), :] = own_ref[...].astype(F32)
+    whole[pl.ds(pl.multiple_of((1 - place[0]) * rows, rows), rows), :] = come_ref[...].astype(F32)
+    out_ref[...] = (short_filtered(whole[...], taps_ref[0]) * conv_ref[...]).astype(BF16)
+
+
+def project_kernel(place, same_ref, cross_ref, weight_ref, other_ref, own_ref):
+    rows, depth = own_ref.shape[0], same_ref.shape[1]
+    here, there = place[0], 1 - place[0]
+    weight_same = weight_ref[pl.ds(pl.multiple_of(here * depth, depth), depth), :]
+    weight_cross = weight_ref[pl.ds(pl.multiple_of(there * depth, depth), depth), :]
+    for out_ref, which in ((other_ref, there), (own_ref, here)):
+        tokens = pl.ds(pl.multiple_of(which * rows, rows), rows)
+        out_ref[...] = (
+            jnp.dot(same_ref[tokens, :], weight_same, preferred_element_type=F32)
+            + jnp.dot(cross_ref[tokens, :], weight_cross, preferred_element_type=F32)
+        ).astype(out_ref.dtype)
+
+
+def params():
+    return pltpu.CompilerParams(vmem_limit_bytes=VMEM_LIMIT)
+
+
+def cost(flops, bytes_accessed):
+    return pl.CostEstimate(flops=int(flops), bytes_accessed=int(bytes_accessed), transcendentals=0)
+
+
+def shape(dims, dtype):
+    return jax.ShapeDtypeStruct(dims, dtype)
+
+
+def two_by_four(query_rows, key_rows, value_rows, long_filter, short_filter, next_weight):
+    sections = lax.axis_size("section")
+    query, key, value, filt = query_rows[0], key_rows[0], value_rows[0], long_filter[0]
+    taps, weight = short_filter[0], next_weight[0]
+    rows, channels = query.shape
+    width = channels // 2
+    length = 2 * rows
+    columns = weight.shape[1] // 2
+    x = lax.axis_index("ctx")
+    z = lax.axis_index("mp")
+    parity = z % 2
+    place = jnp.stack([x, parity]).astype(jnp.int32)
+    high, low, back_high, back_low = (jnp.asarray(t) for t in odd_tables(length))
+
+    swap = [(0, 1), (1, 0)]
+
+    def other_half(array):
+        return lax.dynamic_slice_in_dim(array, (1 - x) * width, width, axis=1)
+
+    filt_come = lax.ppermute(other_half(filt), "ctx", swap)
+    mixed_send, mixed_own = pl.pallas_call(
+        mix_kernel,
+        grid_spec=pltpu.PrefetchScalarGridSpec(
+            num_scalar_prefetch=1,
+            grid=(1,),
+            in_specs=[
+                pl.BlockSpec((rows, channels), lambda i, p: (0, 0)),
+                pl.BlockSpec((rows, channels), lambda i, p: (0, 0)),
+                pl.BlockSpec((3, 3, channels), lambda i, p: (0, 0, 0)),
+            ],
+            out_specs=[pl.BlockSpec((rows + EXTRA, width), lambda i, p: (0, 0))] * 2,
+        ),
+        out_shape=[shape((rows + EXTRA, width), BF16)] * 2,
+        compiler_params=params(),
+        cost_estimate=cost(rows * channels * 20, rows * channels * 6),
+    )(place, key, value, taps)
+    mixed_come = lax.ppermute(mixed_send, "ctx", swap)
+    query_come = lax.ppermute(other_half(query), "ctx", swap)
+
+    block = min(256, width)
+    steps = width // block
+
+    own_lanes = pl.BlockSpec((rows, block), lambda i, p: (0, p[0] * steps + i))
+    lanes = lambda n: pl.BlockSpec((n, block), lambda i, p: (0, i))
+    taps_lanes = pl.BlockSpec((3, 3, block), lambda i, p: (0, 0, p[0] * steps + i))
+    whole = lambda table: pl.BlockSpec(table.shape, lambda i, p: (0, 0))
+
+    spectrum = pl.pallas_call(
+        filter_kernel,
+        grid_spec=pltpu.PrefetchScalarGridSpec(
+            num_scalar_prefetch=1,
+            grid=(steps,),
+            in_specs=[own_lanes, lanes(rows), whole(high), whole(low)],
+            out_specs=lanes(2 * length),
+            scratch_shapes=[pltpu.VMEM((length, block), BF16)],
+        ),
+        out_shape=shape((2 * length, width), F32),
+        compiler_params=params(),
+        cost_estimate=cost(8 * length * length * width, 8 * length * length + 10 * length * width),
+    )(place, filt, filt_come, high, low)
+    convolved = pl.pallas_call(
+        conv_kernel,
+        grid_spec=pltpu.PrefetchScalarGridSpec(
+            num_scalar_prefetch=1,
+            grid=(steps,),
+            in_specs=[
+                lanes(rows + EXTRA),
+                lanes(rows + EXTRA),
+                taps_lanes,
+                lanes(2 * length),
+                whole(high),
+                whole(low),
+                whole(back_high),
+                whole(back_low),
+            ],
+            out_specs=lanes(length),
+            scratch_shapes=[pltpu.VMEM((length, block), BF16)],
+        ),
+        out_shape=shape((length, width), F32),
+        compiler_params=params(),
+        cost_estimate=cost(20 * length * length * width, 16 * length * length + 14 * length * width),
+    )(place, mixed_own, mixed_come, taps, spectrum, high, low, back_high, back_low)
+    hyena = pl.pallas_call(
+        gate_kernel,
+        grid_spec=pltpu.PrefetchScalarGridSpec(
+            num_scalar_prefetch=1,
+            grid=(steps,),
+            in_specs=[own_lanes, lanes(rows), taps_lanes, lanes(length)],
+            out_specs=lanes(length),
+            scratch_shapes=[pltpu.VMEM((length, block), F32)],
+        ),
+        out_shape=shape((length, width), BF16),
+        compiler_params=params(),
+        cost_estimate=cost(10 * length * width, 8 * length * width),
+    )(place, query, query_come, taps, convolved)
+
+    def to_next(array, flip):
+        pairs = [
+            (s * 2 + c, (s + 1) % sections * 2 + (c + flip) % 2) for s in range(sections) for c in range(2)
+        ]
+        return lax.ppermute(array, ("section", "ctx"), pairs)
+
+    cross = to_next(hyena, 1)
+    same = to_next(hyena, 0)
+
+    tile = min(256, columns)
+    tiles = columns // tile
+
+    def project(flip, own_dtype):
+        pick = lambda p: (p[1] + flip) % 2
+        return pl.pallas_call(
+            project_kernel,
+            grid_spec=pltpu.PrefetchScalarGridSpec(
+                num_scalar_prefetch=1,
+                grid=(tiles,),
+                in_specs=[
+                    pl.BlockSpec((length, width), lambda i, p: (0, 0)),
+                    pl.BlockSpec((length, width), lambda i, p: (0, 0)),
+                    pl.BlockSpec((channels, tile), lambda i, p: (0, pick(p) * tiles + i)),
+                ],
+                out_specs=[pl.BlockSpec((rows, tile), lambda i, p: (0, i))] * 2,
+            ),
+            out_shape=[shape((rows, columns), BF16), shape((rows, columns), own_dtype)],
+            compiler_params=params(),
+            cost_estimate=cost(2 * length * channels * columns, 2 * channels * (columns + length) + 2 * length * columns),
+        )(place, same, cross, weight)
+
+    near = [(i, i ^ 1) for i in range(4)]
+    far = [(i, i ^ 2) for i in range(4)]
+    cross_pass, own_pass = project(1, BF16)
+    behind_pass = lax.ppermute(cross_pass, "ctx", swap)
+    own_near = lax.ppermute(own_pass, "mp", near)
+    cross_keep, own_keep = project(0, F32)
+    behind_keep = lax.ppermute(cross_keep, "ctx", swap)
+    behind_near = lax.ppermute(behind_pass, "mp", near)
+    own_sum = own_keep + own_near.astype(F32)
+    behind_sum = behind_keep.astype(F32) + behind_near.astype(F32)
+    at_home = (z // 2) == x
+    leaving = jnp.where(at_home, behind_sum, own_sum).astype(BF16)
+    arriving = lax.ppermute(leaving, "mp", far)
+    staying = jnp.where(at_home, own_sum, behind_sum)
+    return (staying + arriving.astype(F32)).astype(BF16)[None]
 
 
 def from_behind(value, axis, by):
@@ -68,7 +345,7 @@
     )
 
 
-def on_device(query_rows, key_rows, value_rows, long_filter, short_filter, next_weight):
+def any_mesh(query_rows, key_rows, value_rows, long_filter, short_filter, next_weight):
     blocks = lax.axis_size("ctx")
     query_local = query_rows[0]
     key_local = key_rows[0]
@@ -120,6 +397,7 @@
         P("section", "mp", "ctx"),
     )
     out_specs = P("section", "ctx", "mp")
+    two = mesh.shape["ctx"] == 2 and mesh.shape["mp"] == 4
     return jax.shard_map(
-        on_device, mesh=mesh, in_specs=in_specs, out_specs=out_specs, check_vma=False
-    )
+        two_by_four if two else any_mesh, mesh=mesh, in_specs=in_specs, out_specs=out_specs, check_vma=False
+    )

time: 258 us -> 117 us (0.45)
  the two profiles are of different devices: /device:TPU:2 before, /device:TPU:0 now
where the time goes in v1:
time: 117 us
  waiting for transfers between devices  58.6 us (50%)
  Pallas kernels  32.5 us (28%)
  starting transfers between devices  14.7 us (13%)
  local copies, waits for them, and re-layouts  6.26 us (5%)
  other arithmetic  4.61 us (4%)
    ppermute x1, waiting for transfers between devices, two_by_four(): arriving = lax.ppermute(leaving, 'mp', far)  22.7 us
    ppermute x2, waiting for transfers between devices, to_next(): return lax.ppermute(array, ('section', 'ctx'), pairs)  12.7 us
    pallas_call x2, Pallas kernels, project(): pl.pallas_call(project_kernel, grid_spec=pltpu.PrefetchScalarGridSpec(num...  11.1 us
    pallas_call x1, Pallas kernels, two_by_four(): pl.pallas_call(conv_kernel, grid_spec=pltpu.PrefetchScalarGridSpec(num_sc...  9.66 us
    ppermute x1, waiting for transfers between devices, two_by_four(): behind_keep = lax.ppermute(cross_keep, 'ctx', swap)  9.38 us
    ppermute x1, waiting for transfers between devices, two_by_four(): behind_near = lax.ppermute(behind_pass, 'mp', near)  6.87 us
    ppermute x1, waiting for transfers between devices, two_by_four(): behind_pass = lax.ppermute(cross_pass, 'ctx', swap)  5.81 us
    pallas_call x1, Pallas kernels, two_by_four(): pl.pallas_call(filter_kernel, grid_spec=pltpu.PrefetchScalarGridSpec(num_...  4.95 us
  transfers between devices with their start and end apart: 10, of which 7 were waited for; matrix products, arithmetic and copies ran while one was open for 3% of the time, Pallas kernels for 20%

profile of v1, /device:TPU:0, one launch (start us, length us, event | category | flops | bytes accessed | tf_op | source)
XLA Modules:
  0.0 116.7 jit_solution(596336991543608572)
XLA Ops:
  0.0 1.0 dynamic-slice_bitcast_fusion
  1.0 3.0 %collective-permute-start.2 = (bf16[256,512]{1,0:T(8,128)(2,1)S(1)}, bf16[256,512]{1,0:T(8,128)(2,1)S(1)}, u32[]{:S(2)}, u32[]{:S(2)}) collective-permute-start(bf16[256,512]{1,0:T(8,128)(2,1)S(1)} %dynamic-slice_bitcast_fusion), channel_id=1, source_target_pairs={{0,4},{4,0},{1,5},{5,1},{2,6},{6,2},{3,7},{7,3},{8,12},{12,8},{9,1... | collective-permute-start | bytes 786440 | tf_op jit(solution)/shard_map/ppermute | solution.py:161
  4.0 1.4 %copy.13 = f32[1,3,3,1024]{3,2,0,1:T(4,128)} copy(f32[1,3,3,1024]{3,0,2,1:T(1,128)} %param.14) | data formatting | bytes 73728
  5.4 0.6 pad_add_fusion.place
  6.0 3.4 %shard_map.100 = (bf16[272,512]{1,0:T(8,128)(2,1)}, bf16[272,512]{1,0:T(8,128)(2,1)}) custom-call(s32[2]{0:T(128)} %pad_add_fusion.place, bf16[256,1024]{1,0:T(8,128)(2,1)} %bitcast.20, bf16[256,1024]{1,0:T(8,128)(2,1)} %bitcast.21, f32[3,3,1024]{2,1,0:T(4,128)} %bitcast.22), custom_call_target="tpu_custom_call" | custom-call | flops 5242880 | bytes 1572864 | tf_op jit(solution)/shard_map/pallas_call | solution.py:162
  9.4 0.0 collective-permute-start.1
  9.4 1.0 dynamic-slice_bitcast_fusion.1
  10.4 2.1 %collective-permute-start = (bf16[256,512]{1,0:T(8,128)(2,1)S(1)}, bf16[256,512]{1,0:T(8,128)(2,1)S(1)}, u32[]{:S(2)}, u32[]{:S(2)}) collective-permute-start(bf16[256,512]{1,0:T(8,128)(2,1)S(1)} %dynamic-slice_bitcast_fusion.1), channel_id=1, source_target_pairs={{0,4},{4,0},{1,5},{5,1},{2,6},{6,2},{3,7},{7,3},{8,12},{12,8},{9,1... | collective-permute-start | bytes 786440 | tf_op jit(solution)/shard_map/ppermute | solution.py:179
  12.5 0.0 collective-permute-done.2.come_ref
  12.5 0.0 copy-start.2
  12.5 0.7 copy-done.2
  13.2 4.9 %shard_map.101.spec_ref = f32[1024,512]{1,0:T(8,128)} custom-call(s32[2]{0:T(128)} %pad_add_fusion.place, bf16[256,1024]{1,0:T(8,128)(2,1)} %bitcast.18, bf16[256,512]{1,0:T(8,128)(2,1)} %copy-done.2, bf16[1024,512]{1,0:T(8,128)(2,1)} %constant.49.clone.high_ref, bf16[1024,512]{1,0:T(8,128)(2,1)} %constant.50.clone.low_ref), custom_call_target="tpu_custom_call" | custom-call | flops 1073741824 | bytes 4718592 | tf_op jit(solution)/shard_map/pallas_call | solution.py:189
  18.1 1.1 collective-permute-done.1.come_ref
  19.2 0.0 copy-start.5
  19.2 0.7 copy-done.5
  19.9 9.7 %shard_map.102.conv_ref = f32[512,512]{1,0:T(8,128)} custom-call(s32[2]{0:T(128)} %pad_add_fusion.place, bf16[272,512]{1,0:T(8,128)(2,1)} %get-tuple-element.11.own_ref, bf16[272,512]{1,0:T(8,128)(2,1)} %copy-done.5, f32[3,3,1024]{2,1,0:T(4,128)} %bitcast.23, f32[1024,512]{1,0:T(8,128)} %shard_map.101.spec_ref, bf16[1024,512]{1,0:T(8,128)(2,1)} %constant.49.clone.high_ref, ...), custom_call_target="tpu_custom_call" | custom-call | flops 2684354560 | bytes 7864320 | tf_op jit(solution)/shard_map/pallas_call | solution.py:202
  29.6 0.0 collective-permute-done.come_ref
  29.6 0.0 copy-start.3
  29.6 0.7 copy-done.3
  30.3 3.4 %shard_map.103 = bf16[512,512]{1,0:T(8,128)(2,1)} custom-call(s32[2]{0:T(128)} %pad_add_fusion.place, bf16[256,1024]{1,0:T(8,128)(2,1)} %bitcast.19, bf16[256,512]{1,0:T(8,128)(2,1)} %copy-done.3, f32[3,3,1024]{2,1,0:T(4,128)} %bitcast.24, f32[512,512]{1,0:T(8,128)} %shard_map.102.conv_ref), custom_call_target="tpu_custom_call" | custom-call | flops 2621440 | bytes 2097152 | tf_op jit(solution)/shard_map/pallas_call | solution.py:224
  33.7 0.0 collective-permute-start.3
  33.7 1.8 %collective-permute-start.4 = (bf16[512,512]{1,0:T(8,128)(2,1)}, bf16[512,512]{1,0:T(8,128)(2,1)S(1)}, u32[]{:S(2)}, u32[]{:S(2)}) collective-permute-start(bf16[512,512]{1,0:T(8,128)(2,1)} %shard_map.103), channel_id=1, source_target_pairs={{0,12},{4,8},{8,20},{12,16},{16,28},{20,24},{24,4},{28,0},{1,13},{... | collective-permute-start | bytes 1572872 | tf_op jit(solution)/shard_map/ppermute | solution.py:242
  35.5 12.6 %collective-permute-done.3.same_ref = bf16[512,512]{1,0:T(8,128)(2,1)S(1)} collective-permute-done((bf16[512,512]{1,0:T(8,128)(2,1)}, bf16[512,512]{1,0:T(8,128)(2,1)S(1)}, u32[]{:S(2)}, u32[]{:S(2)}) %collective-permute-start.3) | collective-permute-done | bytes 524320 | tf_op jit(solution)/shard_map/ppermute | solution.py:242
  48.1 0.0 copy-start
  48.1 0.1 collective-permute-done.4.cross_ref
  48.2 0.0 copy-start.1
  48.2 0.7 copy-done
  48.9 0.1 copy-done.1
  49.1 5.5 %shard_map.105 = (bf16[256,1024]{1,0:T(8,128)(2,1)}, bf16[256,1024]{1,0:T(8,128)(2,1)}) custom-call(s32[2]{0:T(128)} %pad_add_fusion.place, bf16[512,512]{1,0:T(8,128)(2,1)} %copy-done, bf16[512,512]{1,0:T(8,128)(2,1)} %copy-done.1, bf16[1024,2048]{1,0:T(8,128)(2,1)} %bitcast.16), custom_call_target="tpu_custom_call" | custom-call | flops 1073741824 | bytes 4194304 | tf_op jit(solution)/shard_map/pallas_call | solution.py:252
  54.5 0.0 copy-start.4
  54.5 1.1 collective-permute-start.7
  55.7 5.6 %shard_map.104 = (bf16[256,1024]{1,0:T(8,128)(2,1)}, f32[256,1024]{1,0:T(8,128)}) custom-call(s32[2]{0:T(128)} %pad_add_fusion.place, bf16[512,512]{1,0:T(8,128)(2,1)} %copy-done, bf16[512,512]{1,0:T(8,128)(2,1)} %copy-done.1, bf16[1024,2048]{1,0:T(8,128)(2,1)} %bitcast.17), custom_call_target="tpu_custom_call" | custom-call | flops 1073741824 | bytes 4194304 | tf_op jit(solution)/shard_map/pallas_call | solution.py:252
  61.3 0.9 collective-permute-start.6
  62.2 0.0 copy-done.4
  62.2 1.6 %collective-permute-start.5 = (bf16[256,1024]{1,0:T(8,128)(2,1)S(1)}, bf16[256,1024]{1,0:T(8,128)(2,1)S(1)}, u32[]{:S(2)}, u32[]{:S(2)}) collective-permute-start(bf16[256,1024]{1,0:T(8,128)(2,1)S(1)} %copy-done.4), channel_id=1, source_target_pairs={{0,1},{1,0},{2,3},{3,2},{4,5},{5,4},{6,7},{7,6},{8,9},{9,8},{10,11... | collective-permute-start | bytes 1572872 | tf_op jit(solution)/shard_map/ppermute | solution.py:273
  63.7 5.8 %collective-permute-done.7 = bf16[256,1024]{1,0:T(8,128)(2,1)S(1)} collective-permute-done((bf16[256,1024]{1,0:T(8,128)(2,1)}, bf16[256,1024]{1,0:T(8,128)(2,1)S(1)}, u32[]{:S(2)}, u32[]{:S(2)}) %collective-permute-start.7) | collective-permute-done | bytes 524320 | tf_op jit(solution)/shard_map/ppermute | solution.py:272
  69.5 1.6 %collective-permute-start.8 = (bf16[256,1024]{1,0:T(8,128)(2,1)S(1)}, bf16[256,1024]{1,0:T(8,128)(2,1)S(1)}, u32[]{:S(2)}, u32[]{:S(2)}) collective-permute-start(bf16[256,1024]{1,0:T(8,128)(2,1)S(1)} %collective-permute-done.7), channel_id=1, source_target_pairs={{0,1},{1,0},{2,3},{3,2},{4,5},{5,4},{6,7},{7,6},{8,9},{9,8},{10,11... | collective-permute-start | bytes 1572872 | tf_op jit(solution)/shard_map/ppermute | solution.py:276
  71.1 9.4 %collective-permute-done.6 = bf16[256,1024]{1,0:T(8,128)(2,1)S(1)} collective-permute-done((bf16[256,1024]{1,0:T(8,128)(2,1)}, bf16[256,1024]{1,0:T(8,128)(2,1)S(1)}, u32[]{:S(2)}, u32[]{:S(2)}) %collective-permute-start.6) | collective-permute-done | bytes 524320 | tf_op jit(solution)/shard_map/ppermute | solution.py:275
  80.5 0.0 collective-permute-done.5
  80.5 6.9 %collective-permute-done.8 = bf16[256,1024]{1,0:T(8,128)(2,1)S(1)} collective-permute-done((bf16[256,1024]{1,0:T(8,128)(2,1)S(1)}, bf16[256,1024]{1,0:T(8,128)(2,1)S(1)}, u32[]{:S(2)}, u32[]{:S(2)}) %collective-permute-start.8) | collective-permute-done | bytes 524320 | tf_op jit(solution)/shard_map/ppermute | solution.py:276
  87.4 1.5 %select_convert_fusion = bf16[256,1024]{1,0:T(8,128)(2,1)S(1)} fusion(bf16[256,1024]{1,0:T(8,128)(2,1)S(1)} %collective-permute-done.8, bf16[256,1024]{1,0:T(8,128)(2,1)S(1)} %collective-permute-done.6, f32[256,1024]{1,0:T(8,128)} %get-tuple-element.13, bf16[256,1024]{1,0:T(8,128)(2,1)S(1)} %collective-permute-done.5, pred[]{:T(512)S(6)} %eq.5), kind=kLoop, calls=%fused_computation.1 | loop fusion | flops 1835008 | bytes 3145729 | tf_op jit(solution)/shard_map/convert_element_type | solution.py:280
  88.9 2.7 %collective-permute-start.9 = (bf16[256,1024]{1,0:T(8,128)(2,1)S(1)}, bf16[256,1024]{1,0:T(8,128)(2,1)S(1)}, u32[]{:S(2)}, u32[]{:S(2)}) collective-permute-start(bf16[256,1024]{1,0:T(8,128)(2,1)S(1)} %select_convert_fusion), channel_id=1, source_target_pairs={{0,2},{1,3},{2,0},{3,1},{4,6},{5,7},{6,4},{7,5},{8,10},{9,11},{10,... | collective-permute-start | bytes 1572872 | tf_op jit(solution)/shard_map/ppermute | solution.py:281
  91.6 22.7 %collective-permute-done.9 = bf16[256,1024]{1,0:T(8,128)(2,1)S(1)} collective-permute-done((bf16[256,1024]{1,0:T(8,128)(2,1)S(1)}, bf16[256,1024]{1,0:T(8,128)(2,1)S(1)}, u32[]{:S(2)}, u32[]{:S(2)}) %collective-permute-start.9) | collective-permute-done | bytes 524320 | tf_op jit(solution)/shard_map/ppermute | solution.py:281
  114.3 2.4 %fusion = bf16[1,256,1024]{2,1,0:T(8,128)(2,1)} fusion(bf16[256,1024]{1,0:T(8,128)(2,1)S(1)} %collective-permute-done.9, bf16[256,1024]{1,0:T(8,128)(2,1)S(1)} %collective-permute-done.8, bf16[256,1024]{1,0:T(8,128)(2,1)S(1)} %collective-permute-done.6, f32[256,1024]{1,0:T(8,128)} %get-tuple-element.13, bf16[256,1024]{1,0:T(8,128)(2,1)S(1)} %collective-permute-done.5, ...), kind=kLoop, calls=%fused_computation.4 | loop fusion | flops 2359296 | bytes 3670017 | tf_op jit(solution)/shard_map/broadcast_in_dim | solution.py:283
Async XLA Ops:
  1.0 11.5 %collective-permute-start.2 = (bf16[256,512]{1,0:T(8,128)(2,1)S(1)}, bf16[256,512]{1,0:T(8,128)(2,1)S(1)}, u32[]{:S(2)}, u32[]{:S(2)}) collective-permute-start(bf16[256,512]{1,0:T(8,128)(2,1)S(1)} %dynamic-slice_bitcast_fusion), channel_id=1, source_target_pairs={{0,4},{4,0},{1,5},{5,1},{2,6},{6,2},{3,7},{7,3},{8,12},{12,8},{9,1... | collective-permute-start | bytes 786440 | tf_op jit(solution)/shard_map/ppermute | solution.py:161
  9.4 9.8 %collective-permute-start.1 = (bf16[272,512]{1,0:T(8,128)(2,1)}, bf16[272,512]{1,0:T(8,128)(2,1)S(1)}, u32[]{:S(2)}, u32[]{:S(2)}) collective-permute-start(bf16[272,512]{1,0:T(8,128)(2,1)} %get-tuple-element.12), channel_id=1, source_target_pairs={{0,4},{4,0},{1,5},{5,1},{2,6},{6,2},{3,7},{7,3},{8,12},{12,8},{9,1... | collective-permute-start | bytes 835592 | tf_op jit(solution)/shard_map/ppermute | solution.py:178
  10.4 19.2 %collective-permute-start = (bf16[256,512]{1,0:T(8,128)(2,1)S(1)}, bf16[256,512]{1,0:T(8,128)(2,1)S(1)}, u32[]{:S(2)}, u32[]{:S(2)}) collective-permute-start(bf16[256,512]{1,0:T(8,128)(2,1)S(1)} %dynamic-slice_bitcast_fusion.1), channel_id=1, source_target_pairs={{0,4},{4,0},{1,5},{5,1},{2,6},{6,2},{3,7},{7,3},{8,12},{12,8},{9,1... | collective-permute-start | bytes 786440 | tf_op jit(solution)/shard_map/ppermute | solution.py:179
  12.5 0.7 copy-start.2
  19.2 0.7 copy-start.5
  29.6 0.7 copy-start.3
  33.7 14.4 %collective-permute-start.3 = (bf16[512,512]{1,0:T(8,128)(2,1)}, bf16[512,512]{1,0:T(8,128)(2,1)S(1)}, u32[]{:S(2)}, u32[]{:S(2)}) collective-permute-start(bf16[512,512]{1,0:T(8,128)(2,1)} %shard_map.103), channel_id=1, source_target_pairs={{0,8},{4,12},{8,16},{12,20},{16,24},{20,28},{24,0},{28,4},{1,9},{5... | collective-permute-start | bytes 1572872 | tf_op jit(solution)/shard_map/ppermute | solution.py:242
  33.7 14.5 %collective-permute-start.4 = (bf16[512,512]{1,0:T(8,128)(2,1)}, bf16[512,512]{1,0:T(8,128)(2,1)S(1)}, u32[]{:S(2)}, u32[]{:S(2)}) collective-permute-start(bf16[512,512]{1,0:T(8,128)(2,1)} %shard_map.103), channel_id=1, source_target_pairs={{0,12},{4,8},{8,20},{12,16},{16,28},{20,24},{24,4},{28,0},{1,13},{... | collective-permute-start | bytes 1572872 | tf_op jit(solution)/shard_map/ppermute | solution.py:242
  48.1 0.8 copy-start
  48.2 0.8 copy-start.1
  54.5 7.6 %copy-start.4 = (bf16[256,1024]{1,0:T(8,128)(2,1)S(1)}, bf16[256,1024]{1,0:T(8,128)(2,1)}, u32[]{:S(2)}) copy-start(bf16[256,1024]{1,0:T(8,128)(2,1)} %get-tuple-element.14) | copy-start | bytes 1572868
  54.5 15.0 %collective-permute-start.7 = (bf16[256,1024]{1,0:T(8,128)(2,1)}, bf16[256,1024]{1,0:T(8,128)(2,1)S(1)}, u32[]{:S(2)}, u32[]{:S(2)}) collective-permute-start(bf16[256,1024]{1,0:T(8,128)(2,1)} %get-tuple-element.16), channel_id=1, source_target_pairs={{0,4},{4,0},{1,5},{5,1},{2,6},{6,2},{3,7},{7,3},{8,12},{12,8},{9,1... | collective-permute-start | bytes 1572872 | tf_op jit(solution)/shard_map/ppermute | solution.py:272
  61.3 19.2 %collective-permute-start.6 = (bf16[256,1024]{1,0:T(8,128)(2,1)}, bf16[256,1024]{1,0:T(8,128)(2,1)S(1)}, u32[]{:S(2)}, u32[]{:S(2)}) collective-permute-start(bf16[256,1024]{1,0:T(8,128)(2,1)} %get-tuple-element.15), channel_id=1, source_target_pairs={{0,4},{4,0},{1,5},{5,1},{2,6},{6,2},{3,7},{7,3},{8,12},{12,8},{9,1... | collective-permute-start | bytes 1572872 | tf_op jit(solution)/shard_map/ppermute | solution.py:275
  62.2 18.3 %collective-permute-start.5 = (bf16[256,1024]{1,0:T(8,128)(2,1)S(1)}, bf16[256,1024]{1,0:T(8,128)(2,1)S(1)}, u32[]{:S(2)}, u32[]{:S(2)}) collective-permute-start(bf16[256,1024]{1,0:T(8,128)(2,1)S(1)} %copy-done.4), channel_id=1, source_target_pairs={{0,1},{1,0},{2,3},{3,2},{4,5},{5,4},{6,7},{7,6},{8,9},{9,8},{10,11... | collective-permute-start | bytes 1572872 | tf_op jit(solution)/shard_map/ppermute | solution.py:273
  69.5 17.8 %collective-permute-start.8 = (bf16[256,1024]{1,0:T(8,128)(2,1)S(1)}, bf16[256,1024]{1,0:T(8,128)(2,1)S(1)}, u32[]{:S(2)}, u32[]{:S(2)}) collective-permute-start(bf16[256,1024]{1,0:T(8,128)(2,1)S(1)} %collective-permute-done.7), channel_id=1, source_target_pairs={{0,1},{1,0},{2,3},{3,2},{4,5},{5,4},{6,7},{7,6},{8,9},{9,8},{10,11... | collective-permute-start | bytes 1572872 | tf_op jit(solution)/shard_map/ppermute | solution.py:276
  88.9 25.3 %collective-permute-start.9 = (bf16[256,1024]{1,0:T(8,128)(2,1)S(1)}, bf16[256,1024]{1,0:T(8,128)(2,1)S(1)}, u32[]{:S(2)}, u32[]{:S(2)}) collective-permute-start(bf16[256,1024]{1,0:T(8,128)(2,1)S(1)} %select_convert_fusion), channel_id=1, source_target_pairs={{0,2},{1,3},{2,0},{3,1},{4,6},{5,7},{6,4},{7,5},{8,10},{9,11},{10,... | collective-permute-start | bytes 1572872 | tf_op jit(solution)/shard_map/ppermute | solution.py:281

commit v2 on v0

--- a/solution.py
+++ b/solution.py
@@ -1,9 +1,268 @@
+import functools
 import math
 
 import jax
 import jax.numpy as jnp
+import ml_dtypes
+import numpy as np
 from jax import lax
+from jax.experimental import pallas as pl
+from jax.experimental.pallas import tpu as pltpu
 from jax.sharding import PartitionSpec as P
+
+F32 = jnp.float32
+BF16 = jnp.bfloat16
+EXTRA = 16
+VMEM_LIMIT = 24 * 2**20
+LANES = 256
+WIDE = 512
+CHUNKS = 2
+
+
+def odd_tables(length):
+    k = np.arange(length, dtype=np.int64)[:, None]
+    n = np.arange(length, dtype=np.int64)[None, :]
+    turn = ((2 * k + 1) * n) % (4 * length)
+    angle = turn.astype(np.float64) * (math.pi / (2 * length))
+    forward = np.concatenate([np.cos(angle), np.sin(angle)], axis=0)
+    high = forward.astype(ml_dtypes.bfloat16)
+    low = (forward - high.astype(np.float64)).astype(ml_dtypes.bfloat16)
+    scale = np.float64(1.0 / length)
+    back = forward.T * scale
+    back_high = back.astype(ml_dtypes.bfloat16)
+    back_low = (back - back_high.astype(np.float64)).astype(ml_dtypes.bfloat16)
+    return high, low, back_high, back_low
+
+
+def down(rows, by):
+    index = lax.broadcasted_iota(jnp.int32, rows.shape, 0)
+    return jnp.where(index >= by, pltpu.roll(rows, by, 0), 0.0)
+
+
+def short_filtered(rows, taps):
+    return taps[0:1] * rows + taps[1:2] * down(rows, 1) + taps[2:3] * down(rows, 2)
+
+
+def span(index, size):
+    return pl.ds(pl.multiple_of(index * size, size), size)
+
+
+def mix_kernel(flip, place, key_ref, value_ref, taps_ref, out_ref):
+    rows, width = out_ref.shape[0] - EXTRA, out_ref.shape[1]
+    half = 1 - place[0] if flip else place[0]
+    for lane in range(0, width, LANES):
+        lanes = pl.ds(pl.multiple_of(half * width + lane, LANES), LANES)
+        key = key_ref[0, :, lanes].astype(F32)
+        value = value_ref[0, :, lanes].astype(F32)
+        mixed = short_filtered(key, taps_ref[1, :, 0, lanes]) * short_filtered(value, taps_ref[2, :, 0, lanes])
+        out_ref[:rows, lane : lane + LANES] = mixed.astype(BF16)
+        edges = [key[:2], key[rows - 2 :], value[:2], value[rows - 2 :], jnp.zeros((EXTRA - 8, LANES), F32)]
+        out_ref[rows:, lane : lane + LANES] = jnp.concatenate(edges, axis=0).astype(BF16)
+
+
+def filter_kernel(place, own_ref, come_ref, high_ref, low_ref, spec_ref, whole):
+    rows, width = come_ref.shape
+    whole[span(place[0], rows), :] = own_ref[0, :, span(place[0], width)]
+    whole[span(1 - place[0], rows), :] = come_ref[...]
+    for lane in range(0, width, WIDE):
+        data = whole[:, lane : lane + WIDE]
+        spec_ref[:, lane : lane + WIDE] = jnp.dot(high_ref[...], data, preferred_element_type=F32) + jnp.dot(
+            low_ref[...], data, preferred_element_type=F32
+        )
+
+
+def conv_kernel(
+    place, own_ref, come_ref, taps_ref, spec_ref, high_ref, low_ref, back_high_ref, back_low_ref, out_ref, whole
+):
+    rows, width = own_ref.shape[0] - EXTRA, own_ref.shape[1]
+    first = place[0] == 0
+    whole[span(place[0], rows), :] = own_ref[:rows, :]
+    whole[span(1 - place[0], rows), :] = come_ref[:rows, :]
+    own_edge = own_ref[rows:, :].astype(F32)
+    come_edge = come_ref[rows:, :].astype(F32)
+    before = jnp.where(first, own_edge, come_edge)
+    after = jnp.where(first, come_edge, own_edge)
+
+    def edge_features(branch, base):
+        taps = taps_ref[branch, :, 0, span(place[0], width)]
+        older, old = before[base + 2 : base + 3], before[base + 3 : base + 4]
+        new, newer = after[base : base + 1], after[base + 1 : base + 2]
+        return (
+            taps[0:1] * new + taps[1:2] * old + taps[2:3] * older,
+            taps[0:1] * newer + taps[1:2] * new + taps[2:3] * old,
+        )
+
+    key_0, key_1 = edge_features(1, 0)
+    value_0, value_1 = edge_features(2, 4)
+    tile = whole[rows : rows + EXTRA, :].astype(F32)
+    index = lax.broadcasted_iota(jnp.int32, tile.shape, 0)
+    tile = jnp.where(index == 0, key_0 * value_0, jnp.where(index == 1, key_1 * value_1, tile))
+    whole[rows : rows + EXTRA, :] = tile.astype(BF16)
+
+    half = high_ref.shape[0] // 2
+    for lane in range(0, width, WIDE):
+        lanes = slice(lane, lane + WIDE)
+        data = whole[:, lanes]
+        spec = jnp.dot(high_ref[...], data, preferred_element_type=F32) + jnp.dot(
+            low_ref[...], data, preferred_element_type=F32
+        )
+        cos_a, sin_a = spec[:half], spec[half:]
+        cos_b, sin_b = spec_ref[:half, lanes], spec_ref[half:, lanes]
+        product = jnp.concatenate([cos_a * cos_b - sin_a * sin_b, cos_a * sin_b + sin_a * cos_b], axis=0)
+        product_high = product.astype(BF16)
+        product_low = (product - product_high.astype(F32)).astype(BF16)
+        out_ref[:, lanes] = (
+            jnp.dot(back_high_ref[...], product_high, preferred_element_type=F32)
+            + jnp.dot(back_low_ref[...], product_high, preferred_element_type=F32)
+            + jnp.dot(back_high_ref[...], product_low, preferred_element_type=F32)
+        )
+
+
+def gate_kernel(place, own_ref, come_ref, taps_ref, conv_ref, here_ref, there_ref, whole):
+    rows, width = come_ref.shape
+    whole[span(place[0], rows), :] = own_ref[0, :, span(place[0], width)].astype(F32)
+    whole[span(1 - place[0], rows), :] = come_ref[...].astype(F32)
+    for lane in range(0, width, LANES):
+        lanes = slice(lane, lane + LANES)
+        taps = taps_ref[0, :, 0, pl.ds(pl.multiple_of(place[0] * width + lane, LANES), LANES)]
+        whole[:, lanes] = short_filtered(whole[:, lanes], taps) * conv_ref[:, lanes]
+    here_ref[...] = whole[span(place[0], rows), :].astype(BF16)
+    there_ref[...] = whole[span(1 - place[0], rows), :].astype(BF16)
+
+
+def project_kernel(place, same_ref, cross_ref, weight_ref, *out_refs):
+    depth = same_ref.shape[1]
+    columns = weight_ref.shape[2] // 2
+    for flip, refs in ((1, out_refs[: len(out_refs) // 2]), (0, out_refs[len(out_refs) // 2 :])):
+        block = lax.rem(place[1] + flip, 2)
+        for tile in range(0, columns, WIDE):
+            lanes = pl.ds(pl.multiple_of(block * columns + tile, WIDE), WIDE)
+            value = jnp.dot(
+                same_ref[...], weight_ref[0, span(place[0], depth), lanes], preferred_element_type=F32
+            ) + jnp.dot(
+                cross_ref[...], weight_ref[0, span(1 - place[0], depth), lanes], preferred_element_type=F32
+            )
+            start = 0
+            for ref in refs:
+                ref[:, tile : tile + WIDE] = value[start : start + ref.shape[0]].astype(ref.dtype)
+                start += ref.shape[0]
+
+
+def add_kernel(start, one_ref, two_ref, sum_ref):
+    rows = slice(start, start + sum_ref.shape[0])
+    sum_ref[...] = (one_ref[rows, :].astype(F32) + two_ref[...].astype(F32)).astype(BF16)
+
+
+def last_kernel(place, own_keep_ref, own_near_ref, own_far_ref, *refs):
+    out_ref, groups = refs[-1], len(refs) // 3
+    size = refs[0].shape[0]
+
+    @pl.when(place[2] == place[0])
+    def _():
+        total = own_keep_ref[...] + own_near_ref[...].astype(F32) + own_far_ref[...].astype(F32)
+        out_ref[0] = total.astype(BF16)
+
+    @pl.when(place[2] != place[0])
+    def _():
+        for c in range(groups):
+            total = sum(ref[...].astype(F32) for ref in refs[3 * c : 3 * c + 3])
+            out_ref[0, c * size : (c + 1) * size, :] = total.astype(BF16)
+
+
+def local(kernel, out_shape, flops, *operands, scratch=()):
+    moved = sum(math.prod(a.shape) * a.dtype.itemsize for a in list(operands) + list(out_shape))
+    memory = [pltpu.SMEM if a.dtype == jnp.int32 else pltpu.VMEM for a in operands]
+    return pl.pallas_call(
+        kernel,
+        out_shape=out_shape,
+        in_specs=[pl.BlockSpec(memory_space=space) for space in memory],
+        out_specs=[pl.BlockSpec(memory_space=pltpu.VMEM)] * len(out_shape),
+        scratch_shapes=list(scratch),
+        compiler_params=pltpu.CompilerParams(vmem_limit_bytes=VMEM_LIMIT),
+        cost_estimate=pl.CostEstimate(flops=int(flops), bytes_accessed=int(moved), transcendentals=0),
+    )(*operands)
+
+
+def shape(dims, dtype):
+    return jax.ShapeDtypeStruct(dims, dtype)
+
+
+def two_by_four(query, key, value, filt, taps, weight):
+    sections = lax.axis_size("section")
+    rows, channels = query.shape[1:]
+    width = channels // 2
+    length = 2 * rows
+    columns = weight.shape[2] // 2
+    x = lax.axis_index("ctx")
+    z = lax.axis_index("mp")
+    taps = jnp.transpose(taps, (1, 2, 0, 3))
+    place = jnp.stack([x, z % 2, z // 2]).astype(jnp.int32)
+    high, low, back_high, back_low = (jnp.asarray(t) for t in odd_tables(length))
+
+    swap = [(0, 1), (1, 0)]
+
+    def other_half(array):
+        return lax.dynamic_slice_in_dim(array[0], (1 - x) * width, width, axis=1)
+
+    filt_come = lax.ppermute(other_half(filt), "ctx", swap)
+    mixed = shape((rows + EXTRA, width), BF16)
+    (mixed_send,) = local(functools.partial(mix_kernel, True), [mixed], 20 * rows * width, place, key, value, taps)
+    mixed_come = lax.ppermute(mixed_send, "ctx", swap)
+    query_come = lax.ppermute(other_half(query), "ctx", swap)
+    (mixed_own,) = local(functools.partial(mix_kernel, False), [mixed], 20 * rows * width, place, key, value, taps)
+
+    square = length * length * width
+    half_bf16, half_f32 = pltpu.VMEM((length, width), BF16), pltpu.VMEM((length, width), F32)
+    (spectrum,) = local(
+        filter_kernel, [shape((2 * length, width), F32)], 8 * square, place, filt, filt_come, high, low,
+        scratch=[half_bf16],
+    )
+    (convolved,) = local(
+        conv_kernel, [shape((length, width), F32)], 20 * square, place, mixed_own, mixed_come, taps, spectrum,
+        high, low, back_high, back_low, scratch=[half_bf16],
+    )
+    here, there = local(
+        gate_kernel, [shape((rows, width), BF16)] * 2, 10 * length * width, place, query, query_come, taps, convolved,
+        scratch=[half_f32],
+    )
+
+    def to_next(array, flip):
+        pairs = [
+            (s * 2 + c, (s + 1) % sections * 2 + (c + flip) % 2) for s in range(sections) for c in range(2)
+        ]
+        return lax.ppermute(array, ("section", "ctx"), pairs)
+
+    cross_other, same_other = to_next(here, 1), to_next(there, 0)
+    cross_own, same_own = to_next(there, 1), to_next(here, 0)
+
+    chunk = rows // CHUNKS
+    parts = [shape((chunk, columns), BF16)] * CHUNKS
+    flops = 4 * rows * channels * columns
+    pieces = local(project_kernel, parts + parts, flops, place, same_other, cross_other, weight)
+    diagonal = [(c * 4 + m, (1 - c) * 4 + (m ^ 1)) for c in range(2) for m in range(4)]
+    near = [(m, m ^ 1) for m in range(4)]
+    far_own = [(c * 4 + m, c * 4 + (m ^ 2)) for c in range(2) for m in range(4) if m // 2 != c]
+    far_cross = [(c * 4 + m, c * 4 + (m ^ 2)) for c in range(2) for m in range(4) if m // 2 == c]
+    near_come, keep_come = [], []
+    for c in range(CHUNKS):
+        near_come.append(lax.ppermute(pieces[c], ("ctx", "mp"), diagonal))
+        keep_come.append(lax.ppermute(pieces[CHUNKS + c], "ctx", swap))
+    same_own, cross_own, pieces = lax.optimization_barrier((same_own, cross_own, pieces))
+    pass_on, own_keep = local(
+        project_kernel, [shape((rows, columns), BF16), shape((rows, columns), F32)], flops,
+        place, same_own, cross_own, weight,
+    )
+    own_near = lax.ppermute(pass_on, "mp", near)
+    (own_sum,) = local(functools.partial(add_kernel, 0), [shape((rows, columns), BF16)], rows * columns, own_keep, own_near)
+    own_far = lax.ppermute(own_sum, ("ctx", "mp"), far_own)
+    groups = []
+    for near_part, keep_part in zip(near_come, keep_come):
+        (part,) = local(functools.partial(add_kernel, 0), [shape((chunk, columns), BF16)], chunk * columns, near_part, keep_part)
+        groups += [near_part, keep_part, lax.ppermute(part, ("ctx", "mp"), far_cross)]
+    (result,) = local(
+        last_kernel, [shape((1, rows, columns), BF16)], 3 * rows * columns, place, own_keep, own_near, own_far, *groups
+    )
+    return result
 
 
 def from_behind(value, axis, by):
@@ -68,7 +327,7 @@
     )
 
 
-def on_device(query_rows, key_rows, value_rows, long_filter, short_filter, next_weight):
+def any_mesh(query_rows, key_rows, value_rows, long_filter, short_filter, next_weight):
     blocks = lax.axis_size("ctx")
     query_local = query_rows[0]
     key_local = key_rows[0]
@@ -120,6 +379,7 @@
         P("section", "mp", "ctx"),
     )
     out_specs = P("section", "ctx", "mp")
+    two = mesh.shape["ctx"] == 2 and mesh.shape["mp"] == 4
     return jax.shard_map(
-        on_device, mesh=mesh, in_specs=in_specs, out_specs=out_specs, check_vma=False
-    )
+        two_by_four if two else any_mesh, mesh=mesh, in_specs=in_specs, out_specs=out_specs, check_vma=False
+    )

time: 258 us -> 89.2 us (0.35); the launches traced: 254 us -> 87.9 us
  waiting for transfers between devices: 134 us -> 46.6 us
  matrix products: 72.6 us -> 0 us
  Pallas kernels: 0 us -> 14.2 us
  between operations: 13.8 us -> 0.19 us
  other arithmetic: 8.55 us -> 0.08 us
  starting transfers between devices: 11.1 us -> 19.5 us
  local copies, waits for them, and re-layouts: 13.4 us -> 7.34 us
    reduce_scatter x1 -> x0, waiting for transfers between devices: 78.4 us -> none  [on_device(): lax.psum_scatter(partial_value, 'mp', scatter_dimension=1, tiled=True)]
    dot_general x15 -> x0, matrix products: 72.6 us -> none  [the longest x14 64.8 us: contract(): return jnp.einsum(pattern, table, data, precision=lax.Precision.HIGHEST)]
    all_to_all x2 -> x0, waiting for transfers between devices: 44.4 us -> none  [the longest x1 29.6 us: on_device(): whole = lax.all_to_all(pair, 'ctx', split_axis=2, concat_axis=1, tiled=True)]
    ppermute x2 -> x15, waiting for transfers between devices: 10.9 us -> 46.6 us  [the longest x2 13.2 us: two_by_four(): near_come.append(lax.ppermute(pieces[c], ('ctx', 'mp'), diagonal))]
    ppermute x2 -> x15, starting transfers between devices: 1.35 us -> 19.5 us  [the longest x1 4.53 us: two_by_four(): own_far = lax.ppermute(own_sum, ('ctx', 'mp'), far_own)]
    pallas_call x0 -> x11, Pallas kernels: none -> 14.2 us  [local(): pl.pallas_call(kernel, out_shape=out_shape, in_specs=[pl.BlockSpec(memory...]
    all_to_all x2 -> x0, starting transfers between devices: 9.75 us -> none  [the longest x1 5.65 us: on_device(): lax.all_to_all(values_out, 'ctx', split_axis=0, concat_axis=1, tiled=True)]
    all_to_all x3 -> x0, local copies, waits for them, and re-layouts: 5.15 us -> none  [the longest x2 3.77 us: on_device(): whole = lax.all_to_all(pair, 'ctx', split_axis=2, concat_axis=1, tiled=True)]
  transfers between devices with their start and end apart: 6 -> 15, of which waited for: 5 -> 12; matrix products, arithmetic and copies ran while one was open for 31% -> 1% of each run, Pallas kernels for 0% -> 11%
where the time goes in v2:
time: 89.2 us; the launch traced here: 87.9 us
  waiting for transfers between devices  46.6 us (52%)
  starting transfers between devices  19.5 us (22%)
  Pallas kernels  14.2 us (16%)
  local copies, waits for them, and re-layouts  7.34 us (8%)
    pallas_call x11, Pallas kernels, local(): pl.pallas_call(kernel, out_shape=out_shape, in_specs=[pl.BlockSpec(memory...  14.2 us
    ppermute x2, waiting for transfers between devices, two_by_four(): near_come.append(lax.ppermute(pieces[c], ('ctx', 'mp'), diagonal))  13.2 us
    ppermute x2, waiting for transfers between devices, two_by_four(): lax.ppermute(part, ('ctx', 'mp'), far_cross)  12.5 us
    ppermute x4, waiting for transfers between devices, to_next(): return lax.ppermute(array, ('section', 'ctx'), pairs)  9.08 us
    ppermute x1, waiting for transfers between devices, two_by_four(): own_near = lax.ppermute(pass_on, 'mp', near)  8.25 us
    unnamed x26, local copies, waits for them, and re-layouts  5.34 us
    ppermute x1, starting transfers between devices, two_by_four(): own_far = lax.ppermute(own_sum, ('ctx', 'mp'), far_own)  4.53 us
    ppermute x4, starting transfers between devices, to_next(): return lax.ppermute(array, ('section', 'ctx'), pairs)  3.54 us
  transfers between devices with their start and end apart: 15, of which 12 were waited for; matrix products, arithmetic and copies ran while one was open for 1% of the time, Pallas kernels for 11%

profile of v2, /device:TPU:2, one launch (start us, length us, event | category | flops | bytes accessed | tf_op | source)
XLA Modules:
  0.0 87.9 jit_solution(6766184295388473231)
XLA Ops:
  0.0 1.0 %dynamic-slice_bitcast_fusion = bf16[256,512]{1,0:T(8,128)(2,1)S(1)} fusion(bf16[1,256,1024]{2,1,0:T(8,128)(2,1)} %own_ref.2, s32[]{:T(128)S(6)} %select_n.17), kind=kLoop, calls=%fused_computation | loop fusion | bytes 524292 | tf_op jit(solution)/shard_map/dynamic_slice | solution.py:205
  1.0 0.0 copy-start.10
  1.1 0.1 collective-permute-start.2
  1.2 0.1 pad_add_fusion.place
  1.2 1.0 %copy-done.1 = bf16[1,256,1024]{2,1,0:T(8,128)(2,1)S(1)} copy-done((bf16[1,256,1024]{2,1,0:T(8,128)(2,1)S(1)}, bf16[1,256,1024]{2,1,0:T(8,128)(2,1)}, u32[]{:S(2)}) %copy-start.1) | copy-done | bytes 524312
  2.3 1.0 %copy-done.2 = bf16[1,256,1024]{2,1,0:T(8,128)(2,1)S(1)} copy-done((bf16[1,256,1024]{2,1,0:T(8,128)(2,1)S(1)}, bf16[1,256,1024]{2,1,0:T(8,128)(2,1)}, u32[]{:S(2)}) %copy-start.2) | copy-done | bytes 524312
  3.3 0.8 copy-done.9
  4.1 0.9 %shard_map.101 = bf16[272,512]{1,0:T(8,128)(2,1)S(1)} custom-call(s32[3]{0:T(128)S(1)} %pad_add_fusion.place, bf16[1,256,1024]{2,1,0:T(8,128)(2,1)S(1)} %copy-done.1, bf16[1,256,1024]{2,1,0:T(8,128)(2,1)S(1)} %copy-done.2, f32[3,3,1,1024]{3,2,1,0:T(1,128)S(1)} %bitcast.8), custom_call_target="tpu_custom_call" | custom-call | flops 2621440 | bytes 1363980 | tf_op jit(solution)/shard_map/pallas_call | solution.py:175
  5.0 2.1 %collective-permute-start.1 = (bf16[272,512]{1,0:T(8,128)(2,1)S(1)}, bf16[272,512]{1,0:T(8,128)(2,1)S(1)}, u32[]{:S(2)}, u32[]{:S(2)}) collective-permute-start(bf16[272,512]{1,0:T(8,128)(2,1)S(1)} %shard_map.101), channel_id=1, source_target_pairs={{0,4},{4,0},{1,5},{5,1},{2,6},{6,2},{3,7},{7,3},{8,12},{12,8},{9,1... | collective-permute-start | bytes 835592 | tf_op jit(solution)/shard_map/ppermute | solution.py:210
  7.1 1.0 %dynamic-slice_bitcast_fusion.1 = bf16[256,512]{1,0:T(8,128)(2,1)S(1)} fusion(bf16[1,256,1024]{2,1,0:T(8,128)(2,1)} %own_ref.3, s32[]{:T(128)S(6)} %select_n.17), kind=kLoop, calls=%fused_computation.1 | loop fusion | bytes 524292 | tf_op jit(solution)/shard_map/dynamic_slice | solution.py:205
  8.0 0.1 collective-permute-start
  8.1 0.9 %shard_map.100.own_ref = bf16[272,512]{1,0:T(8,128)(2,1)S(1)} custom-call(s32[3]{0:T(128)S(1)} %pad_add_fusion.place, bf16[1,256,1024]{2,1,0:T(8,128)(2,1)S(1)} %copy-done.1, bf16[1,256,1024]{2,1,0:T(8,128)(2,1)S(1)} %copy-done.2, f32[3,3,1,1024]{3,2,1,0:T(1,128)S(1)} %bitcast.9), custom_call_target="tpu_custom_call" | custom-call | flops 2621440 | bytes 1363980 | tf_op jit(solution)/shard_map/pallas_call | solution.py:175
  9.1 1.2 %collective-permute-done.2.come_ref = bf16[256,512]{1,0:T(8,128)(2,1)S(1)} collective-permute-done((bf16[256,512]{1,0:T(8,128)(2,1)S(1)}, bf16[256,512]{1,0:T(8,128)(2,1)S(1)}, u32[]{:S(2)}, u32[]{:S(2)}) %collective-permute-start.2) | collective-permute-done | bytes 262176 | tf_op jit(solution)/shard_map/ppermute | solution.py:207
  10.3 1.2 %copy-done.5 = bf16[1024,512]{1,0:T(8,128)(2,1)S(1)} copy-done((bf16[1024,512]{1,0:T(8,128)(2,1)S(1)}, bf16[1024,512]{1,0:T(8,128)(2,1)}, u32[]{:S(2)}) %copy-start.5) | copy-done | bytes 1048600
  11.5 1.2 %copy-done.7 = bf16[1024,512]{1,0:T(8,128)(2,1)S(1)} copy-done((bf16[1024,512]{1,0:T(8,128)(2,1)S(1)}, bf16[1024,512]{1,0:T(8,128)(2,1)}, u32[]{:S(2)}) %copy-start.7) | copy-done | bytes 1048600
  12.8 1.8 %shard_map.102.spec_ref = f32[1024,512]{1,0:T(8,128)S(1)} custom-call(s32[3]{0:T(128)S(1)} %pad_add_fusion.place, bf16[1,256,1024]{2,1,0:T(8,128)(2,1)S(1)} %copy-done.3, bf16[256,512]{1,0:T(8,128)(2,1)S(1)} %collective-permute-done.2.come_ref, bf16[1024,512]{1,0:T(8,128)(2,1)S(1)} %copy-done.5, bf16[1024,512]{1,0:T(8,128)(2,1)S(1)} %copy-done.7), custom_call_target="tpu_custom_call" | custom-call | flops 1073741824 | bytes 4980748 | tf_op jit(solution)/shard_map/pallas_call | solution.py:175
  14.6 0.0 copy-start.4
  14.6 0.0 copy-start
  14.6 1.7 %collective-permute-done.1.come_ref = bf16[272,512]{1,0:T(8,128)(2,1)S(1)} collective-permute-done((bf16[272,512]{1,0:T(8,128)(2,1)S(1)}, bf16[272,512]{1,0:T(8,128)(2,1)S(1)}, u32[]{:S(2)}, u32[]{:S(2)}) %collective-permute-start.1) | collective-permute-done | bytes 278560 | tf_op jit(solution)/shard_map/ppermute | solution.py:210
  16.3 3.7 %shard_map.103.conv_ref = f32[512,512]{1,0:T(8,128)S(1)} custom-call(s32[3]{0:T(128)S(1)} %pad_add_fusion.place, bf16[272,512]{1,0:T(8,128)(2,1)S(1)} %shard_map.100.own_ref, bf16[272,512]{1,0:T(8,128)(2,1)S(1)} %collective-permute-done.1.come_ref, f32[3,3,1,1024]{3,2,1,0:T(1,128)S(1)} %bitcast.10, f32[1024,512]{1,0:T(8,128)S(1)} %shard_map.102.spec_ref, ...), custom_call_target="tpu_custom_call" | custom-call | flops 2684354560 | bytes 7933964 | tf_op jit(solution)/shard_map/pallas_call | solution.py:175
  20.0 0.7 collective-permute-done.come_ref
  20.8 1.4 %shard_map.104 = (bf16[256,512]{1,0:T(8,128)(2,1)S(1)}, bf16[256,512]{1,0:T(8,128)(2,1)S(1)}) custom-call(s32[3]{0:T(128)S(1)} %pad_add_fusion.place, bf16[1,256,1024]{2,1,0:T(8,128)(2,1)S(1)} %copy-done.4, bf16[256,512]{1,0:T(8,128)(2,1)S(1)} %collective-permute-done.come_ref, f32[3,3,1,1024]{3,2,1,0:T(1,128)S(1)} %bitcast.11, ...), custom_call_target="tpu_custom_call" | custom-call | flops 2621440 | bytes 2396172 | tf_op jit(solution)/shard_map/pallas_call | solution.py:175
  22.2 0.1 collective-permute-start.5
  22.2 1.8 %collective-permute-start.6 = (bf16[256,512]{1,0:T(8,128)(2,1)S(1)}, bf16[256,512]{1,0:T(8,128)(2,1)S(1)}, u32[]{:S(2)}, u32[]{:S(2)}) collective-permute-start(bf16[256,512]{1,0:T(8,128)(2,1)S(1)} %get-tuple-element.15), channel_id=1, source_target_pairs={{0,12},{4,8},{8,20},{12,16},{16,28},{20,24},{24,4},{28,0},{1,13},{... | collective-permute-start | bytes 786440 | tf_op jit(solution)/shard_map/ppermute | solution.py:233
  24.0 1.7 %collective-permute-start.4 = (bf16[256,512]{1,0:T(8,128)(2,1)S(1)}, bf16[256,512]{1,0:T(8,128)(2,1)S(1)}, u32[]{:S(2)}, u32[]{:S(2)}) collective-permute-start(bf16[256,512]{1,0:T(8,128)(2,1)S(1)} %get-tuple-element.16), channel_id=1, source_target_pairs={{0,12},{4,8},{8,20},{12,16},{16,28},{20,24},{24,4},{28,0},{1,13},{... | collective-permute-start | bytes 786440 | tf_op jit(solution)/shard_map/ppermute | solution.py:233
  25.7 4.9 %collective-permute-done.5.same_ref = bf16[256,512]{1,0:T(8,128)(2,1)S(1)} collective-permute-done((bf16[256,512]{1,0:T(8,128)(2,1)S(1)}, bf16[256,512]{1,0:T(8,128)(2,1)S(1)}, u32[]{:S(2)}, u32[]{:S(2)}) %collective-permute-start.5) | collective-permute-done | bytes 262176 | tf_op jit(solution)/shard_map/ppermute | solution.py:233
  30.6 0.4 collective-permute-done.6.cross_ref
  31.0 1.8 %shard_map.105 = (bf16[128,1024]{1,0:T(8,128)(2,1)S(1)}, bf16[128,1024]{1,0:T(8,128)(2,1)S(1)}, bf16[128,1024]{1,0:T(8,128)(2,1)S(1)}, bf16[128,1024]{1,0:T(8,128)(2,1)S(1)}) custom-call(s32[3]{0:T(128)S(1)} %pad_add_fusion.place, bf16[256,512]{1,0:T(8,128)(2,1)S(1)} %collective-permute-done.5.same_ref, ...), custom_call_target="tpu_custom_call" | custom-call | flops 1073741824 | bytes 5767180 | tf_op jit(solution)/shard_map/pallas_call | solution.py:175
  32.9 3.4 %collective-permute-done.3.same_ref = bf16[256,512]{1,0:T(8,128)(2,1)S(1)} collective-permute-done((bf16[256,512]{1,0:T(8,128)(2,1)S(1)}, bf16[256,512]{1,0:T(8,128)(2,1)S(1)}, u32[]{:S(2)}, u32[]{:S(2)}) %collective-permute-start.3) | collective-permute-done | bytes 262176 | tf_op jit(solution)/shard_map/ppermute | solution.py:233
  36.2 0.4 collective-permute-done.4.cross_ref
  36.6 1.8 %shard_map.106 = (bf16[256,1024]{1,0:T(8,128)(2,1)S(1)}, f32[256,1024]{1,0:T(8,128)S(1)}) custom-call(s32[3]{0:T(128)S(1)} %pad_add_fusion.place, bf16[256,512]{1,0:T(8,128)(2,1)S(1)} %collective-permute-done.3.same_ref, bf16[256,512]{1,0:T(8,128)(2,1)S(1)} %collective-permute-done.4.cross_ref, bf16[1,1024,2048]{2,1,0:T(8,128)(2,1)S(1)} %copy-done), custom_call_target="tpu_custom_call" | custom-call | flops 1073741824 | bytes 6291468 | tf_op jit(solution)/shard_map/pallas_call | solution.py:175
  38.5 1.6 %collective-permute-start.7 = (bf16[256,1024]{1,0:T(8,128)(2,1)S(1)}, bf16[256,1024]{1,0:T(8,128)(2,1)S(1)}, u32[]{:S(2)}, u32[]{:S(2)}) collective-permute-start(bf16[256,1024]{1,0:T(8,128)(2,1)S(1)} %get-tuple-element.24), channel_id=1, source_target_pairs={{0,1},{1,0},{2,3},{3,2},{4,5},{5,4},{6,7},{7,6},{8,9},{9,8},{10,11... | collective-permute-start | bytes 1572872 | tf_op jit(solution)/shard_map/ppermute | solution.py:255
  40.1 0.6 collective-permute-start.9
  40.8 1.3 %collective-permute-start.10 = (bf16[128,1024]{1,0:T(8,128)(2,1)S(1)}, bf16[128,1024]{1,0:T(8,128)(2,1)S(1)}, u32[]{:S(2)}, u32[]{:S(2)}) collective-permute-start(bf16[128,1024]{1,0:T(8,128)(2,1)S(1)} %get-tuple-element.19), channel_id=1, source_target_pairs={{0,4},{4,0},{1,5},{5,1},{2,6},{6,2},{3,7},{7,3},{8,12},{12,8},{9,1... | collective-permute-start | bytes 786440 | tf_op jit(solution)/shard_map/ppermute | solution.py:249
  42.1 1.6 %collective-permute-start.12 = (bf16[128,1024]{1,0:T(8,128)(2,1)S(1)}, bf16[128,1024]{1,0:T(8,128)(2,1)S(1)}, u32[]{:S(2)}, u32[]{:S(2)}) collective-permute-start(bf16[128,1024]{1,0:T(8,128)(2,1)S(1)} %get-tuple-element.18), channel_id=1, source_target_pairs={{0,5},{1,4},{2,7},{3,6},{4,1},{5,0},{6,3},{7,2},{8,13},{9,12},{10,... | collective-permute-start | bytes 786440 | tf_op jit(solution)/shard_map/ppermute | solution.py:248
  43.6 1.5 %collective-permute-start.13 = (bf16[128,1024]{1,0:T(8,128)(2,1)S(1)}, bf16[128,1024]{1,0:T(8,128)(2,1)S(1)}, u32[]{:S(2)}, u32[]{:S(2)}) collective-permute-start(bf16[128,1024]{1,0:T(8,128)(2,1)S(1)} %get-tuple-element.20), channel_id=1, source_target_pairs={{0,4},{4,0},{1,5},{5,1},{2,6},{6,2},{3,7},{7,3},{8,12},{12,8},{9,1... | collective-permute-start | bytes 786440 | tf_op jit(solution)/shard_map/ppermute | solution.py:249
  45.1 8.3 %collective-permute-done.7.two_ref.own_near_ref = bf16[256,1024]{1,0:T(8,128)(2,1)S(1)} collective-permute-done((bf16[256,1024]{1,0:T(8,128)(2,1)S(1)}, bf16[256,1024]{1,0:T(8,128)(2,1)S(1)}, u32[]{:S(2)}, u32[]{:S(2)}) %collective-permute-start.7) | collective-permute-done | bytes 524320 | tf_op jit(solution)/shard_map/ppermute | solution.py:255
  53.3 0.1 shard_map.107
  53.4 4.5 %collective-permute-start.8 = (bf16[256,1024]{1,0:T(8,128)(2,1)S(1)}, bf16[256,1024]{1,0:T(8,128)(2,1)S(1)}, u32[]{:S(2)}, u32[]{:S(2)}) collective-permute-start(bf16[256,1024]{1,0:T(8,128)(2,1)S(1)} %shard_map.107), channel_id=1, source_target_pairs={{2,0},{3,1},{4,6},{5,7},{10,8},{11,9},{12,14},{13,15},{18,16},{19,... | collective-permute-start | bytes 1572872 | tf_op jit(solution)/shard_map/ppermute | solution.py:257
  58.0 9.4 %collective-permute-done.9.one_ref.refs_0_ = bf16[128,1024]{1,0:T(8,128)(2,1)S(1)} collective-permute-done((bf16[128,1024]{1,0:T(8,128)(2,1)S(1)}, bf16[128,1024]{1,0:T(8,128)(2,1)S(1)}, u32[]{:S(2)}, u32[]{:S(2)}) %collective-permute-start.9) | collective-permute-done | bytes 262176 | tf_op jit(solution)/shard_map/ppermute | solution.py:248
  67.3 0.1 shard_map.108
  67.4 1.3 %collective-permute-start.11 = (bf16[128,1024]{1,0:T(8,128)(2,1)S(1)}, bf16[128,1024]{1,0:T(8,128)(2,1)S(1)}, u32[]{:S(2)}, u32[]{:S(2)}) collective-permute-start(bf16[128,1024]{1,0:T(8,128)(2,1)S(1)} %shard_map.108), channel_id=1, source_target_pairs={{0,2},{1,3},{6,4},{7,5},{8,10},{9,11},{14,12},{15,13},{16,18},{17,... | collective-permute-start | bytes 786440 | tf_op jit(solution)/shard_map/ppermute | solution.py:261
  68.7 3.8 %collective-permute-done.12.one_ref.refs_3_ = bf16[128,1024]{1,0:T(8,128)(2,1)S(1)} collective-permute-done((bf16[128,1024]{1,0:T(8,128)(2,1)S(1)}, bf16[128,1024]{1,0:T(8,128)(2,1)S(1)}, u32[]{:S(2)}, u32[]{:S(2)}) %collective-permute-start.12) | collective-permute-done | bytes 262176 | tf_op jit(solution)/shard_map/ppermute | solution.py:248
  72.5 0.1 shard_map.109
  72.6 1.3 %collective-permute-start.14 = (bf16[128,1024]{1,0:T(8,128)(2,1)S(1)}, bf16[128,1024]{1,0:T(8,128)(2,1)S(1)}, u32[]{:S(2)}, u32[]{:S(2)}) collective-permute-start(bf16[128,1024]{1,0:T(8,128)(2,1)S(1)} %shard_map.109), channel_id=1, source_target_pairs={{0,2},{1,3},{6,4},{7,5},{8,10},{9,11},{14,12},{15,13},{16,18},{17,... | collective-permute-start | bytes 786440 | tf_op jit(solution)/shard_map/ppermute | solution.py:261
  73.9 9.5 %collective-permute-done.11.refs_2_ = bf16[128,1024]{1,0:T(8,128)(2,1)S(1)} collective-permute-done((bf16[128,1024]{1,0:T(8,128)(2,1)S(1)}, bf16[128,1024]{1,0:T(8,128)(2,1)S(1)}, u32[]{:S(2)}, u32[]{:S(2)}) %collective-permute-start.11) | collective-permute-done | bytes 262176 | tf_op jit(solution)/shard_map/ppermute | solution.py:261
  83.3 3.0 %collective-permute-done.14.refs_5_ = bf16[128,1024]{1,0:T(8,128)(2,1)S(1)} collective-permute-done((bf16[128,1024]{1,0:T(8,128)(2,1)S(1)}, bf16[128,1024]{1,0:T(8,128)(2,1)S(1)}, u32[]{:S(2)}, u32[]{:S(2)}) %collective-permute-start.14) | collective-permute-done | bytes 262176 | tf_op jit(solution)/shard_map/ppermute | solution.py:261
  86.3 1.5 %shard_map.110 = bf16[1,256,1024]{2,1,0:T(8,128)(2,1)} custom-call(s32[3]{0:T(128)S(1)} %pad_add_fusion.place, f32[256,1024]{1,0:T(8,128)S(1)} %get-tuple-element.23.one_ref.own_keep_ref, bf16[256,1024]{1,0:T(8,128)(2,1)S(1)} %collective-permute-done.7.two_ref.own_near_ref, bf16[256,1024]{1,0:T(8,128)(2,1)S(1)} %collective-permute-done.8.own_far_ref, ...), custom_call_target="tpu_custom_call" | custom-call | flops 786432 | bytes 4194316 | tf_op jit(solution)/shard_map/pallas_call | solution.py:175
  (22 shorter events, 0.0 us)
Async XLA Ops:
  0.0 10.3 %copy-start.3 = (bf16[1,256,1024]{2,1,0:T(8,128)(2,1)S(1)}, bf16[1,256,1024]{2,1,0:T(8,128)(2,1)}, u32[]{:S(2)}) copy-start(bf16[1,256,1024]{2,1,0:T(8,128)(2,1)} %own_ref.2) | copy-start | bytes 1572868
  1.0 15.2 %copy-start.10 = (f32[1,3,3,1024]{3,0,2,1:T(1,128)S(1)}, f32[1,3,3,1024]{3,0,2,1:T(1,128)}, u32[]{:S(2)}) copy-start(f32[1,3,3,1024]{3,0,2,1:T(1,128)} %param.14) | copy-start | bytes 110596
  1.1 9.3 %collective-permute-start.2 = (bf16[256,512]{1,0:T(8,128)(2,1)S(1)}, bf16[256,512]{1,0:T(8,128)(2,1)S(1)}, u32[]{:S(2)}, u32[]{:S(2)}) collective-permute-start(bf16[256,512]{1,0:T(8,128)(2,1)S(1)} %dynamic-slice_bitcast_fusion), channel_id=1, source_target_pairs={{0,4},{4,0},{1,5},{5,1},{2,6},{6,2},{3,7},{7,3},{8,12},{12,8},{9,1... | collective-permute-start | bytes 786440 | tf_op jit(solution)/shard_map/ppermute | solution.py:207
  1.2 1.0 %copy-start.1 = (bf16[1,256,1024]{2,1,0:T(8,128)(2,1)S(1)}, bf16[1,256,1024]{2,1,0:T(8,128)(2,1)}, u32[]{:S(2)}) copy-start(bf16[1,256,1024]{2,1,0:T(8,128)(2,1)} %key_ref.3) | copy-start | bytes 1572868
  2.3 1.0 %copy-start.2 = (bf16[1,256,1024]{2,1,0:T(8,128)(2,1)S(1)}, bf16[1,256,1024]{2,1,0:T(8,128)(2,1)}, u32[]{:S(2)}) copy-start(bf16[1,256,1024]{2,1,0:T(8,128)(2,1)} %value_ref.3) | copy-start | bytes 1572868
  3.3 0.8 copy-start.9
  4.1 12.2 %copy-start.6 = (bf16[1024,512]{1,0:T(8,128)(2,1)S(1)}, bf16[1024,512]{1,0:T(8,128)(2,1)}, u32[]{:S(2)}) copy-start(bf16[1024,512]{1,0:T(8,128)(2,1)} %constant.49.clone.high_ref) | copy-start | bytes 3145732
  4.1 12.2 %copy-start.8 = (bf16[1024,512]{1,0:T(8,128)(2,1)S(1)}, bf16[1024,512]{1,0:T(8,128)(2,1)}, u32[]{:S(2)}) copy-start(bf16[1024,512]{1,0:T(8,128)(2,1)} %constant.50.clone.low_ref) | copy-start | bytes 3145732
  4.1 12.2 %copy-start.11 = (bf16[512,1024]{1,0:T(8,128)(2,1)S(1)}, bf16[512,1024]{1,0:T(8,128)(2,1)}, u32[]{:S(2)}) copy-start(bf16[512,1024]{1,0:T(8,128)(2,1)} %constant.51.clone.back_high_ref) | copy-start | bytes 3145732
  5.0 11.3 %collective-permute-start.1 = (bf16[272,512]{1,0:T(8,128)(2,1)S(1)}, bf16[272,512]{1,0:T(8,128)(2,1)S(1)}, u32[]{:S(2)}, u32[]{:S(2)}) collective-permute-start(bf16[272,512]{1,0:T(8,128)(2,1)S(1)} %shard_map.101), channel_id=1, source_target_pairs={{0,4},{4,0},{1,5},{5,1},{2,6},{6,2},{3,7},{7,3},{8,12},{12,8},{9,1... | collective-permute-start | bytes 835592 | tf_op jit(solution)/shard_map/ppermute | solution.py:210
  8.0 12.7 %collective-permute-start = (bf16[256,512]{1,0:T(8,128)(2,1)S(1)}, bf16[256,512]{1,0:T(8,128)(2,1)S(1)}, u32[]{:S(2)}, u32[]{:S(2)}) collective-permute-start(bf16[256,512]{1,0:T(8,128)(2,1)S(1)} %dynamic-slice_bitcast_fusion.1), channel_id=1, source_target_pairs={{0,4},{4,0},{1,5},{5,1},{2,6},{6,2},{3,7},{7,3},{8,12},{12,8},{9,1... | collective-permute-start | bytes 786440 | tf_op jit(solution)/shard_map/ppermute | solution.py:211
  10.3 1.2 %copy-start.5 = (bf16[1024,512]{1,0:T(8,128)(2,1)S(1)}, bf16[1024,512]{1,0:T(8,128)(2,1)}, u32[]{:S(2)}) copy-start(bf16[1024,512]{1,0:T(8,128)(2,1)} %constant.49.clone.high_ref) | copy-start | bytes 3145732
  11.5 1.2 %copy-start.7 = (bf16[1024,512]{1,0:T(8,128)(2,1)S(1)}, bf16[1024,512]{1,0:T(8,128)(2,1)}, u32[]{:S(2)}) copy-start(bf16[1024,512]{1,0:T(8,128)(2,1)} %constant.50.clone.low_ref) | copy-start | bytes 3145732
  12.8 3.5 %copy-start.12 = (bf16[512,1024]{1,0:T(8,128)(2,1)S(1)}, bf16[512,1024]{1,0:T(8,128)(2,1)}, u32[]{:S(2)}) copy-start(bf16[512,1024]{1,0:T(8,128)(2,1)} %constant.52.clone.back_low_ref) | copy-start | bytes 3145732
  14.6 6.2 %copy-start.4 = (bf16[1,256,1024]{2,1,0:T(8,128)(2,1)S(1)}, bf16[1,256,1024]{2,1,0:T(8,128)(2,1)}, u32[]{:S(2)}) copy-start(bf16[1,256,1024]{2,1,0:T(8,128)(2,1)} %own_ref.3) | copy-start | bytes 1572868
  14.6 16.4 %copy-start = (bf16[1,1024,2048]{2,1,0:T(8,128)(2,1)S(1)}, bf16[1,1024,2048]{2,1,0:T(8,128)(2,1)}, u32[]{:S(2)}) copy-start(bf16[1,1024,2048]{2,1,0:T(8,128)(2,1)} %weight_ref.3) | copy-start | bytes 12582916
  22.2 8.4 %collective-permute-start.5 = (bf16[256,512]{1,0:T(8,128)(2,1)S(1)}, bf16[256,512]{1,0:T(8,128)(2,1)S(1)}, u32[]{:S(2)}, u32[]{:S(2)}) collective-permute-start(bf16[256,512]{1,0:T(8,128)(2,1)S(1)} %get-tuple-element.16), channel_id=1, source_target_pairs={{0,8},{4,12},{8,16},{12,20},{16,24},{20,28},{24,0},{28,4},{1,9},{5... | collective-permute-start | bytes 786440 | tf_op jit(solution)/shard_map/ppermute | solution.py:233
  22.2 8.8 %collective-permute-start.6 = (bf16[256,512]{1,0:T(8,128)(2,1)S(1)}, bf16[256,512]{1,0:T(8,128)(2,1)S(1)}, u32[]{:S(2)}, u32[]{:S(2)}) collective-permute-start(bf16[256,512]{1,0:T(8,128)(2,1)S(1)} %get-tuple-element.15), channel_id=1, source_target_pairs={{0,12},{4,8},{8,20},{12,16},{16,28},{20,24},{24,4},{28,0},{1,13},{... | collective-permute-start | bytes 786440 | tf_op jit(solution)/shard_map/ppermute | solution.py:233
  24.0 12.2 %collective-permute-start.3 = (bf16[256,512]{1,0:T(8,128)(2,1)S(1)}, bf16[256,512]{1,0:T(8,128)(2,1)S(1)}, u32[]{:S(2)}, u32[]{:S(2)}) collective-permute-start(bf16[256,512]{1,0:T(8,128)(2,1)S(1)} %get-tuple-element.15), channel_id=1, source_target_pairs={{0,8},{4,12},{8,16},{12,20},{16,24},{20,28},{24,0},{28,4},{1,9},{5... | collective-permute-start | bytes 786440 | tf_op jit(solution)/shard_map/ppermute | solution.py:233
  24.0 12.6 %collective-permute-start.4 = (bf16[256,512]{1,0:T(8,128)(2,1)S(1)}, bf16[256,512]{1,0:T(8,128)(2,1)S(1)}, u32[]{:S(2)}, u32[]{:S(2)}) collective-permute-start(bf16[256,512]{1,0:T(8,128)(2,1)S(1)} %get-tuple-element.16), channel_id=1, source_target_pairs={{0,12},{4,8},{8,20},{12,16},{16,28},{20,24},{24,4},{28,0},{1,13},{... | collective-permute-start | bytes 786440 | tf_op jit(solution)/shard_map/ppermute | solution.py:233
  38.5 14.9 %collective-permute-start.7 = (bf16[256,1024]{1,0:T(8,128)(2,1)S(1)}, bf16[256,1024]{1,0:T(8,128)(2,1)S(1)}, u32[]{:S(2)}, u32[]{:S(2)}) collective-permute-start(bf16[256,1024]{1,0:T(8,128)(2,1)S(1)} %get-tuple-element.24), channel_id=1, source_target_pairs={{0,1},{1,0},{2,3},{3,2},{4,5},{5,4},{6,7},{7,6},{8,9},{9,8},{10,11... | collective-permute-start | bytes 1572872 | tf_op jit(solution)/shard_map/ppermute | solution.py:255
  40.1 27.2 %collective-permute-start.9 = (bf16[128,1024]{1,0:T(8,128)(2,1)S(1)}, bf16[128,1024]{1,0:T(8,128)(2,1)S(1)}, u32[]{:S(2)}, u32[]{:S(2)}) collective-permute-start(bf16[128,1024]{1,0:T(8,128)(2,1)S(1)} %get-tuple-element.17), channel_id=1, source_target_pairs={{0,5},{1,4},{2,7},{3,6},{4,1},{5,0},{6,3},{7,2},{8,13},{9,12},{10,... | collective-permute-start | bytes 786440 | tf_op jit(solution)/shard_map/ppermute | solution.py:248
  40.8 26.6 %collective-permute-start.10 = (bf16[128,1024]{1,0:T(8,128)(2,1)S(1)}, bf16[128,1024]{1,0:T(8,128)(2,1)S(1)}, u32[]{:S(2)}, u32[]{:S(2)}) collective-permute-start(bf16[128,1024]{1,0:T(8,128)(2,1)S(1)} %get-tuple-element.19), channel_id=1, source_target_pairs={{0,4},{4,0},{1,5},{5,1},{2,6},{6,2},{3,7},{7,3},{8,12},{12,8},{9,1... | collective-permute-start | bytes 786440 | tf_op jit(solution)/shard_map/ppermute | solution.py:249
  42.1 30.4 %collective-permute-start.12 = (bf16[128,1024]{1,0:T(8,128)(2,1)S(1)}, bf16[128,1024]{1,0:T(8,128)(2,1)S(1)}, u32[]{:S(2)}, u32[]{:S(2)}) collective-permute-start(bf16[128,1024]{1,0:T(8,128)(2,1)S(1)} %get-tuple-element.18), channel_id=1, source_target_pairs={{0,5},{1,4},{2,7},{3,6},{4,1},{5,0},{6,3},{7,2},{8,13},{9,12},{10,... | collective-permute-start | bytes 786440 | tf_op jit(solution)/shard_map/ppermute | solution.py:248
  43.6 28.9 %collective-permute-start.13 = (bf16[128,1024]{1,0:T(8,128)(2,1)S(1)}, bf16[128,1024]{1,0:T(8,128)(2,1)S(1)}, u32[]{:S(2)}, u32[]{:S(2)}) collective-permute-start(bf16[128,1024]{1,0:T(8,128)(2,1)S(1)} %get-tuple-element.20), channel_id=1, source_target_pairs={{0,4},{4,0},{1,5},{5,1},{2,6},{6,2},{3,7},{7,3},{8,12},{12,8},{9,1... | collective-permute-start | bytes 786440 | tf_op jit(solution)/shard_map/ppermute | solution.py:249
  53.4 32.9 %collective-permute-start.8 = (bf16[256,1024]{1,0:T(8,128)(2,1)S(1)}, bf16[256,1024]{1,0:T(8,128)(2,1)S(1)}, u32[]{:S(2)}, u32[]{:S(2)}) collective-permute-start(bf16[256,1024]{1,0:T(8,128)(2,1)S(1)} %shard_map.107), channel_id=1, source_target_pairs={{2,0},{3,1},{4,6},{5,7},{10,8},{11,9},{12,14},{13,15},{18,16},{19,... | collective-permute-start | bytes 1572872 | tf_op jit(solution)/shard_map/ppermute | solution.py:257
  67.4 15.9 %collective-permute-start.11 = (bf16[128,1024]{1,0:T(8,128)(2,1)S(1)}, bf16[128,1024]{1,0:T(8,128)(2,1)S(1)}, u32[]{:S(2)}, u32[]{:S(2)}) collective-permute-start(bf16[128,1024]{1,0:T(8,128)(2,1)S(1)} %shard_map.108), channel_id=1, source_target_pairs={{0,2},{1,3},{6,4},{7,5},{8,10},{9,11},{14,12},{15,13},{16,18},{17,... | collective-permute-start | bytes 786440 | tf_op jit(solution)/shard_map/ppermute | solution.py:261
  72.6 13.8 %collective-permute-start.14 = (bf16[128,1024]{1,0:T(8,128)(2,1)S(1)}, bf16[128,1024]{1,0:T(8,128)(2,1)S(1)}, u32[]{:S(2)}, u32[]{:S(2)}) collective-permute-start(bf16[128,1024]{1,0:T(8,128)(2,1)S(1)} %shard_map.109), channel_id=1, source_target_pairs={{0,2},{1,3},{6,4},{7,5},{8,10},{9,11},{14,12},{15,13},{16,18},{17,... | collective-permute-start | bytes 786440 | tf_op jit(solution)/shard_map/ppermute | solution.py:261

commit v3 on v2

--- a/solution.py
+++ b/solution.py
@@ -16,7 +16,8 @@
 VMEM_LIMIT = 24 * 2**20
 LANES = 256
 WIDE = 512
-CHUNKS = 2
+OWN, CROSS = 2, 2
+ORDER = [(0, 0), (1, 0), (0, 1), (1, 1)]
 
 
 def odd_tables(length):
@@ -148,25 +149,20 @@
                 start += ref.shape[0]
 
 
-def add_kernel(start, one_ref, two_ref, sum_ref):
-    rows = slice(start, start + sum_ref.shape[0])
-    sum_ref[...] = (one_ref[rows, :].astype(F32) + two_ref[...].astype(F32)).astype(BF16)
-
-
-def last_kernel(place, own_keep_ref, own_near_ref, own_far_ref, *refs):
-    out_ref, groups = refs[-1], len(refs) // 3
-    size = refs[0].shape[0]
-
-    @pl.when(place[2] == place[0])
-    def _():
-        total = own_keep_ref[...] + own_near_ref[...].astype(F32) + own_far_ref[...].astype(F32)
-        out_ref[0] = total.astype(BF16)
-
-    @pl.when(place[2] != place[0])
-    def _():
-        for c in range(groups):
-            total = sum(ref[...].astype(F32) for ref in refs[3 * c : 3 * c + 3])
-            out_ref[0, c * size : (c + 1) * size, :] = total.astype(BF16)
+def add_kernel(one_ref, two_ref, sum_ref):
+    sum_ref[...] = (one_ref[...].astype(F32) + two_ref[...].astype(F32)).astype(BF16)
+
+
+def last_kernel(own, place, *refs):
+    out_ref = refs[-1]
+    for at_home, group in ((True, refs[: 3 * own]), (False, refs[3 * own : -1])):
+
+        @pl.when((place[2] == place[0]) == at_home)
+        def _():
+            size = group[0].shape[0]
+            for c in range(len(group) // 3):
+                total = sum(ref[...].astype(F32) for ref in group[3 * c : 3 * c + 3])
+                out_ref[0, c * size : (c + 1) * size, :] = total.astype(BF16)
 
 
 def local(kernel, out_shape, flops, *operands, scratch=()):
@@ -232,35 +228,44 @@
         ]
         return lax.ppermute(array, ("section", "ctx"), pairs)
 
+    cross_own, same_own = to_next(there, 1), to_next(here, 0)
     cross_other, same_other = to_next(here, 1), to_next(there, 0)
-    cross_own, same_own = to_next(there, 1), to_next(here, 0)
-
-    chunk = rows // CHUNKS
-    parts = [shape((chunk, columns), BF16)] * CHUNKS
+
     flops = 4 * rows * channels * columns
-    pieces = local(project_kernel, parts + parts, flops, place, same_other, cross_other, weight)
     diagonal = [(c * 4 + m, (1 - c) * 4 + (m ^ 1)) for c in range(2) for m in range(4)]
     near = [(m, m ^ 1) for m in range(4)]
     far_own = [(c * 4 + m, c * 4 + (m ^ 2)) for c in range(2) for m in range(4) if m // 2 != c]
     far_cross = [(c * 4 + m, c * 4 + (m ^ 2)) for c in range(2) for m in range(4) if m // 2 == c]
-    near_come, keep_come = [], []
-    for c in range(CHUNKS):
-        near_come.append(lax.ppermute(pieces[c], ("ctx", "mp"), diagonal))
-        keep_come.append(lax.ppermute(pieces[CHUNKS + c], "ctx", swap))
-    same_own, cross_own, pieces = lax.optimization_barrier((same_own, cross_own, pieces))
-    pass_on, own_keep = local(
-        project_kernel, [shape((rows, columns), BF16), shape((rows, columns), F32)], flops,
-        place, same_own, cross_own, weight,
-    )
-    own_near = lax.ppermute(pass_on, "mp", near)
-    (own_sum,) = local(functools.partial(add_kernel, 0), [shape((rows, columns), BF16)], rows * columns, own_keep, own_near)
-    own_far = lax.ppermute(own_sum, ("ctx", "mp"), far_own)
+
+    def blocks(count, dtype):
+        return [shape((rows // count, columns), dtype)] * count
+
+    def add(one, two):
+        return local(add_kernel, [shape(one.shape, BF16)], math.prod(one.shape), one, two)[0]
+
+    owned = local(
+        project_kernel, blocks(OWN, BF16) + blocks(OWN, F32), flops, place, same_own, cross_own, weight
+    )
+    same_other, cross_other, owned = lax.optimization_barrier((same_other, cross_other, owned))
+    pieces = local(
+        project_kernel, blocks(CROSS, BF16) + blocks(CROSS, BF16), flops, place, same_other, cross_other, weight
+    )
+    own_near = [lax.ppermute(piece, "mp", near) for piece in owned[:OWN]]
+    near_come = [lax.ppermute(piece, ("ctx", "mp"), diagonal) for piece in pieces[:CROSS]]
+    keep_come = [lax.ppermute(piece, "ctx", swap) for piece in pieces[CROSS:]]
+    pairs = {0: list(zip(owned[OWN:], own_near)), 1: list(zip(near_come, keep_come))}
+    held, sums = None, {}
+    for role, c in ORDER:
+        pair = pairs[role][c]
+        if held is not None:
+            pair = lax.optimization_barrier(pair + (held,))[:2]
+        held = sums[role, c] = add(*pair)
     groups = []
-    for near_part, keep_part in zip(near_come, keep_come):
-        (part,) = local(functools.partial(add_kernel, 0), [shape((chunk, columns), BF16)], chunk * columns, near_part, keep_part)
-        groups += [near_part, keep_part, lax.ppermute(part, ("ctx", "mp"), far_cross)]
+    for role, count, far in ((0, OWN, far_own), (1, CROSS, far_cross)):
+        for c in range(count):
+            groups += [*pairs[role][c], lax.ppermute(sums[role, c], ("ctx", "mp"), far)]
     (result,) = local(
-        last_kernel, [shape((1, rows, columns), BF16)], 3 * rows * columns, place, own_keep, own_near, own_far, *groups
+        functools.partial(last_kernel, OWN), [shape((1, rows, columns), BF16)], 3 * rows * columns, place, *groups
     )
     return result
 

time: 89.2 us -> 83.9 us (0.941)
  waiting for transfers between devices: 46.6 us -> 34.8 us
  starting transfers between devices: 19.5 us -> 26.8 us
    ppermute x8 -> x10, waiting for transfers between devices: 33.9 us -> 22 us  [the longest x4 11.5 us: two_by_four(): groups += [*pairs[role][c], lax.ppermute(sums[role, c], ('ctx', 'mp'), far)]]
    ppermute x8 -> x10, starting transfers between devices: 13.7 us -> 21.2 us  [the longest x4 13.6 us: two_by_four(): groups += [*pairs[role][c], lax.ppermute(sums[role, c], ('ctx', 'mp'), far)]]
    pallas_call x11 -> x12, Pallas kernels: 14.2 us -> 14.2 us  [local(): pl.pallas_call(kernel, out_shape=out_shape, in_specs=[pl.BlockSpec(memory...]
    unnamed x26 -> x24, local copies, waits for them, and re-layouts: 5.34 us -> 5.33 us
  transfers between devices with their start and end apart: 15 -> 17, of which waited for: 12 -> 12; matrix products, arithmetic and copies ran while one was open for 1% -> 1% of each run, Pallas kernels for 11% -> 13%
where the time goes in v3:
time: 83.9 us; the launch traced here: 83.4 us
  waiting for transfers between devices  34.8 us (41%)
  starting transfers between devices  26.8 us (32%)
  Pallas kernels  14.2 us (17%)
  local copies, waits for them, and re-layouts  7.34 us (9%)
    pallas_call x12, Pallas kernels, local(): pl.pallas_call(kernel, out_shape=out_shape, in_specs=[pl.BlockSpec(memory...  14.2 us
    ppermute x4, starting transfers between devices, two_by_four(): groups += [*pairs[role][c], lax.ppermute(sums[role, c], ('ctx', 'mp'), far)]  13.6 us
    ppermute x4, waiting for transfers between devices, two_by_four(): groups += [*pairs[role][c], lax.ppermute(sums[role, c], ('ctx', 'mp'), far)]  11.5 us
    ppermute x2, waiting for transfers between devices, two_by_four(): lax.ppermute(piece, ('ctx', 'mp'), diagonal)  9.64 us
    ppermute x4, waiting for transfers between devices, to_next(): return lax.ppermute(array, ('section', 'ctx'), pairs)  9.15 us
    unnamed x24, local copies, waits for them, and re-layouts  5.33 us
    ppermute x4, starting transfers between devices, to_next(): return lax.ppermute(array, ('section', 'ctx'), pairs)  3.37 us
    ppermute x2, starting transfers between devices, two_by_four(): own_near = [lax.ppermute(piece, 'mp', near) for piece in owned[:OWN]]  3.15 us
  transfers between devices with their start and end apart: 17, of which 12 were waited for; matrix products, arithmetic and copies ran while one was open for 1% of the time, Pallas kernels for 13%

profile of v3, /device:TPU:2, one launch (start us, length us, event | category | flops | bytes accessed | tf_op | source)
XLA Modules:
  0.0 83.4 jit_solution(8488166059275670288)
XLA Ops:
  0.0 1.0 %dynamic-slice_bitcast_fusion = bf16[256,512]{1,0:T(8,128)(2,1)S(1)} fusion(bf16[1,256,1024]{2,1,0:T(8,128)(2,1)} %own_ref.2, s32[]{:T(128)S(6)} %select_n.17), kind=kLoop, calls=%fused_computation | loop fusion | bytes 524292 | tf_op jit(solution)/shard_map/dynamic_slice | solution.py:201
  1.1 0.1 collective-permute-start.2
  1.2 0.1 pad_add_fusion.place
  1.2 1.0 %copy-done.1 = bf16[1,256,1024]{2,1,0:T(8,128)(2,1)S(1)} copy-done((bf16[1,256,1024]{2,1,0:T(8,128)(2,1)S(1)}, bf16[1,256,1024]{2,1,0:T(8,128)(2,1)}, u32[]{:S(2)}) %copy-start.1) | copy-done | bytes 524312
  2.3 1.0 %copy-done.2 = bf16[1,256,1024]{2,1,0:T(8,128)(2,1)S(1)} copy-done((bf16[1,256,1024]{2,1,0:T(8,128)(2,1)S(1)}, bf16[1,256,1024]{2,1,0:T(8,128)(2,1)}, u32[]{:S(2)}) %copy-start.2) | copy-done | bytes 524312
  3.3 0.8 copy-done.8
  4.1 0.9 %shard_map.101 = bf16[272,512]{1,0:T(8,128)(2,1)S(1)} custom-call(s32[3]{0:T(128)S(1)} %pad_add_fusion.place, bf16[1,256,1024]{2,1,0:T(8,128)(2,1)S(1)} %copy-done.1, bf16[1,256,1024]{2,1,0:T(8,128)(2,1)S(1)} %copy-done.2, f32[3,3,1,1024]{3,2,1,0:T(1,128)S(1)} %bitcast.8), custom_call_target="tpu_custom_call" | custom-call | flops 2621440 | bytes 1363980 | tf_op jit(solution)/shard_map/pallas_call | solution.py:171
  5.0 2.1 %collective-permute-start.1 = (bf16[272,512]{1,0:T(8,128)(2,1)S(1)}, bf16[272,512]{1,0:T(8,128)(2,1)S(1)}, u32[]{:S(2)}, u32[]{:S(2)}) collective-permute-start(bf16[272,512]{1,0:T(8,128)(2,1)S(1)} %shard_map.101), channel_id=1, source_target_pairs={{0,4},{4,0},{1,5},{5,1},{2,6},{6,2},{3,7},{7,3},{8,12},{12,8},{9,1... | collective-permute-start | bytes 835592 | tf_op jit(solution)/shard_map/ppermute | solution.py:206
  7.1 1.0 %dynamic-slice_bitcast_fusion.1 = bf16[256,512]{1,0:T(8,128)(2,1)S(1)} fusion(bf16[1,256,1024]{2,1,0:T(8,128)(2,1)} %own_ref.3, s32[]{:T(128)S(6)} %select_n.17), kind=kLoop, calls=%fused_computation.1 | loop fusion | bytes 524292 | tf_op jit(solution)/shard_map/dynamic_slice | solution.py:201
  8.0 0.1 collective-permute-start
  8.1 0.9 %shard_map.100.own_ref = bf16[272,512]{1,0:T(8,128)(2,1)S(1)} custom-call(s32[3]{0:T(128)S(1)} %pad_add_fusion.place, bf16[1,256,1024]{2,1,0:T(8,128)(2,1)S(1)} %copy-done.1, bf16[1,256,1024]{2,1,0:T(8,128)(2,1)S(1)} %copy-done.2, f32[3,3,1,1024]{3,2,1,0:T(1,128)S(1)} %bitcast.9), custom_call_target="tpu_custom_call" | custom-call | flops 2621440 | bytes 1363980 | tf_op jit(solution)/shard_map/pallas_call | solution.py:171
  9.1 1.2 %collective-permute-done.2.come_ref = bf16[256,512]{1,0:T(8,128)(2,1)S(1)} collective-permute-done((bf16[256,512]{1,0:T(8,128)(2,1)S(1)}, bf16[256,512]{1,0:T(8,128)(2,1)S(1)}, u32[]{:S(2)}, u32[]{:S(2)}) %collective-permute-start.2) | collective-permute-done | bytes 262176 | tf_op jit(solution)/shard_map/ppermute | solution.py:203
  10.3 1.2 %copy-done.5 = bf16[1024,512]{1,0:T(8,128)(2,1)S(1)} copy-done((bf16[1024,512]{1,0:T(8,128)(2,1)S(1)}, bf16[1024,512]{1,0:T(8,128)(2,1)}, u32[]{:S(2)}) %copy-start.5) | copy-done | bytes 1048600
  11.5 1.2 %copy-done.7 = bf16[1024,512]{1,0:T(8,128)(2,1)S(1)} copy-done((bf16[1024,512]{1,0:T(8,128)(2,1)S(1)}, bf16[1024,512]{1,0:T(8,128)(2,1)}, u32[]{:S(2)}) %copy-start.7) | copy-done | bytes 1048600
  12.8 1.8 %shard_map.102.spec_ref = f32[1024,512]{1,0:T(8,128)S(1)} custom-call(s32[3]{0:T(128)S(1)} %pad_add_fusion.place, bf16[1,256,1024]{2,1,0:T(8,128)(2,1)S(1)} %copy-done.3, bf16[256,512]{1,0:T(8,128)(2,1)S(1)} %collective-permute-done.2.come_ref, bf16[1024,512]{1,0:T(8,128)(2,1)S(1)} %copy-done.7, bf16[1024,512]{1,0:T(8,128)(2,1)S(1)} %copy-done.5), custom_call_target="tpu_custom_call" | custom-call | flops 1073741824 | bytes 4980748 | tf_op jit(solution)/shard_map/pallas_call | solution.py:171
  14.6 1.7 %collective-permute-done.1.come_ref = bf16[272,512]{1,0:T(8,128)(2,1)S(1)} collective-permute-done((bf16[272,512]{1,0:T(8,128)(2,1)S(1)}, bf16[272,512]{1,0:T(8,128)(2,1)S(1)}, u32[]{:S(2)}, u32[]{:S(2)}) %collective-permute-start.1) | collective-permute-done | bytes 278560 | tf_op jit(solution)/shard_map/ppermute | solution.py:206
  16.3 3.7 %shard_map.103.conv_ref = f32[512,512]{1,0:T(8,128)S(1)} custom-call(s32[3]{0:T(128)S(1)} %pad_add_fusion.place, bf16[272,512]{1,0:T(8,128)(2,1)S(1)} %shard_map.100.own_ref, bf16[272,512]{1,0:T(8,128)(2,1)S(1)} %collective-permute-done.1.come_ref, f32[3,3,1,1024]{3,2,1,0:T(1,128)S(1)} %bitcast.10, f32[1024,512]{1,0:T(8,128)S(1)} %shard_map.102.spec_ref, ...), custom_call_target="tpu_custom_call" | custom-call | flops 2684354560 | bytes 7933964 | tf_op jit(solution)/shard_map/pallas_call | solution.py:171
  20.0 0.7 collective-permute-done.come_ref
  20.8 1.4 %shard_map.104 = (bf16[256,512]{1,0:T(8,128)(2,1)S(1)}, bf16[256,512]{1,0:T(8,128)(2,1)S(1)}) custom-call(s32[3]{0:T(128)S(1)} %pad_add_fusion.place, bf16[1,256,1024]{2,1,0:T(8,128)(2,1)S(1)} %copy-done.4, bf16[256,512]{1,0:T(8,128)(2,1)S(1)} %collective-permute-done.come_ref, f32[3,3,1,1024]{3,2,1,0:T(1,128)S(1)} %bitcast.11, ...), custom_call_target="tpu_custom_call" | custom-call | flops 2621440 | bytes 2396172 | tf_op jit(solution)/shard_map/pallas_call | solution.py:171
  22.2 0.1 collective-permute-start.6
  22.2 1.6 %collective-permute-start.5 = (bf16[256,512]{1,0:T(8,128)(2,1)S(1)}, bf16[256,512]{1,0:T(8,128)(2,1)S(1)}, u32[]{:S(2)}, u32[]{:S(2)}) collective-permute-start(bf16[256,512]{1,0:T(8,128)(2,1)S(1)} %get-tuple-element.28), channel_id=1, source_target_pairs={{0,8},{4,12},{8,16},{12,20},{16,24},{20,28},{24,0},{28,4},{1,9},{5... | collective-permute-start | bytes 786440 | tf_op jit(solution)/shard_map/ppermute | solution.py:229
  23.8 0.1 collective-permute-start.3
  23.9 1.6 %collective-permute-start.4 = (bf16[256,512]{1,0:T(8,128)(2,1)S(1)}, bf16[256,512]{1,0:T(8,128)(2,1)S(1)}, u32[]{:S(2)}, u32[]{:S(2)}) collective-permute-start(bf16[256,512]{1,0:T(8,128)(2,1)S(1)} %get-tuple-element.28), channel_id=1, source_target_pairs={{0,12},{4,8},{8,20},{12,16},{16,28},{20,24},{24,4},{28,0},{1,13},{... | collective-permute-start | bytes 786440 | tf_op jit(solution)/shard_map/ppermute | solution.py:229
  25.5 6.1 %collective-permute-done.6.cross_ref = bf16[256,512]{1,0:T(8,128)(2,1)S(1)} collective-permute-done((bf16[256,512]{1,0:T(8,128)(2,1)S(1)}, bf16[256,512]{1,0:T(8,128)(2,1)S(1)}, u32[]{:S(2)}, u32[]{:S(2)}) %collective-permute-start.6) | collective-permute-done | bytes 262176 | tf_op jit(solution)/shard_map/ppermute | solution.py:229
  31.7 1.8 %shard_map.105 = (bf16[128,1024]{1,0:T(8,128)(2,1)S(1)}, bf16[128,1024]{1,0:T(8,128)(2,1)S(1)}, f32[128,1024]{1,0:T(8,128)S(1)}, f32[128,1024]{1,0:T(8,128)S(1)}) custom-call(s32[3]{0:T(128)S(1)} %pad_add_fusion.place, bf16[256,512]{1,0:T(8,128)(2,1)S(1)} %collective-permute-done.5.same_ref, bf16[256,512]{1,0:T(8,128)(2,1)S(1)} %collective-permute-done.6.cross_ref, ...), custom_call_target="tpu_custom_call" | custom-call | flops 1073741824 | bytes 6291468 | tf_op jit(solution)/shard_map/pallas_call | solution.py:171
  33.5 2.2 %collective-permute-done.3.same_ref = bf16[256,512]{1,0:T(8,128)(2,1)S(1)} collective-permute-done((bf16[256,512]{1,0:T(8,128)(2,1)S(1)}, bf16[256,512]{1,0:T(8,128)(2,1)S(1)}, u32[]{:S(2)}, u32[]{:S(2)}) %collective-permute-start.3) | collective-permute-done | bytes 262176 | tf_op jit(solution)/shard_map/ppermute | solution.py:229
  35.7 0.8 %collective-permute-done.4.cross_ref = bf16[256,512]{1,0:T(8,128)(2,1)S(1)} collective-permute-done((bf16[256,512]{1,0:T(8,128)(2,1)S(1)}, bf16[256,512]{1,0:T(8,128)(2,1)S(1)}, u32[]{:S(2)}, u32[]{:S(2)}) %collective-permute-start.4) | collective-permute-done | bytes 262176 | tf_op jit(solution)/shard_map/ppermute | solution.py:229
  36.5 1.6 %collective-permute-start.7 = (bf16[128,1024]{1,0:T(8,128)(2,1)S(1)}, bf16[128,1024]{1,0:T(8,128)(2,1)S(1)}, u32[]{:S(2)}, u32[]{:S(2)}) collective-permute-start(bf16[128,1024]{1,0:T(8,128)(2,1)S(1)} %get-tuple-element.34), channel_id=1, source_target_pairs={{0,1},{1,0},{2,3},{3,2},{4,5},{5,4},{6,7},{7,6},{8,9},{9,8},{10,11... | collective-permute-start | bytes 786440 | tf_op jit(solution)/shard_map/ppermute | solution.py:253
  38.1 1.8 %shard_map.107 = (bf16[128,1024]{1,0:T(8,128)(2,1)S(1)}, bf16[128,1024]{1,0:T(8,128)(2,1)S(1)}, bf16[128,1024]{1,0:T(8,128)(2,1)S(1)}, bf16[128,1024]{1,0:T(8,128)(2,1)S(1)}) custom-call(s32[3]{0:T(128)S(1)} %pad_add_fusion.place, bf16[256,512]{1,0:T(8,128)(2,1)S(1)} %collective-permute-done.3.same_ref, ...), custom_call_target="tpu_custom_call" | custom-call | flops 1073741824 | bytes 5767180 | tf_op jit(solution)/shard_map/pallas_call | solution.py:171
  40.0 1.0 %collective-permute-start.10 = (bf16[128,1024]{1,0:T(8,128)(2,1)S(1)}, bf16[128,1024]{1,0:T(8,128)(2,1)S(1)}, u32[]{:S(2)}, u32[]{:S(2)}) collective-permute-start(bf16[128,1024]{1,0:T(8,128)(2,1)S(1)} %get-tuple-element.39), channel_id=1, source_target_pairs={{0,5},{1,4},{2,7},{3,6},{4,1},{5,0},{6,3},{7,2},{8,13},{9,12},{10,... | collective-permute-start | bytes 786440 | tf_op jit(solution)/shard_map/ppermute | solution.py:254
  41.0 0.9 %collective-permute-start.11 = (bf16[128,1024]{1,0:T(8,128)(2,1)S(1)}, bf16[128,1024]{1,0:T(8,128)(2,1)S(1)}, u32[]{:S(2)}, u32[]{:S(2)}) collective-permute-start(bf16[128,1024]{1,0:T(8,128)(2,1)S(1)} %get-tuple-element.40), channel_id=1, source_target_pairs={{0,4},{4,0},{1,5},{5,1},{2,6},{6,2},{3,7},{7,3},{8,12},{12,8},{9,1... | collective-permute-start | bytes 786440 | tf_op jit(solution)/shard_map/ppermute | solution.py:255
  41.9 1.6 %collective-permute-start.9 = (bf16[128,1024]{1,0:T(8,128)(2,1)S(1)}, bf16[128,1024]{1,0:T(8,128)(2,1)S(1)}, u32[]{:S(2)}, u32[]{:S(2)}) collective-permute-start(bf16[128,1024]{1,0:T(8,128)(2,1)S(1)} %get-tuple-element.36), channel_id=1, source_target_pairs={{0,1},{1,0},{2,3},{3,2},{4,5},{5,4},{6,7},{7,6},{8,9},{9,8},{10,11... | collective-permute-start | bytes 786440 | tf_op jit(solution)/shard_map/ppermute | solution.py:253
  43.5 1.0 %collective-permute-start.14 = (bf16[128,1024]{1,0:T(8,128)(2,1)S(1)}, bf16[128,1024]{1,0:T(8,128)(2,1)S(1)}, u32[]{:S(2)}, u32[]{:S(2)}) collective-permute-start(bf16[128,1024]{1,0:T(8,128)(2,1)S(1)} %get-tuple-element.45), channel_id=1, source_target_pairs={{0,5},{1,4},{2,7},{3,6},{4,1},{5,0},{6,3},{7,2},{8,13},{9,12},{10,... | collective-permute-start | bytes 786440 | tf_op jit(solution)/shard_map/ppermute | solution.py:254
  44.5 0.9 %collective-permute-done.7.two_ref.refs_1_ = bf16[128,1024]{1,0:T(8,128)(2,1)S(1)} collective-permute-done((bf16[128,1024]{1,0:T(8,128)(2,1)S(1)}, bf16[128,1024]{1,0:T(8,128)(2,1)S(1)}, u32[]{:S(2)}, u32[]{:S(2)}) %collective-permute-start.7) | collective-permute-done | bytes 262176 | tf_op jit(solution)/shard_map/ppermute | solution.py:253
  45.4 1.5 %collective-permute-start.15 = (bf16[128,1024]{1,0:T(8,128)(2,1)S(1)}, bf16[128,1024]{1,0:T(8,128)(2,1)S(1)}, u32[]{:S(2)}, u32[]{:S(2)}) collective-permute-start(bf16[128,1024]{1,0:T(8,128)(2,1)S(1)} %get-tuple-element.46), channel_id=1, source_target_pairs={{0,4},{4,0},{1,5},{5,1},{2,6},{6,2},{3,7},{7,3},{8,12},{12,8},{9,1... | collective-permute-start | bytes 786440 | tf_op jit(solution)/shard_map/ppermute | solution.py:255
  46.9 5.0 %collective-permute-done.10.one_ref.refs_6_ = bf16[128,1024]{1,0:T(8,128)(2,1)S(1)} collective-permute-done((bf16[128,1024]{1,0:T(8,128)(2,1)S(1)}, bf16[128,1024]{1,0:T(8,128)(2,1)S(1)}, u32[]{:S(2)}, u32[]{:S(2)}) %collective-permute-start.10) | collective-permute-done | bytes 262176 | tf_op jit(solution)/shard_map/ppermute | solution.py:254
  52.0 4.8 %collective-permute-start.8 = (bf16[128,1024]{1,0:T(8,128)(2,1)S(1)}, bf16[128,1024]{1,0:T(8,128)(2,1)S(1)}, u32[]{:S(2)}, u32[]{:S(2)}) collective-permute-start(bf16[128,1024]{1,0:T(8,128)(2,1)S(1)} %shard_map.106), channel_id=1, source_target_pairs={{2,0},{3,1},{4,6},{5,7},{10,8},{11,9},{12,14},{13,15},{18,16},{19,... | collective-permute-start | bytes 786440 | tf_op jit(solution)/shard_map/ppermute | solution.py:266
  56.7 0.1 shard_map.108
  56.8 1.3 %collective-permute-start.13 = (bf16[128,1024]{1,0:T(8,128)(2,1)S(1)}, bf16[128,1024]{1,0:T(8,128)(2,1)S(1)}, u32[]{:S(2)}, u32[]{:S(2)}) collective-permute-start(bf16[128,1024]{1,0:T(8,128)(2,1)S(1)} %shard_map.108), channel_id=1, source_target_pairs={{0,2},{1,3},{6,4},{7,5},{8,10},{9,11},{14,12},{15,13},{16,18},{17,... | collective-permute-start | bytes 786440 | tf_op jit(solution)/shard_map/ppermute | solution.py:266
  58.1 0.1 shard_map.109
  58.2 6.3 %collective-permute-start.12 = (bf16[128,1024]{1,0:T(8,128)(2,1)S(1)}, bf16[128,1024]{1,0:T(8,128)(2,1)S(1)}, u32[]{:S(2)}, u32[]{:S(2)}) collective-permute-start(bf16[128,1024]{1,0:T(8,128)(2,1)S(1)} %shard_map.109), channel_id=1, source_target_pairs={{2,0},{3,1},{4,6},{5,7},{10,8},{11,9},{12,14},{13,15},{18,16},{19,... | collective-permute-start | bytes 786440 | tf_op jit(solution)/shard_map/ppermute | solution.py:266
  64.5 4.6 %collective-permute-done.14.one_ref.refs_9_ = bf16[128,1024]{1,0:T(8,128)(2,1)S(1)} collective-permute-done((bf16[128,1024]{1,0:T(8,128)(2,1)S(1)}, bf16[128,1024]{1,0:T(8,128)(2,1)S(1)}, u32[]{:S(2)}, u32[]{:S(2)}) %collective-permute-start.14) | collective-permute-done | bytes 262176 | tf_op jit(solution)/shard_map/ppermute | solution.py:254
  69.1 0.1 shard_map.110
  69.1 1.3 %collective-permute-start.16 = (bf16[128,1024]{1,0:T(8,128)(2,1)S(1)}, bf16[128,1024]{1,0:T(8,128)(2,1)S(1)}, u32[]{:S(2)}, u32[]{:S(2)}) collective-permute-start(bf16[128,1024]{1,0:T(8,128)(2,1)S(1)} %shard_map.110), channel_id=1, source_target_pairs={{0,2},{1,3},{6,4},{7,5},{8,10},{9,11},{14,12},{15,13},{16,18},{17,... | collective-permute-start | bytes 786440 | tf_op jit(solution)/shard_map/ppermute | solution.py:266
  70.4 0.8 collective-permute-done.12.refs_5_
  71.2 5.5 %collective-permute-done.13.refs_8_ = bf16[128,1024]{1,0:T(8,128)(2,1)S(1)} collective-permute-done((bf16[128,1024]{1,0:T(8,128)(2,1)S(1)}, bf16[128,1024]{1,0:T(8,128)(2,1)S(1)}, u32[]{:S(2)}, u32[]{:S(2)}) %collective-permute-start.13) | collective-permute-done | bytes 262176 | tf_op jit(solution)/shard_map/ppermute | solution.py:266
  76.7 5.2 %collective-permute-done.16.refs_11_ = bf16[128,1024]{1,0:T(8,128)(2,1)S(1)} collective-permute-done((bf16[128,1024]{1,0:T(8,128)(2,1)S(1)}, bf16[128,1024]{1,0:T(8,128)(2,1)S(1)}, u32[]{:S(2)}, u32[]{:S(2)}) %collective-permute-start.16) | collective-permute-done | bytes 262176 | tf_op jit(solution)/shard_map/ppermute | solution.py:266
  81.9 1.5 %shard_map.111 = bf16[1,256,1024]{2,1,0:T(8,128)(2,1)} custom-call(s32[3]{0:T(128)S(1)} %pad_add_fusion.place, f32[128,1024]{1,0:T(8,128)S(1)} %get-tuple-element.33.one_ref.refs_0_, bf16[128,1024]{1,0:T(8,128)(2,1)S(1)} %collective-permute-done.7.two_ref.refs_1_, bf16[128,1024]{1,0:T(8,128)(2,1)S(1)} %collective-permute-done.8.refs_2_, ...), custom_call_target="tpu_custom_call" | custom-call | flops 786432 | bytes 4194316 | tf_op jit(solution)/shard_map/pallas_call | solution.py:171
  (25 shorter events, 0.1 us)
Async XLA Ops:
  0.0 10.3 %copy-start.3 = (bf16[1,256,1024]{2,1,0:T(8,128)(2,1)S(1)}, bf16[1,256,1024]{2,1,0:T(8,128)(2,1)}, u32[]{:S(2)}) copy-start(bf16[1,256,1024]{2,1,0:T(8,128)(2,1)} %own_ref.2) | copy-start | bytes 1572868
  1.0 15.2 %copy-start.9 = (f32[1,3,3,1024]{3,0,2,1:T(1,128)S(1)}, f32[1,3,3,1024]{3,0,2,1:T(1,128)}, u32[]{:S(2)}) copy-start(f32[1,3,3,1024]{3,0,2,1:T(1,128)} %param.14) | copy-start | bytes 110596
  1.1 9.3 %collective-permute-start.2 = (bf16[256,512]{1,0:T(8,128)(2,1)S(1)}, bf16[256,512]{1,0:T(8,128)(2,1)S(1)}, u32[]{:S(2)}, u32[]{:S(2)}) collective-permute-start(bf16[256,512]{1,0:T(8,128)(2,1)S(1)} %dynamic-slice_bitcast_fusion), channel_id=1, source_target_pairs={{0,4},{4,0},{1,5},{5,1},{2,6},{6,2},{3,7},{7,3},{8,12},{12,8},{9,1... | collective-permute-start | bytes 786440 | tf_op jit(solution)/shard_map/ppermute | solution.py:203
  1.2 1.0 %copy-start.1 = (bf16[1,256,1024]{2,1,0:T(8,128)(2,1)S(1)}, bf16[1,256,1024]{2,1,0:T(8,128)(2,1)}, u32[]{:S(2)}) copy-start(bf16[1,256,1024]{2,1,0:T(8,128)(2,1)} %key_ref.3) | copy-start | bytes 1572868
  2.3 1.0 %copy-start.2 = (bf16[1,256,1024]{2,1,0:T(8,128)(2,1)S(1)}, bf16[1,256,1024]{2,1,0:T(8,128)(2,1)}, u32[]{:S(2)}) copy-start(bf16[1,256,1024]{2,1,0:T(8,128)(2,1)} %value_ref.3) | copy-start | bytes 1572868
  3.3 0.8 copy-start.8
  4.1 12.2 %copy-start.6 = (bf16[1024,512]{1,0:T(8,128)(2,1)S(1)}, bf16[1024,512]{1,0:T(8,128)(2,1)}, u32[]{:S(2)}) copy-start(bf16[1024,512]{1,0:T(8,128)(2,1)} %constant.50.clone.low_ref) | copy-start | bytes 3145732
  4.1 12.2 %copy-start.10 = (bf16[512,1024]{1,0:T(8,128)(2,1)S(1)}, bf16[512,1024]{1,0:T(8,128)(2,1)}, u32[]{:S(2)}) copy-start(bf16[512,1024]{1,0:T(8,128)(2,1)} %constant.52.clone.back_low_ref) | copy-start | bytes 3145732
  4.1 12.2 %copy-start.11 = (bf16[512,1024]{1,0:T(8,128)(2,1)S(1)}, bf16[512,1024]{1,0:T(8,128)(2,1)}, u32[]{:S(2)}) copy-start(bf16[512,1024]{1,0:T(8,128)(2,1)} %constant.51.clone.back_high_ref) | copy-start | bytes 3145732
  5.0 11.3 %collective-permute-start.1 = (bf16[272,512]{1,0:T(8,128)(2,1)S(1)}, bf16[272,512]{1,0:T(8,128)(2,1)S(1)}, u32[]{:S(2)}, u32[]{:S(2)}) collective-permute-start(bf16[272,512]{1,0:T(8,128)(2,1)S(1)} %shard_map.101), channel_id=1, source_target_pairs={{0,4},{4,0},{1,5},{5,1},{2,6},{6,2},{3,7},{7,3},{8,12},{12,8},{9,1... | collective-permute-start | bytes 835592 | tf_op jit(solution)/shard_map/ppermute | solution.py:206
  8.0 12.7 %collective-permute-start = (bf16[256,512]{1,0:T(8,128)(2,1)S(1)}, bf16[256,512]{1,0:T(8,128)(2,1)S(1)}, u32[]{:S(2)}, u32[]{:S(2)}) collective-permute-start(bf16[256,512]{1,0:T(8,128)(2,1)S(1)} %dynamic-slice_bitcast_fusion.1), channel_id=1, source_target_pairs={{0,4},{4,0},{1,5},{5,1},{2,6},{6,2},{3,7},{7,3},{8,12},{12,8},{9,1... | collective-permute-start | bytes 786440 | tf_op jit(solution)/shard_map/ppermute | solution.py:207
  10.3 1.2 %copy-start.5 = (bf16[1024,512]{1,0:T(8,128)(2,1)S(1)}, bf16[1024,512]{1,0:T(8,128)(2,1)}, u32[]{:S(2)}) copy-start(bf16[1024,512]{1,0:T(8,128)(2,1)} %constant.50.clone.low_ref) | copy-start | bytes 3145732
  11.5 1.2 %copy-start.7 = (bf16[1024,512]{1,0:T(8,128)(2,1)S(1)}, bf16[1024,512]{1,0:T(8,128)(2,1)}, u32[]{:S(2)}) copy-start(bf16[1024,512]{1,0:T(8,128)(2,1)} %constant.49.clone.high_ref) | copy-start | bytes 3145732
  14.6 6.2 %copy-start.4 = (bf16[1,256,1024]{2,1,0:T(8,128)(2,1)S(1)}, bf16[1,256,1024]{2,1,0:T(8,128)(2,1)}, u32[]{:S(2)}) copy-start(bf16[1,256,1024]{2,1,0:T(8,128)(2,1)} %own_ref.3) | copy-start | bytes 1572868
  14.6 17.1 %copy-start = (bf16[1,1024,2048]{2,1,0:T(8,128)(2,1)S(1)}, bf16[1,1024,2048]{2,1,0:T(8,128)(2,1)}, u32[]{:S(2)}) copy-start(bf16[1,1024,2048]{2,1,0:T(8,128)(2,1)} %weight_ref.3) | copy-start | bytes 12582916
  22.2 9.5 %collective-permute-start.6 = (bf16[256,512]{1,0:T(8,128)(2,1)S(1)}, bf16[256,512]{1,0:T(8,128)(2,1)S(1)}, u32[]{:S(2)}, u32[]{:S(2)}) collective-permute-start(bf16[256,512]{1,0:T(8,128)(2,1)S(1)} %get-tuple-element.27), channel_id=1, source_target_pairs={{0,12},{4,8},{8,20},{12,16},{16,28},{20,24},{24,4},{28,0},{1,13},{... | collective-permute-start | bytes 786440 | tf_op jit(solution)/shard_map/ppermute | solution.py:229
  22.2 9.5 %collective-permute-start.5 = (bf16[256,512]{1,0:T(8,128)(2,1)S(1)}, bf16[256,512]{1,0:T(8,128)(2,1)S(1)}, u32[]{:S(2)}, u32[]{:S(2)}) collective-permute-start(bf16[256,512]{1,0:T(8,128)(2,1)S(1)} %get-tuple-element.28), channel_id=1, source_target_pairs={{0,8},{4,12},{8,16},{12,20},{16,24},{20,28},{24,0},{28,4},{1,9},{5... | collective-permute-start | bytes 786440 | tf_op jit(solution)/shard_map/ppermute | solution.py:229
  23.8 11.9 %collective-permute-start.3 = (bf16[256,512]{1,0:T(8,128)(2,1)S(1)}, bf16[256,512]{1,0:T(8,128)(2,1)S(1)}, u32[]{:S(2)}, u32[]{:S(2)}) collective-permute-start(bf16[256,512]{1,0:T(8,128)(2,1)S(1)} %get-tuple-element.27), channel_id=1, source_target_pairs={{0,8},{4,12},{8,16},{12,20},{16,24},{20,28},{24,0},{28,4},{1,9},{5... | collective-permute-start | bytes 786440 | tf_op jit(solution)/shard_map/ppermute | solution.py:229
  23.9 12.6 %collective-permute-start.4 = (bf16[256,512]{1,0:T(8,128)(2,1)S(1)}, bf16[256,512]{1,0:T(8,128)(2,1)S(1)}, u32[]{:S(2)}, u32[]{:S(2)}) collective-permute-start(bf16[256,512]{1,0:T(8,128)(2,1)S(1)} %get-tuple-element.28), channel_id=1, source_target_pairs={{0,12},{4,8},{8,20},{12,16},{16,28},{20,24},{24,4},{28,0},{1,13},{... | collective-permute-start | bytes 786440 | tf_op jit(solution)/shard_map/ppermute | solution.py:229
  36.5 8.9 %collective-permute-start.7 = (bf16[128,1024]{1,0:T(8,128)(2,1)S(1)}, bf16[128,1024]{1,0:T(8,128)(2,1)S(1)}, u32[]{:S(2)}, u32[]{:S(2)}) collective-permute-start(bf16[128,1024]{1,0:T(8,128)(2,1)S(1)} %get-tuple-element.34), channel_id=1, source_target_pairs={{0,1},{1,0},{2,3},{3,2},{4,5},{5,4},{6,7},{7,6},{8,9},{9,8},{10,11... | collective-permute-start | bytes 786440 | tf_op jit(solution)/shard_map/ppermute | solution.py:253
  40.0 12.0 %collective-permute-start.10 = (bf16[128,1024]{1,0:T(8,128)(2,1)S(1)}, bf16[128,1024]{1,0:T(8,128)(2,1)S(1)}, u32[]{:S(2)}, u32[]{:S(2)}) collective-permute-start(bf16[128,1024]{1,0:T(8,128)(2,1)S(1)} %get-tuple-element.39), channel_id=1, source_target_pairs={{0,5},{1,4},{2,7},{3,6},{4,1},{5,0},{6,3},{7,2},{8,13},{9,12},{10,... | collective-permute-start | bytes 786440 | tf_op jit(solution)/shard_map/ppermute | solution.py:254
  41.0 15.7 %collective-permute-start.11 = (bf16[128,1024]{1,0:T(8,128)(2,1)S(1)}, bf16[128,1024]{1,0:T(8,128)(2,1)S(1)}, u32[]{:S(2)}, u32[]{:S(2)}) collective-permute-start(bf16[128,1024]{1,0:T(8,128)(2,1)S(1)} %get-tuple-element.40), channel_id=1, source_target_pairs={{0,4},{4,0},{1,5},{5,1},{2,6},{6,2},{3,7},{7,3},{8,12},{12,8},{9,1... | collective-permute-start | bytes 786440 | tf_op jit(solution)/shard_map/ppermute | solution.py:255
  41.9 16.2 %collective-permute-start.9 = (bf16[128,1024]{1,0:T(8,128)(2,1)S(1)}, bf16[128,1024]{1,0:T(8,128)(2,1)S(1)}, u32[]{:S(2)}, u32[]{:S(2)}) collective-permute-start(bf16[128,1024]{1,0:T(8,128)(2,1)S(1)} %get-tuple-element.36), channel_id=1, source_target_pairs={{0,1},{1,0},{2,3},{3,2},{4,5},{5,4},{6,7},{7,6},{8,9},{9,8},{10,11... | collective-permute-start | bytes 786440 | tf_op jit(solution)/shard_map/ppermute | solution.py:253
  43.5 25.5 %collective-permute-start.14 = (bf16[128,1024]{1,0:T(8,128)(2,1)S(1)}, bf16[128,1024]{1,0:T(8,128)(2,1)S(1)}, u32[]{:S(2)}, u32[]{:S(2)}) collective-permute-start(bf16[128,1024]{1,0:T(8,128)(2,1)S(1)} %get-tuple-element.45), channel_id=1, source_target_pairs={{0,5},{1,4},{2,7},{3,6},{4,1},{5,0},{6,3},{7,2},{8,13},{9,12},{10,... | collective-permute-start | bytes 786440 | tf_op jit(solution)/shard_map/ppermute | solution.py:254
  45.4 23.7 %collective-permute-start.15 = (bf16[128,1024]{1,0:T(8,128)(2,1)S(1)}, bf16[128,1024]{1,0:T(8,128)(2,1)S(1)}, u32[]{:S(2)}, u32[]{:S(2)}) collective-permute-start(bf16[128,1024]{1,0:T(8,128)(2,1)S(1)} %get-tuple-element.46), channel_id=1, source_target_pairs={{0,4},{4,0},{1,5},{5,1},{2,6},{6,2},{3,7},{7,3},{8,12},{12,8},{9,1... | collective-permute-start | bytes 786440 | tf_op jit(solution)/shard_map/ppermute | solution.py:255
  52.0 18.5 %collective-permute-start.8 = (bf16[128,1024]{1,0:T(8,128)(2,1)S(1)}, bf16[128,1024]{1,0:T(8,128)(2,1)S(1)}, u32[]{:S(2)}, u32[]{:S(2)}) collective-permute-start(bf16[128,1024]{1,0:T(8,128)(2,1)S(1)} %shard_map.106), channel_id=1, source_target_pairs={{2,0},{3,1},{4,6},{5,7},{10,8},{11,9},{12,14},{13,15},{18,16},{19,... | collective-permute-start | bytes 786440 | tf_op jit(solution)/shard_map/ppermute | solution.py:266
  56.8 19.9 %collective-permute-start.13 = (bf16[128,1024]{1,0:T(8,128)(2,1)S(1)}, bf16[128,1024]{1,0:T(8,128)(2,1)S(1)}, u32[]{:S(2)}, u32[]{:S(2)}) collective-permute-start(bf16[128,1024]{1,0:T(8,128)(2,1)S(1)} %shard_map.108), channel_id=1, source_target_pairs={{0,2},{1,3},{6,4},{7,5},{8,10},{9,11},{14,12},{15,13},{16,18},{17,... | collective-permute-start | bytes 786440 | tf_op jit(solution)/shard_map/ppermute | solution.py:266
  58.2 13.0 %collective-permute-start.12 = (bf16[128,1024]{1,0:T(8,128)(2,1)S(1)}, bf16[128,1024]{1,0:T(8,128)(2,1)S(1)}, u32[]{:S(2)}, u32[]{:S(2)}) collective-permute-start(bf16[128,1024]{1,0:T(8,128)(2,1)S(1)} %shard_map.109), channel_id=1, source_target_pairs={{2,0},{3,1},{4,6},{5,7},{10,8},{11,9},{12,14},{13,15},{18,16},{19,... | collective-permute-start | bytes 786440 | tf_op jit(solution)/shard_map/ppermute | solution.py:266
  69.1 12.8 %collective-permute-start.16 = (bf16[128,1024]{1,0:T(8,128)(2,1)S(1)}, bf16[128,1024]{1,0:T(8,128)(2,1)S(1)}, u32[]{:S(2)}, u32[]{:S(2)}) collective-permute-start(bf16[128,1024]{1,0:T(8,128)(2,1)S(1)} %shard_map.110), channel_id=1, source_target_pairs={{0,2},{1,3},{6,4},{7,5},{8,10},{9,11},{14,12},{15,13},{16,18},{17,... | collective-permute-start | bytes 786440 | tf_op jit(solution)/shard_map/ppermute | solution.py:266

commit v4 on v3

--- a/solution.py
+++ b/solution.py
@@ -17,7 +17,7 @@
 LANES = 256
 WIDE = 512
 OWN, CROSS = 2, 2
-ORDER = [(0, 0), (1, 0), (0, 1), (1, 1)]
+ORDER = [(0, 0, None), (1, 0, None), (0, 1, (1, 0)), (1, 1, (0, 1))]
 
 
 def odd_tables(length):
@@ -119,16 +119,25 @@
         )
 
 
-def gate_kernel(place, own_ref, come_ref, taps_ref, conv_ref, here_ref, there_ref, whole):
-    rows, width = come_ref.shape
-    whole[span(place[0], rows), :] = own_ref[0, :, span(place[0], width)].astype(F32)
-    whole[span(1 - place[0], rows), :] = come_ref[...].astype(F32)
+def gate_kernel(own, place, current_ref, previous_ref, taps_ref, conv_ref, out_ref):
+    rows, width = out_ref.shape
+    half = place[0] if own else 1 - place[0]
     for lane in range(0, width, LANES):
-        lanes = slice(lane, lane + LANES)
-        taps = taps_ref[0, :, 0, pl.ds(pl.multiple_of(place[0] * width + lane, LANES), LANES)]
-        whole[:, lanes] = short_filtered(whole[:, lanes], taps) * conv_ref[:, lanes]
-    here_ref[...] = whole[span(place[0], rows), :].astype(BF16)
-    there_ref[...] = whole[span(1 - place[0], rows), :].astype(BF16)
+        mine = pl.ds(pl.multiple_of(place[0] * width + lane, LANES), LANES)
+        rest = slice(lane, lane + LANES)
+        taps = taps_ref[0, :, 0, mine]
+        if own:
+            current, before = current_ref[0, :, mine], previous_ref[rows - EXTRA :, rest]
+        else:
+            current, before = current_ref[:, rest], previous_ref[0, rows - EXTRA :, mine]
+        current = current.astype(F32)
+        before = jnp.where(half == 1, before.astype(F32), 0.0)
+        old, older = before[EXTRA - 1 :], before[EXTRA - 2 : EXTRA - 1]
+        index = lax.broadcasted_iota(jnp.int32, current.shape, 0)
+        one = jnp.where(index == 0, old, pltpu.roll(current, 1, 0))
+        two = jnp.where(index == 0, older, jnp.where(index == 1, old, pltpu.roll(current, 2, 0)))
+        feature = taps[0:1] * current + taps[1:2] * one + taps[2:3] * two
+        out_ref[:, rest] = (feature * conv_ref[span(half, rows), rest]).astype(BF16)
 
 
 def project_kernel(place, same_ref, cross_ref, weight_ref, *out_refs):
@@ -208,7 +217,7 @@
     (mixed_own,) = local(functools.partial(mix_kernel, False), [mixed], 20 * rows * width, place, key, value, taps)
 
     square = length * length * width
-    half_bf16, half_f32 = pltpu.VMEM((length, width), BF16), pltpu.VMEM((length, width), F32)
+    half_bf16 = pltpu.VMEM((length, width), BF16)
     (spectrum,) = local(
         filter_kernel, [shape((2 * length, width), F32)], 8 * square, place, filt, filt_come, high, low,
         scratch=[half_bf16],
@@ -217,10 +226,13 @@
         conv_kernel, [shape((length, width), F32)], 20 * square, place, mixed_own, mixed_come, taps, spectrum,
         high, low, back_high, back_low, scratch=[half_bf16],
     )
-    here, there = local(
-        gate_kernel, [shape((rows, width), BF16)] * 2, 10 * length * width, place, query, query_come, taps, convolved,
-        scratch=[half_f32],
-    )
+    half = [shape((rows, width), BF16)]
+    there = local(
+        functools.partial(gate_kernel, False), half, 5 * length * width, place, query_come, query, taps, convolved
+    )[0]
+    here = local(
+        functools.partial(gate_kernel, True), half, 5 * length * width, place, query, query_come, taps, convolved
+    )[0]
 
     def to_next(array, flip):
         pairs = [
@@ -254,12 +266,12 @@
     near_come = [lax.ppermute(piece, ("ctx", "mp"), diagonal) for piece in pieces[:CROSS]]
     keep_come = [lax.ppermute(piece, "ctx", swap) for piece in pieces[CROSS:]]
     pairs = {0: list(zip(owned[OWN:], own_near)), 1: list(zip(near_come, keep_come))}
-    held, sums = None, {}
-    for role, c in ORDER:
+    sums = {}
+    for role, c, after in ORDER:
         pair = pairs[role][c]
-        if held is not None:
-            pair = lax.optimization_barrier(pair + (held,))[:2]
-        held = sums[role, c] = add(*pair)
+        if after is not None:
+            pair = lax.optimization_barrier(pair + (sums[after],))[:2]
+        sums[role, c] = add(*pair)
     groups = []
     for role, count, far in ((0, OWN, far_own), (1, CROSS, far_cross)):
         for c in range(count):

time: 83.9 us -> 83.6 us (level)
    ppermute x2, waiting for transfers between devices: 9.64 us -> 8.33 us  [two_by_four(): lax.ppermute(piece, ('ctx', 'mp'), diagonal)]
    ppermute x4, starting transfers between devices: 13.6 us -> 14.7 us  [two_by_four(): groups += [*pairs[role][c], lax.ppermute(sums[role, c], ('ctx', 'mp'), far)]]
    pallas_call x12 -> x13, Pallas kernels: 14.2 us -> 14.2 us  [local(): pl.pallas_call(kernel, out_shape=out_shape, in_specs=[pl.BlockSpec(memory...]
    unnamed x24 -> x22, local copies, waits for them, and re-layouts: 5.33 us -> 5.33 us
  transfers between devices with their start and end apart: 17 -> 17, of which waited for: 12 -> 11; matrix products, arithmetic and copies ran while one was open for 1% -> 1% of each run, Pallas kernels for 13% -> 14%
where the time goes in v4:
time: 83.6 us; the launch traced here: 83.2 us
  waiting for transfers between devices  34.4 us (41%)
  starting transfers between devices  26.9 us (32%)
  Pallas kernels  14.2 us (17%)
  local copies, waits for them, and re-layouts  7.34 us (9%)
    ppermute x4, starting transfers between devices, two_by_four(): groups += [*pairs[role][c], lax.ppermute(sums[role, c], ('ctx', 'mp'), far)]  14.7 us
    pallas_call x13, Pallas kernels, local(): pl.pallas_call(kernel, out_shape=out_shape, in_specs=[pl.BlockSpec(memory...  14.2 us
    ppermute x4, waiting for transfers between devices, two_by_four(): groups += [*pairs[role][c], lax.ppermute(sums[role, c], ('ctx', 'mp'), far)]  11.7 us
    ppermute x4, waiting for transfers between devices, to_next(): return lax.ppermute(array, ('section', 'ctx'), pairs)  9.11 us
    ppermute x2, waiting for transfers between devices, two_by_four(): lax.ppermute(piece, ('ctx', 'mp'), diagonal)  8.33 us
    unnamed x22, local copies, waits for them, and re-layouts  5.33 us
    ppermute x4, starting transfers between devices, to_next(): return lax.ppermute(array, ('section', 'ctx'), pairs)  3.42 us
    ppermute x2, starting transfers between devices, two_by_four(): own_near = [lax.ppermute(piece, 'mp', near) for piece in owned[:OWN]]  3.15 us
  transfers between devices with their start and end apart: 17, of which 11 were waited for; matrix products, arithmetic and copies ran while one was open for 1% of the time, Pallas kernels for 14%

profile of v4, /device:TPU:2, one launch (start us, length us, event | category | flops | bytes accessed | tf_op | source)
XLA Modules:
  0.0 83.2 jit_solution(8905790975650258213)
XLA Ops:
  0.0 1.0 %dynamic-slice_bitcast_fusion = bf16[256,512]{1,0:T(8,128)(2,1)S(1)} fusion(bf16[1,256,1024]{2,1,0:T(8,128)(2,1)} %own_ref.1, s32[]{:T(128)S(6)} %select_n.17), kind=kLoop, calls=%fused_computation | loop fusion | bytes 524292 | tf_op jit(solution)/shard_map/dynamic_slice | solution.py:210
  1.1 0.1 collective-permute-start.2
  1.2 0.1 pad_add_fusion.place
  1.2 1.0 %copy-done.2 = bf16[1,256,1024]{2,1,0:T(8,128)(2,1)S(1)} copy-done((bf16[1,256,1024]{2,1,0:T(8,128)(2,1)S(1)}, bf16[1,256,1024]{2,1,0:T(8,128)(2,1)}, u32[]{:S(2)}) %copy-start.2) | copy-done | bytes 524312
  2.3 1.0 %copy-done.3 = bf16[1,256,1024]{2,1,0:T(8,128)(2,1)S(1)} copy-done((bf16[1,256,1024]{2,1,0:T(8,128)(2,1)S(1)}, bf16[1,256,1024]{2,1,0:T(8,128)(2,1)}, u32[]{:S(2)}) %copy-start.3) | copy-done | bytes 524312
  3.3 0.8 copy-done.7
  4.1 0.9 %shard_map.101 = bf16[272,512]{1,0:T(8,128)(2,1)S(1)} custom-call(s32[3]{0:T(128)S(1)} %pad_add_fusion.place, bf16[1,256,1024]{2,1,0:T(8,128)(2,1)S(1)} %copy-done.2, bf16[1,256,1024]{2,1,0:T(8,128)(2,1)S(1)} %copy-done.3, f32[3,3,1,1024]{3,2,1,0:T(1,128)S(1)} %bitcast.8), custom_call_target="tpu_custom_call" | custom-call | flops 2621440 | bytes 1363980 | tf_op jit(solution)/shard_map/pallas_call | solution.py:180
  5.0 2.1 %collective-permute-start.1 = (bf16[272,512]{1,0:T(8,128)(2,1)S(1)}, bf16[272,512]{1,0:T(8,128)(2,1)S(1)}, u32[]{:S(2)}, u32[]{:S(2)}) collective-permute-start(bf16[272,512]{1,0:T(8,128)(2,1)S(1)} %shard_map.101), channel_id=1, source_target_pairs={{0,4},{4,0},{1,5},{5,1},{2,6},{6,2},{3,7},{7,3},{8,12},{12,8},{9,1... | collective-permute-start | bytes 835592 | tf_op jit(solution)/shard_map/ppermute | solution.py:215
  7.1 1.0 %dynamic-slice_bitcast_fusion.1 = bf16[256,512]{1,0:T(8,128)(2,1)S(1)} fusion(bf16[1,256,1024]{2,1,0:T(8,128)(2,1)} %current_ref.1, s32[]{:T(128)S(6)} %select_n.17), kind=kLoop, calls=%fused_computation.1 | loop fusion | bytes 524292 | tf_op jit(solution)/shard_map/dynamic_slice | solution.py:210
  8.0 0.1 collective-permute-start
  8.1 0.9 %shard_map.100.own_ref = bf16[272,512]{1,0:T(8,128)(2,1)S(1)} custom-call(s32[3]{0:T(128)S(1)} %pad_add_fusion.place, bf16[1,256,1024]{2,1,0:T(8,128)(2,1)S(1)} %copy-done.2, bf16[1,256,1024]{2,1,0:T(8,128)(2,1)S(1)} %copy-done.3, f32[3,3,1,1024]{3,2,1,0:T(1,128)S(1)} %bitcast.9), custom_call_target="tpu_custom_call" | custom-call | flops 2621440 | bytes 1363980 | tf_op jit(solution)/shard_map/pallas_call | solution.py:180
  9.1 1.3 %collective-permute-done.2.come_ref = bf16[256,512]{1,0:T(8,128)(2,1)S(1)} collective-permute-done((bf16[256,512]{1,0:T(8,128)(2,1)S(1)}, bf16[256,512]{1,0:T(8,128)(2,1)S(1)}, u32[]{:S(2)}, u32[]{:S(2)}) %collective-permute-start.2) | collective-permute-done | bytes 262176 | tf_op jit(solution)/shard_map/ppermute | solution.py:212
  10.3 1.2 %copy-done.5 = bf16[1024,512]{1,0:T(8,128)(2,1)S(1)} copy-done((bf16[1024,512]{1,0:T(8,128)(2,1)S(1)}, bf16[1024,512]{1,0:T(8,128)(2,1)}, u32[]{:S(2)}) %copy-start.5) | copy-done | bytes 1048600
  11.5 1.2 %copy-done.6 = bf16[1024,512]{1,0:T(8,128)(2,1)S(1)} copy-done((bf16[1024,512]{1,0:T(8,128)(2,1)S(1)}, bf16[1024,512]{1,0:T(8,128)(2,1)}, u32[]{:S(2)}) %copy-start.6) | copy-done | bytes 1048600
  12.8 1.8 %shard_map.102.spec_ref = f32[1024,512]{1,0:T(8,128)S(1)} custom-call(s32[3]{0:T(128)S(1)} %pad_add_fusion.place, bf16[1,256,1024]{2,1,0:T(8,128)(2,1)S(1)} %copy-done.4, bf16[256,512]{1,0:T(8,128)(2,1)S(1)} %collective-permute-done.2.come_ref, bf16[1024,512]{1,0:T(8,128)(2,1)S(1)} %copy-done.6, bf16[1024,512]{1,0:T(8,128)(2,1)S(1)} %copy-done.5), custom_call_target="tpu_custom_call" | custom-call | flops 1073741824 | bytes 4980748 | tf_op jit(solution)/shard_map/pallas_call | solution.py:180
  14.6 1.7 %collective-permute-done.1.come_ref = bf16[272,512]{1,0:T(8,128)(2,1)S(1)} collective-permute-done((bf16[272,512]{1,0:T(8,128)(2,1)S(1)}, bf16[272,512]{1,0:T(8,128)(2,1)S(1)}, u32[]{:S(2)}, u32[]{:S(2)}) %collective-permute-start.1) | collective-permute-done | bytes 278560 | tf_op jit(solution)/shard_map/ppermute | solution.py:215
  16.3 3.7 %shard_map.103.conv_ref = f32[512,512]{1,0:T(8,128)S(1)} custom-call(s32[3]{0:T(128)S(1)} %pad_add_fusion.place, bf16[272,512]{1,0:T(8,128)(2,1)S(1)} %shard_map.100.own_ref, bf16[272,512]{1,0:T(8,128)(2,1)S(1)} %collective-permute-done.1.come_ref, f32[3,3,1,1024]{3,2,1,0:T(1,128)S(1)} %bitcast.10, f32[1024,512]{1,0:T(8,128)S(1)} %shard_map.102.spec_ref, ...), custom_call_target="tpu_custom_call" | custom-call | flops 2684354560 | bytes 7933964 | tf_op jit(solution)/shard_map/pallas_call | solution.py:180
  20.0 0.7 collective-permute-done.current_ref.previous_ref
  20.8 0.7 shard_map.104
  21.5 0.1 collective-permute-start.6
  21.6 0.8 shard_map.105
  22.3 1.6 %collective-permute-start.5 = (bf16[256,512]{1,0:T(8,128)(2,1)S(1)}, bf16[256,512]{1,0:T(8,128)(2,1)S(1)}, u32[]{:S(2)}, u32[]{:S(2)}) collective-permute-start(bf16[256,512]{1,0:T(8,128)(2,1)S(1)} %shard_map.105), channel_id=1, source_target_pairs={{0,8},{4,12},{8,16},{12,20},{16,24},{20,28},{24,0},{28,4},{1,9},{5... | collective-permute-start | bytes 786440 | tf_op jit(solution)/shard_map/ppermute | solution.py:241
  24.0 0.1 collective-permute-start.3
  24.0 1.7 %collective-permute-start.4 = (bf16[256,512]{1,0:T(8,128)(2,1)S(1)}, bf16[256,512]{1,0:T(8,128)(2,1)S(1)}, u32[]{:S(2)}, u32[]{:S(2)}) collective-permute-start(bf16[256,512]{1,0:T(8,128)(2,1)S(1)} %shard_map.105), channel_id=1, source_target_pairs={{0,12},{4,8},{8,20},{12,16},{16,28},{20,24},{24,4},{28,0},{1,13},{... | collective-permute-start | bytes 786440 | tf_op jit(solution)/shard_map/ppermute | solution.py:241
  25.7 5.3 %collective-permute-done.6.cross_ref = bf16[256,512]{1,0:T(8,128)(2,1)S(1)} collective-permute-done((bf16[256,512]{1,0:T(8,128)(2,1)S(1)}, bf16[256,512]{1,0:T(8,128)(2,1)S(1)}, u32[]{:S(2)}, u32[]{:S(2)}) %collective-permute-start.6) | collective-permute-done | bytes 262176 | tf_op jit(solution)/shard_map/ppermute | solution.py:241
  31.0 1.8 %shard_map.106 = (bf16[128,1024]{1,0:T(8,128)(2,1)S(1)}, bf16[128,1024]{1,0:T(8,128)(2,1)S(1)}, f32[128,1024]{1,0:T(8,128)S(1)}, f32[128,1024]{1,0:T(8,128)S(1)}) custom-call(s32[3]{0:T(128)S(1)} %pad_add_fusion.place, bf16[256,512]{1,0:T(8,128)(2,1)S(1)} %collective-permute-done.5.same_ref, bf16[256,512]{1,0:T(8,128)(2,1)S(1)} %collective-permute-done.6.cross_ref, ...), custom_call_target="tpu_custom_call" | custom-call | flops 1073741824 | bytes 6291468 | tf_op jit(solution)/shard_map/pallas_call | solution.py:180
  32.8 3.8 %collective-permute-done.3.same_ref = bf16[256,512]{1,0:T(8,128)(2,1)S(1)} collective-permute-done((bf16[256,512]{1,0:T(8,128)(2,1)S(1)}, bf16[256,512]{1,0:T(8,128)(2,1)S(1)}, u32[]{:S(2)}, u32[]{:S(2)}) %collective-permute-start.3) | collective-permute-done | bytes 262176 | tf_op jit(solution)/shard_map/ppermute | solution.py:241
  36.6 1.6 %collective-permute-start.7 = (bf16[128,1024]{1,0:T(8,128)(2,1)S(1)}, bf16[128,1024]{1,0:T(8,128)(2,1)S(1)}, u32[]{:S(2)}, u32[]{:S(2)}) collective-permute-start(bf16[128,1024]{1,0:T(8,128)(2,1)S(1)} %get-tuple-element.28), channel_id=1, source_target_pairs={{0,1},{1,0},{2,3},{3,2},{4,5},{5,4},{6,7},{7,6},{8,9},{9,8},{10,11... | collective-permute-start | bytes 786440 | tf_op jit(solution)/shard_map/ppermute | solution.py:265
  38.2 1.8 %shard_map.108 = (bf16[128,1024]{1,0:T(8,128)(2,1)S(1)}, bf16[128,1024]{1,0:T(8,128)(2,1)S(1)}, bf16[128,1024]{1,0:T(8,128)(2,1)S(1)}, bf16[128,1024]{1,0:T(8,128)(2,1)S(1)}) custom-call(s32[3]{0:T(128)S(1)} %pad_add_fusion.place, bf16[256,512]{1,0:T(8,128)(2,1)S(1)} %collective-permute-done.3.same_ref, ...), custom_call_target="tpu_custom_call" | custom-call | flops 1073741824 | bytes 5767180 | tf_op jit(solution)/shard_map/pallas_call | solution.py:180
  40.0 0.7 collective-permute-start.10
  40.7 1.2 %collective-permute-start.11 = (bf16[128,1024]{1,0:T(8,128)(2,1)S(1)}, bf16[128,1024]{1,0:T(8,128)(2,1)S(1)}, u32[]{:S(2)}, u32[]{:S(2)}) collective-permute-start(bf16[128,1024]{1,0:T(8,128)(2,1)S(1)} %get-tuple-element.34), channel_id=1, source_target_pairs={{0,4},{4,0},{1,5},{5,1},{2,6},{6,2},{3,7},{7,3},{8,12},{12,8},{9,1... | collective-permute-start | bytes 786440 | tf_op jit(solution)/shard_map/ppermute | solution.py:267
  42.0 1.6 %collective-permute-start.9 = (bf16[128,1024]{1,0:T(8,128)(2,1)S(1)}, bf16[128,1024]{1,0:T(8,128)(2,1)S(1)}, u32[]{:S(2)}, u32[]{:S(2)}) collective-permute-start(bf16[128,1024]{1,0:T(8,128)(2,1)S(1)} %get-tuple-element.30), channel_id=1, source_target_pairs={{0,1},{1,0},{2,3},{3,2},{4,5},{5,4},{6,7},{7,6},{8,9},{9,8},{10,11... | collective-permute-start | bytes 786440 | tf_op jit(solution)/shard_map/ppermute | solution.py:265
  43.5 0.7 collective-permute-start.14
  44.2 1.6 %collective-permute-done.7.two_ref.refs_1_ = bf16[128,1024]{1,0:T(8,128)(2,1)S(1)} collective-permute-done((bf16[128,1024]{1,0:T(8,128)(2,1)S(1)}, bf16[128,1024]{1,0:T(8,128)(2,1)S(1)}, u32[]{:S(2)}, u32[]{:S(2)}) %collective-permute-start.7) | collective-permute-done | bytes 262176 | tf_op jit(solution)/shard_map/ppermute | solution.py:265
  45.9 0.8 collective-permute-start.15
  46.7 5.1 %collective-permute-done.10.one_ref.refs_6_ = bf16[128,1024]{1,0:T(8,128)(2,1)S(1)} collective-permute-done((bf16[128,1024]{1,0:T(8,128)(2,1)S(1)}, bf16[128,1024]{1,0:T(8,128)(2,1)S(1)}, u32[]{:S(2)}, u32[]{:S(2)}) %collective-permute-start.10) | collective-permute-done | bytes 262176 | tf_op jit(solution)/shard_map/ppermute | solution.py:266
  51.7 4.7 %collective-permute-start.8 = (bf16[128,1024]{1,0:T(8,128)(2,1)S(1)}, bf16[128,1024]{1,0:T(8,128)(2,1)S(1)}, u32[]{:S(2)}, u32[]{:S(2)}) collective-permute-start(bf16[128,1024]{1,0:T(8,128)(2,1)S(1)} %shard_map.107), channel_id=1, source_target_pairs={{2,0},{3,1},{4,6},{5,7},{10,8},{11,9},{12,14},{13,15},{18,16},{19,... | collective-permute-start | bytes 786440 | tf_op jit(solution)/shard_map/ppermute | solution.py:278
  56.5 0.1 shard_map.109
  56.5 1.3 %collective-permute-start.13 = (bf16[128,1024]{1,0:T(8,128)(2,1)S(1)}, bf16[128,1024]{1,0:T(8,128)(2,1)S(1)}, u32[]{:S(2)}, u32[]{:S(2)}) collective-permute-start(bf16[128,1024]{1,0:T(8,128)(2,1)S(1)} %shard_map.109), channel_id=1, source_target_pairs={{0,2},{1,3},{6,4},{7,5},{8,10},{9,11},{14,12},{15,13},{16,18},{17,... | collective-permute-start | bytes 786440 | tf_op jit(solution)/shard_map/ppermute | solution.py:278
  57.8 0.1 shard_map.110
  57.9 7.4 %collective-permute-start.12 = (bf16[128,1024]{1,0:T(8,128)(2,1)S(1)}, bf16[128,1024]{1,0:T(8,128)(2,1)S(1)}, u32[]{:S(2)}, u32[]{:S(2)}) collective-permute-start(bf16[128,1024]{1,0:T(8,128)(2,1)S(1)} %shard_map.110), channel_id=1, source_target_pairs={{2,0},{3,1},{4,6},{5,7},{10,8},{11,9},{12,14},{13,15},{18,16},{19,... | collective-permute-start | bytes 786440 | tf_op jit(solution)/shard_map/ppermute | solution.py:278
  65.3 3.3 %collective-permute-done.14.one_ref.refs_9_ = bf16[128,1024]{1,0:T(8,128)(2,1)S(1)} collective-permute-done((bf16[128,1024]{1,0:T(8,128)(2,1)S(1)}, bf16[128,1024]{1,0:T(8,128)(2,1)S(1)}, u32[]{:S(2)}, u32[]{:S(2)}) %collective-permute-start.14) | collective-permute-done | bytes 262176 | tf_op jit(solution)/shard_map/ppermute | solution.py:266
  68.6 0.1 shard_map.111
  68.7 1.3 %collective-permute-start.16 = (bf16[128,1024]{1,0:T(8,128)(2,1)S(1)}, bf16[128,1024]{1,0:T(8,128)(2,1)S(1)}, u32[]{:S(2)}, u32[]{:S(2)}) collective-permute-start(bf16[128,1024]{1,0:T(8,128)(2,1)S(1)} %shard_map.111), channel_id=1, source_target_pairs={{0,2},{1,3},{6,4},{7,5},{8,10},{9,11},{14,12},{15,13},{16,18},{17,... | collective-permute-start | bytes 786440 | tf_op jit(solution)/shard_map/ppermute | solution.py:278
  70.0 1.3 %collective-permute-done.12.refs_5_ = bf16[128,1024]{1,0:T(8,128)(2,1)S(1)} collective-permute-done((bf16[128,1024]{1,0:T(8,128)(2,1)S(1)}, bf16[128,1024]{1,0:T(8,128)(2,1)S(1)}, u32[]{:S(2)}, u32[]{:S(2)}) %collective-permute-start.12) | collective-permute-done | bytes 262176 | tf_op jit(solution)/shard_map/ppermute | solution.py:278
  71.3 2.5 %collective-permute-done.13.refs_8_ = bf16[128,1024]{1,0:T(8,128)(2,1)S(1)} collective-permute-done((bf16[128,1024]{1,0:T(8,128)(2,1)S(1)}, bf16[128,1024]{1,0:T(8,128)(2,1)S(1)}, u32[]{:S(2)}, u32[]{:S(2)}) %collective-permute-start.13) | collective-permute-done | bytes 262176 | tf_op jit(solution)/shard_map/ppermute | solution.py:278
  73.8 7.9 %collective-permute-done.16.refs_11_ = bf16[128,1024]{1,0:T(8,128)(2,1)S(1)} collective-permute-done((bf16[128,1024]{1,0:T(8,128)(2,1)S(1)}, bf16[128,1024]{1,0:T(8,128)(2,1)S(1)}, u32[]{:S(2)}, u32[]{:S(2)}) %collective-permute-start.16) | collective-permute-done | bytes 262176 | tf_op jit(solution)/shard_map/ppermute | solution.py:278
  81.6 1.5 %shard_map.112 = bf16[1,256,1024]{2,1,0:T(8,128)(2,1)} custom-call(s32[3]{0:T(128)S(1)} %pad_add_fusion.place, f32[128,1024]{1,0:T(8,128)S(1)} %get-tuple-element.27.one_ref.refs_0_, bf16[128,1024]{1,0:T(8,128)(2,1)S(1)} %collective-permute-done.7.two_ref.refs_1_, bf16[128,1024]{1,0:T(8,128)(2,1)S(1)} %collective-permute-done.8.refs_2_, ...), custom_call_target="tpu_custom_call" | custom-call | flops 786432 | bytes 4194316 | tf_op jit(solution)/shard_map/pallas_call | solution.py:180
  (24 shorter events, 0.1 us)
Async XLA Ops:
  0.0 10.3 %copy-start.4 = (bf16[1,256,1024]{2,1,0:T(8,128)(2,1)S(1)}, bf16[1,256,1024]{2,1,0:T(8,128)(2,1)}, u32[]{:S(2)}) copy-start(bf16[1,256,1024]{2,1,0:T(8,128)(2,1)} %own_ref.1) | copy-start | bytes 1572868
  1.0 15.2 %copy-start.8 = (f32[1,3,3,1024]{3,0,2,1:T(1,128)S(1)}, f32[1,3,3,1024]{3,0,2,1:T(1,128)}, u32[]{:S(2)}) copy-start(f32[1,3,3,1024]{3,0,2,1:T(1,128)} %param.14) | copy-start | bytes 110596
  1.1 9.3 %collective-permute-start.2 = (bf16[256,512]{1,0:T(8,128)(2,1)S(1)}, bf16[256,512]{1,0:T(8,128)(2,1)S(1)}, u32[]{:S(2)}, u32[]{:S(2)}) collective-permute-start(bf16[256,512]{1,0:T(8,128)(2,1)S(1)} %dynamic-slice_bitcast_fusion), channel_id=1, source_target_pairs={{0,4},{4,0},{1,5},{5,1},{2,6},{6,2},{3,7},{7,3},{8,12},{12,8},{9,1... | collective-permute-start | bytes 786440 | tf_op jit(solution)/shard_map/ppermute | solution.py:212
  1.2 1.0 %copy-start.2 = (bf16[1,256,1024]{2,1,0:T(8,128)(2,1)S(1)}, bf16[1,256,1024]{2,1,0:T(8,128)(2,1)}, u32[]{:S(2)}) copy-start(bf16[1,256,1024]{2,1,0:T(8,128)(2,1)} %key_ref.3) | copy-start | bytes 1572868
  2.3 1.0 %copy-start.3 = (bf16[1,256,1024]{2,1,0:T(8,128)(2,1)S(1)}, bf16[1,256,1024]{2,1,0:T(8,128)(2,1)}, u32[]{:S(2)}) copy-start(bf16[1,256,1024]{2,1,0:T(8,128)(2,1)} %value_ref.3) | copy-start | bytes 1572868
  3.3 0.8 copy-start.7
  4.1 12.2 %copy-start.9 = (bf16[512,1024]{1,0:T(8,128)(2,1)S(1)}, bf16[512,1024]{1,0:T(8,128)(2,1)}, u32[]{:S(2)}) copy-start(bf16[512,1024]{1,0:T(8,128)(2,1)} %constant.52.clone.back_low_ref) | copy-start | bytes 3145732
  4.1 12.2 %copy-start.10 = (bf16[512,1024]{1,0:T(8,128)(2,1)S(1)}, bf16[512,1024]{1,0:T(8,128)(2,1)}, u32[]{:S(2)}) copy-start(bf16[512,1024]{1,0:T(8,128)(2,1)} %constant.51.clone.back_high_ref) | copy-start | bytes 3145732
  5.0 11.3 %collective-permute-start.1 = (bf16[272,512]{1,0:T(8,128)(2,1)S(1)}, bf16[272,512]{1,0:T(8,128)(2,1)S(1)}, u32[]{:S(2)}, u32[]{:S(2)}) collective-permute-start(bf16[272,512]{1,0:T(8,128)(2,1)S(1)} %shard_map.101), channel_id=1, source_target_pairs={{0,4},{4,0},{1,5},{5,1},{2,6},{6,2},{3,7},{7,3},{8,12},{12,8},{9,1... | collective-permute-start | bytes 835592 | tf_op jit(solution)/shard_map/ppermute | solution.py:215
  8.0 12.7 %collective-permute-start = (bf16[256,512]{1,0:T(8,128)(2,1)S(1)}, bf16[256,512]{1,0:T(8,128)(2,1)S(1)}, u32[]{:S(2)}, u32[]{:S(2)}) collective-permute-start(bf16[256,512]{1,0:T(8,128)(2,1)S(1)} %dynamic-slice_bitcast_fusion.1), channel_id=1, source_target_pairs={{0,4},{4,0},{1,5},{5,1},{2,6},{6,2},{3,7},{7,3},{8,12},{12,8},{9,1... | collective-permute-start | bytes 786440 | tf_op jit(solution)/shard_map/ppermute | solution.py:216
  10.3 1.2 %copy-start.5 = (bf16[1024,512]{1,0:T(8,128)(2,1)S(1)}, bf16[1024,512]{1,0:T(8,128)(2,1)}, u32[]{:S(2)}) copy-start(bf16[1024,512]{1,0:T(8,128)(2,1)} %constant.50.clone.low_ref) | copy-start | bytes 3145732
  11.5 1.2 %copy-start.6 = (bf16[1024,512]{1,0:T(8,128)(2,1)S(1)}, bf16[1024,512]{1,0:T(8,128)(2,1)}, u32[]{:S(2)}) copy-start(bf16[1024,512]{1,0:T(8,128)(2,1)} %constant.49.clone.high_ref) | copy-start | bytes 3145732
  14.6 6.2 %copy-start.1 = (bf16[1,256,1024]{2,1,0:T(8,128)(2,1)S(1)}, bf16[1,256,1024]{2,1,0:T(8,128)(2,1)}, u32[]{:S(2)}) copy-start(bf16[1,256,1024]{2,1,0:T(8,128)(2,1)} %current_ref.1) | copy-start | bytes 1572868
  20.0 11.0 %copy-start = (bf16[1,1024,2048]{2,1,0:T(8,128)(2,1)S(1)}, bf16[1,1024,2048]{2,1,0:T(8,128)(2,1)}, u32[]{:S(2)}) copy-start(bf16[1,1024,2048]{2,1,0:T(8,128)(2,1)} %weight_ref.3) | copy-start | bytes 12582916
  21.5 9.5 %collective-permute-start.6 = (bf16[256,512]{1,0:T(8,128)(2,1)S(1)}, bf16[256,512]{1,0:T(8,128)(2,1)S(1)}, u32[]{:S(2)}, u32[]{:S(2)}) collective-permute-start(bf16[256,512]{1,0:T(8,128)(2,1)S(1)} %shard_map.104), channel_id=1, source_target_pairs={{0,12},{4,8},{8,20},{12,16},{16,28},{20,24},{24,4},{28,0},{1,13},{... | collective-permute-start | bytes 786440 | tf_op jit(solution)/shard_map/ppermute | solution.py:241
  22.3 8.7 %collective-permute-start.5 = (bf16[256,512]{1,0:T(8,128)(2,1)S(1)}, bf16[256,512]{1,0:T(8,128)(2,1)S(1)}, u32[]{:S(2)}, u32[]{:S(2)}) collective-permute-start(bf16[256,512]{1,0:T(8,128)(2,1)S(1)} %shard_map.105), channel_id=1, source_target_pairs={{0,8},{4,12},{8,16},{12,20},{16,24},{20,28},{24,0},{28,4},{1,9},{5... | collective-permute-start | bytes 786440 | tf_op jit(solution)/shard_map/ppermute | solution.py:241
  24.0 12.6 %collective-permute-start.3 = (bf16[256,512]{1,0:T(8,128)(2,1)S(1)}, bf16[256,512]{1,0:T(8,128)(2,1)S(1)}, u32[]{:S(2)}, u32[]{:S(2)}) collective-permute-start(bf16[256,512]{1,0:T(8,128)(2,1)S(1)} %shard_map.104), channel_id=1, source_target_pairs={{0,8},{4,12},{8,16},{12,20},{16,24},{20,28},{24,0},{28,4},{1,9},{5... | collective-permute-start | bytes 786440 | tf_op jit(solution)/shard_map/ppermute | solution.py:241
  24.0 12.6 %collective-permute-start.4 = (bf16[256,512]{1,0:T(8,128)(2,1)S(1)}, bf16[256,512]{1,0:T(8,128)(2,1)S(1)}, u32[]{:S(2)}, u32[]{:S(2)}) collective-permute-start(bf16[256,512]{1,0:T(8,128)(2,1)S(1)} %shard_map.105), channel_id=1, source_target_pairs={{0,12},{4,8},{8,20},{12,16},{16,28},{20,24},{24,4},{28,0},{1,13},{... | collective-permute-start | bytes 786440 | tf_op jit(solution)/shard_map/ppermute | solution.py:241
  36.6 9.2 %collective-permute-start.7 = (bf16[128,1024]{1,0:T(8,128)(2,1)S(1)}, bf16[128,1024]{1,0:T(8,128)(2,1)S(1)}, u32[]{:S(2)}, u32[]{:S(2)}) collective-permute-start(bf16[128,1024]{1,0:T(8,128)(2,1)S(1)} %get-tuple-element.28), channel_id=1, source_target_pairs={{0,1},{1,0},{2,3},{3,2},{4,5},{5,4},{6,7},{7,6},{8,9},{9,8},{10,11... | collective-permute-start | bytes 786440 | tf_op jit(solution)/shard_map/ppermute | solution.py:265
  40.0 11.7 %collective-permute-start.10 = (bf16[128,1024]{1,0:T(8,128)(2,1)S(1)}, bf16[128,1024]{1,0:T(8,128)(2,1)S(1)}, u32[]{:S(2)}, u32[]{:S(2)}) collective-permute-start(bf16[128,1024]{1,0:T(8,128)(2,1)S(1)} %get-tuple-element.33), channel_id=1, source_target_pairs={{0,5},{1,4},{2,7},{3,6},{4,1},{5,0},{6,3},{7,2},{8,13},{9,12},{10,... | collective-permute-start | bytes 786440 | tf_op jit(solution)/shard_map/ppermute | solution.py:266
  40.7 15.7 %collective-permute-start.11 = (bf16[128,1024]{1,0:T(8,128)(2,1)S(1)}, bf16[128,1024]{1,0:T(8,128)(2,1)S(1)}, u32[]{:S(2)}, u32[]{:S(2)}) collective-permute-start(bf16[128,1024]{1,0:T(8,128)(2,1)S(1)} %get-tuple-element.34), channel_id=1, source_target_pairs={{0,4},{4,0},{1,5},{5,1},{2,6},{6,2},{3,7},{7,3},{8,12},{12,8},{9,1... | collective-permute-start | bytes 786440 | tf_op jit(solution)/shard_map/ppermute | solution.py:267
  42.0 15.9 %collective-permute-start.9 = (bf16[128,1024]{1,0:T(8,128)(2,1)S(1)}, bf16[128,1024]{1,0:T(8,128)(2,1)S(1)}, u32[]{:S(2)}, u32[]{:S(2)}) collective-permute-start(bf16[128,1024]{1,0:T(8,128)(2,1)S(1)} %get-tuple-element.30), channel_id=1, source_target_pairs={{0,1},{1,0},{2,3},{3,2},{4,5},{5,4},{6,7},{7,6},{8,9},{9,8},{10,11... | collective-permute-start | bytes 786440 | tf_op jit(solution)/shard_map/ppermute | solution.py:265
  43.5 25.0 %collective-permute-start.14 = (bf16[128,1024]{1,0:T(8,128)(2,1)S(1)}, bf16[128,1024]{1,0:T(8,128)(2,1)S(1)}, u32[]{:S(2)}, u32[]{:S(2)}) collective-permute-start(bf16[128,1024]{1,0:T(8,128)(2,1)S(1)} %get-tuple-element.37), channel_id=1, source_target_pairs={{0,5},{1,4},{2,7},{3,6},{4,1},{5,0},{6,3},{7,2},{8,13},{9,12},{10,... | collective-permute-start | bytes 786440 | tf_op jit(solution)/shard_map/ppermute | solution.py:266
  45.9 22.7 %collective-permute-start.15 = (bf16[128,1024]{1,0:T(8,128)(2,1)S(1)}, bf16[128,1024]{1,0:T(8,128)(2,1)S(1)}, u32[]{:S(2)}, u32[]{:S(2)}) collective-permute-start(bf16[128,1024]{1,0:T(8,128)(2,1)S(1)} %get-tuple-element.38), channel_id=1, source_target_pairs={{0,4},{4,0},{1,5},{5,1},{2,6},{6,2},{3,7},{7,3},{8,12},{12,8},{9,1... | collective-permute-start | bytes 786440 | tf_op jit(solution)/shard_map/ppermute | solution.py:267
  51.7 18.2 %collective-permute-start.8 = (bf16[128,1024]{1,0:T(8,128)(2,1)S(1)}, bf16[128,1024]{1,0:T(8,128)(2,1)S(1)}, u32[]{:S(2)}, u32[]{:S(2)}) collective-permute-start(bf16[128,1024]{1,0:T(8,128)(2,1)S(1)} %shard_map.107), channel_id=1, source_target_pairs={{2,0},{3,1},{4,6},{5,7},{10,8},{11,9},{12,14},{13,15},{18,16},{19,... | collective-permute-start | bytes 786440 | tf_op jit(solution)/shard_map/ppermute | solution.py:278
  56.5 17.2 %collective-permute-start.13 = (bf16[128,1024]{1,0:T(8,128)(2,1)S(1)}, bf16[128,1024]{1,0:T(8,128)(2,1)S(1)}, u32[]{:S(2)}, u32[]{:S(2)}) collective-permute-start(bf16[128,1024]{1,0:T(8,128)(2,1)S(1)} %shard_map.109), channel_id=1, source_target_pairs={{0,2},{1,3},{6,4},{7,5},{8,10},{9,11},{14,12},{15,13},{16,18},{17,... | collective-permute-start | bytes 786440 | tf_op jit(solution)/shard_map/ppermute | solution.py:278
  57.9 13.4 %collective-permute-start.12 = (bf16[128,1024]{1,0:T(8,128)(2,1)S(1)}, bf16[128,1024]{1,0:T(8,128)(2,1)S(1)}, u32[]{:S(2)}, u32[]{:S(2)}) collective-permute-start(bf16[128,1024]{1,0:T(8,128)(2,1)S(1)} %shard_map.110), channel_id=1, source_target_pairs={{2,0},{3,1},{4,6},{5,7},{10,8},{11,9},{12,14},{13,15},{18,16},{19,... | collective-permute-start | bytes 786440 | tf_op jit(solution)/shard_map/ppermute | solution.py:278
  68.7 13.0 %collective-permute-start.16 = (bf16[128,1024]{1,0:T(8,128)(2,1)S(1)}, bf16[128,1024]{1,0:T(8,128)(2,1)S(1)}, u32[]{:S(2)}, u32[]{:S(2)}) collective-permute-start(bf16[128,1024]{1,0:T(8,128)(2,1)S(1)} %shard_map.111), channel_id=1, source_target_pairs={{0,2},{1,3},{6,4},{7,5},{8,10},{9,11},{14,12},{15,13},{16,18},{17,... | collective-permute-start | bytes 786440 | tf_op jit(solution)/shard_map/ppermute | solution.py:278

commit v5 on v4

--- a/solution.py
+++ b/solution.py
@@ -14,7 +14,7 @@
 BF16 = jnp.bfloat16
 EXTRA = 16
 VMEM_LIMIT = 24 * 2**20
-LANES = 256
+LANES = 512
 WIDE = 512
 OWN, CROSS = 2, 2
 ORDER = [(0, 0, None), (1, 0, None), (0, 1, (1, 0)), (1, 1, (0, 1))]

time: 83.6 us -> 83.6 us (level)
  no operation moved by 1% of the time
where the time goes in v5:
time: 83.6 us; the launch traced here: 83.2 us
  waiting for transfers between devices  34.3 us (41%)
  starting transfers between devices  26.9 us (32%)
  Pallas kernels  14.3 us (17%)
  local copies, waits for them, and re-layouts  7.34 us (9%)
    ppermute x4, starting transfers between devices, two_by_four(): groups += [*pairs[role][c], lax.ppermute(sums[role, c], ('ctx', 'mp'), far)]  14.7 us
    pallas_call x13, Pallas kernels, local(): pl.pallas_call(kernel, out_shape=out_shape, in_specs=[pl.BlockSpec(memory...  14.3 us
    ppermute x4, waiting for transfers between devices, two_by_four(): groups += [*pairs[role][c], lax.ppermute(sums[role, c], ('ctx', 'mp'), far)]  11.7 us
    ppermute x4, waiting for transfers between devices, to_next(): return lax.ppermute(array, ('section', 'ctx'), pairs)  9.11 us
    ppermute x2, waiting for transfers between devices, two_by_four(): lax.ppermute(piece, ('ctx', 'mp'), diagonal)  8.33 us
    unnamed x22, local copies, waits for them, and re-layouts  5.33 us
    ppermute x4, starting transfers between devices, to_next(): return lax.ppermute(array, ('section', 'ctx'), pairs)  3.42 us
    ppermute x2, starting transfers between devices, two_by_four(): own_near = [lax.ppermute(piece, 'mp', near) for piece in owned[:OWN]]  3.15 us
  transfers between devices with their start and end apart: 17, of which 11 were waited for; matrix products, arithmetic and copies ran while one was open for 1% of the time, Pallas kernels for 14%

profile of v5, /device:TPU:2, one launch (start us, length us, event | category | flops | bytes accessed | tf_op | source)
XLA Modules:
  0.0 83.2 jit_solution(17935726126365204337)
XLA Ops:
  0.0 1.0 %dynamic-slice_bitcast_fusion = bf16[256,512]{1,0:T(8,128)(2,1)S(1)} fusion(bf16[1,256,1024]{2,1,0:T(8,128)(2,1)} %own_ref.1, s32[]{:T(128)S(6)} %select_n.17), kind=kLoop, calls=%fused_computation | loop fusion | bytes 524292 | tf_op jit(solution)/shard_map/dynamic_slice | solution.py:210
  1.1 0.1 collective-permute-start.2
  1.2 0.1 pad_add_fusion.place
  1.2 1.0 %copy-done.2 = bf16[1,256,1024]{2,1,0:T(8,128)(2,1)S(1)} copy-done((bf16[1,256,1024]{2,1,0:T(8,128)(2,1)S(1)}, bf16[1,256,1024]{2,1,0:T(8,128)(2,1)}, u32[]{:S(2)}) %copy-start.2) | copy-done | bytes 524312
  2.3 1.0 %copy-done.3 = bf16[1,256,1024]{2,1,0:T(8,128)(2,1)S(1)} copy-done((bf16[1,256,1024]{2,1,0:T(8,128)(2,1)S(1)}, bf16[1,256,1024]{2,1,0:T(8,128)(2,1)}, u32[]{:S(2)}) %copy-start.3) | copy-done | bytes 524312
  3.3 0.8 copy-done.7
  4.1 1.0 %shard_map.101 = bf16[272,512]{1,0:T(8,128)(2,1)S(1)} custom-call(s32[3]{0:T(128)S(1)} %pad_add_fusion.place, bf16[1,256,1024]{2,1,0:T(8,128)(2,1)S(1)} %copy-done.2, bf16[1,256,1024]{2,1,0:T(8,128)(2,1)S(1)} %copy-done.3, f32[3,3,1,1024]{3,2,1,0:T(1,128)S(1)} %bitcast.8), custom_call_target="tpu_custom_call" | custom-call | flops 2621440 | bytes 1363980 | tf_op jit(solution)/shard_map/pallas_call | solution.py:180
  5.1 2.1 %collective-permute-start.1 = (bf16[272,512]{1,0:T(8,128)(2,1)S(1)}, bf16[272,512]{1,0:T(8,128)(2,1)S(1)}, u32[]{:S(2)}, u32[]{:S(2)}) collective-permute-start(bf16[272,512]{1,0:T(8,128)(2,1)S(1)} %shard_map.101), channel_id=1, source_target_pairs={{0,4},{4,0},{1,5},{5,1},{2,6},{6,2},{3,7},{7,3},{8,12},{12,8},{9,1... | collective-permute-start | bytes 835592 | tf_op jit(solution)/shard_map/ppermute | solution.py:215
  7.1 1.0 %dynamic-slice_bitcast_fusion.1 = bf16[256,512]{1,0:T(8,128)(2,1)S(1)} fusion(bf16[1,256,1024]{2,1,0:T(8,128)(2,1)} %current_ref.1, s32[]{:T(128)S(6)} %select_n.17), kind=kLoop, calls=%fused_computation.1 | loop fusion | bytes 524292 | tf_op jit(solution)/shard_map/dynamic_slice | solution.py:210
  8.1 0.1 collective-permute-start
  8.2 1.0 %shard_map.100.own_ref = bf16[272,512]{1,0:T(8,128)(2,1)S(1)} custom-call(s32[3]{0:T(128)S(1)} %pad_add_fusion.place, bf16[1,256,1024]{2,1,0:T(8,128)(2,1)S(1)} %copy-done.2, bf16[1,256,1024]{2,1,0:T(8,128)(2,1)S(1)} %copy-done.3, f32[3,3,1,1024]{3,2,1,0:T(1,128)S(1)} %bitcast.9), custom_call_target="tpu_custom_call" | custom-call | flops 2621440 | bytes 1363980 | tf_op jit(solution)/shard_map/pallas_call | solution.py:180
  9.2 1.2 %collective-permute-done.2.come_ref = bf16[256,512]{1,0:T(8,128)(2,1)S(1)} collective-permute-done((bf16[256,512]{1,0:T(8,128)(2,1)S(1)}, bf16[256,512]{1,0:T(8,128)(2,1)S(1)}, u32[]{:S(2)}, u32[]{:S(2)}) %collective-permute-start.2) | collective-permute-done | bytes 262176 | tf_op jit(solution)/shard_map/ppermute | solution.py:212
  10.3 1.2 %copy-done.5 = bf16[1024,512]{1,0:T(8,128)(2,1)S(1)} copy-done((bf16[1024,512]{1,0:T(8,128)(2,1)S(1)}, bf16[1024,512]{1,0:T(8,128)(2,1)}, u32[]{:S(2)}) %copy-start.5) | copy-done | bytes 1048600
  11.5 1.2 %copy-done.6 = bf16[1024,512]{1,0:T(8,128)(2,1)S(1)} copy-done((bf16[1024,512]{1,0:T(8,128)(2,1)S(1)}, bf16[1024,512]{1,0:T(8,128)(2,1)}, u32[]{:S(2)}) %copy-start.6) | copy-done | bytes 1048600
  12.8 1.8 %shard_map.102.spec_ref = f32[1024,512]{1,0:T(8,128)S(1)} custom-call(s32[3]{0:T(128)S(1)} %pad_add_fusion.place, bf16[1,256,1024]{2,1,0:T(8,128)(2,1)S(1)} %copy-done.4, bf16[256,512]{1,0:T(8,128)(2,1)S(1)} %collective-permute-done.2.come_ref, bf16[1024,512]{1,0:T(8,128)(2,1)S(1)} %copy-done.6, bf16[1024,512]{1,0:T(8,128)(2,1)S(1)} %copy-done.5), custom_call_target="tpu_custom_call" | custom-call | flops 1073741824 | bytes 4980748 | tf_op jit(solution)/shard_map/pallas_call | solution.py:180
  14.6 1.7 %collective-permute-done.1.come_ref = bf16[272,512]{1,0:T(8,128)(2,1)S(1)} collective-permute-done((bf16[272,512]{1,0:T(8,128)(2,1)S(1)}, bf16[272,512]{1,0:T(8,128)(2,1)S(1)}, u32[]{:S(2)}, u32[]{:S(2)}) %collective-permute-start.1) | collective-permute-done | bytes 278560 | tf_op jit(solution)/shard_map/ppermute | solution.py:215
  16.3 3.7 %shard_map.103.conv_ref = f32[512,512]{1,0:T(8,128)S(1)} custom-call(s32[3]{0:T(128)S(1)} %pad_add_fusion.place, bf16[272,512]{1,0:T(8,128)(2,1)S(1)} %shard_map.100.own_ref, bf16[272,512]{1,0:T(8,128)(2,1)S(1)} %collective-permute-done.1.come_ref, f32[3,3,1,1024]{3,2,1,0:T(1,128)S(1)} %bitcast.10, f32[1024,512]{1,0:T(8,128)S(1)} %shard_map.102.spec_ref, ...), custom_call_target="tpu_custom_call" | custom-call | flops 2684354560 | bytes 7933964 | tf_op jit(solution)/shard_map/pallas_call | solution.py:180
  20.0 0.7 collective-permute-done.current_ref.previous_ref
  20.8 0.7 shard_map.104
  21.5 0.1 collective-permute-start.6
  21.6 0.8 shard_map.105
  22.3 1.6 %collective-permute-start.5 = (bf16[256,512]{1,0:T(8,128)(2,1)S(1)}, bf16[256,512]{1,0:T(8,128)(2,1)S(1)}, u32[]{:S(2)}, u32[]{:S(2)}) collective-permute-start(bf16[256,512]{1,0:T(8,128)(2,1)S(1)} %shard_map.105), channel_id=1, source_target_pairs={{0,8},{4,12},{8,16},{12,20},{16,24},{20,28},{24,0},{28,4},{1,9},{5... | collective-permute-start | bytes 786440 | tf_op jit(solution)/shard_map/ppermute | solution.py:241
  24.0 0.1 collective-permute-start.3
  24.0 1.7 %collective-permute-start.4 = (bf16[256,512]{1,0:T(8,128)(2,1)S(1)}, bf16[256,512]{1,0:T(8,128)(2,1)S(1)}, u32[]{:S(2)}, u32[]{:S(2)}) collective-permute-start(bf16[256,512]{1,0:T(8,128)(2,1)S(1)} %shard_map.105), channel_id=1, source_target_pairs={{0,12},{4,8},{8,20},{12,16},{16,28},{20,24},{24,4},{28,0},{1,13},{... | collective-permute-start | bytes 786440 | tf_op jit(solution)/shard_map/ppermute | solution.py:241
  25.7 5.3 %collective-permute-done.6.cross_ref = bf16[256,512]{1,0:T(8,128)(2,1)S(1)} collective-permute-done((bf16[256,512]{1,0:T(8,128)(2,1)S(1)}, bf16[256,512]{1,0:T(8,128)(2,1)S(1)}, u32[]{:S(2)}, u32[]{:S(2)}) %collective-permute-start.6) | collective-permute-done | bytes 262176 | tf_op jit(solution)/shard_map/ppermute | solution.py:241
  31.0 1.8 %shard_map.106 = (bf16[128,1024]{1,0:T(8,128)(2,1)S(1)}, bf16[128,1024]{1,0:T(8,128)(2,1)S(1)}, f32[128,1024]{1,0:T(8,128)S(1)}, f32[128,1024]{1,0:T(8,128)S(1)}) custom-call(s32[3]{0:T(128)S(1)} %pad_add_fusion.place, bf16[256,512]{1,0:T(8,128)(2,1)S(1)} %collective-permute-done.5.same_ref, bf16[256,512]{1,0:T(8,128)(2,1)S(1)} %collective-permute-done.6.cross_ref, ...), custom_call_target="tpu_custom_call" | custom-call | flops 1073741824 | bytes 6291468 | tf_op jit(solution)/shard_map/pallas_call | solution.py:180
  32.8 3.8 %collective-permute-done.3.same_ref = bf16[256,512]{1,0:T(8,128)(2,1)S(1)} collective-permute-done((bf16[256,512]{1,0:T(8,128)(2,1)S(1)}, bf16[256,512]{1,0:T(8,128)(2,1)S(1)}, u32[]{:S(2)}, u32[]{:S(2)}) %collective-permute-start.3) | collective-permute-done | bytes 262176 | tf_op jit(solution)/shard_map/ppermute | solution.py:241
  36.6 1.6 %collective-permute-start.7 = (bf16[128,1024]{1,0:T(8,128)(2,1)S(1)}, bf16[128,1024]{1,0:T(8,128)(2,1)S(1)}, u32[]{:S(2)}, u32[]{:S(2)}) collective-permute-start(bf16[128,1024]{1,0:T(8,128)(2,1)S(1)} %get-tuple-element.28), channel_id=1, source_target_pairs={{0,1},{1,0},{2,3},{3,2},{4,5},{5,4},{6,7},{7,6},{8,9},{9,8},{10,11... | collective-permute-start | bytes 786440 | tf_op jit(solution)/shard_map/ppermute | solution.py:265
  38.2 1.8 %shard_map.108 = (bf16[128,1024]{1,0:T(8,128)(2,1)S(1)}, bf16[128,1024]{1,0:T(8,128)(2,1)S(1)}, bf16[128,1024]{1,0:T(8,128)(2,1)S(1)}, bf16[128,1024]{1,0:T(8,128)(2,1)S(1)}) custom-call(s32[3]{0:T(128)S(1)} %pad_add_fusion.place, bf16[256,512]{1,0:T(8,128)(2,1)S(1)} %collective-permute-done.3.same_ref, ...), custom_call_target="tpu_custom_call" | custom-call | flops 1073741824 | bytes 5767180 | tf_op jit(solution)/shard_map/pallas_call | solution.py:180
  40.0 0.7 collective-permute-start.10
  40.7 1.2 %collective-permute-start.11 = (bf16[128,1024]{1,0:T(8,128)(2,1)S(1)}, bf16[128,1024]{1,0:T(8,128)(2,1)S(1)}, u32[]{:S(2)}, u32[]{:S(2)}) collective-permute-start(bf16[128,1024]{1,0:T(8,128)(2,1)S(1)} %get-tuple-element.34), channel_id=1, source_target_pairs={{0,4},{4,0},{1,5},{5,1},{2,6},{6,2},{3,7},{7,3},{8,12},{12,8},{9,1... | collective-permute-start | bytes 786440 | tf_op jit(solution)/shard_map/ppermute | solution.py:267
  42.0 1.6 %collective-permute-start.9 = (bf16[128,1024]{1,0:T(8,128)(2,1)S(1)}, bf16[128,1024]{1,0:T(8,128)(2,1)S(1)}, u32[]{:S(2)}, u32[]{:S(2)}) collective-permute-start(bf16[128,1024]{1,0:T(8,128)(2,1)S(1)} %get-tuple-element.30), channel_id=1, source_target_pairs={{0,1},{1,0},{2,3},{3,2},{4,5},{5,4},{6,7},{7,6},{8,9},{9,8},{10,11... | collective-permute-start | bytes 786440 | tf_op jit(solution)/shard_map/ppermute | solution.py:265
  43.5 0.7 collective-permute-start.14
  44.2 1.6 %collective-permute-done.7.two_ref.refs_1_ = bf16[128,1024]{1,0:T(8,128)(2,1)S(1)} collective-permute-done((bf16[128,1024]{1,0:T(8,128)(2,1)S(1)}, bf16[128,1024]{1,0:T(8,128)(2,1)S(1)}, u32[]{:S(2)}, u32[]{:S(2)}) %collective-permute-start.7) | collective-permute-done | bytes 262176 | tf_op jit(solution)/shard_map/ppermute | solution.py:265
  45.9 0.8 collective-permute-start.15
  46.7 5.1 %collective-permute-done.10.one_ref.refs_6_ = bf16[128,1024]{1,0:T(8,128)(2,1)S(1)} collective-permute-done((bf16[128,1024]{1,0:T(8,128)(2,1)S(1)}, bf16[128,1024]{1,0:T(8,128)(2,1)S(1)}, u32[]{:S(2)}, u32[]{:S(2)}) %collective-permute-start.10) | collective-permute-done | bytes 262176 | tf_op jit(solution)/shard_map/ppermute | solution.py:266
  51.7 4.7 %collective-permute-start.8 = (bf16[128,1024]{1,0:T(8,128)(2,1)S(1)}, bf16[128,1024]{1,0:T(8,128)(2,1)S(1)}, u32[]{:S(2)}, u32[]{:S(2)}) collective-permute-start(bf16[128,1024]{1,0:T(8,128)(2,1)S(1)} %shard_map.107), channel_id=1, source_target_pairs={{2,0},{3,1},{4,6},{5,7},{10,8},{11,9},{12,14},{13,15},{18,16},{19,... | collective-permute-start | bytes 786440 | tf_op jit(solution)/shard_map/ppermute | solution.py:278
  56.5 0.1 shard_map.109
  56.5 1.3 %collective-permute-start.13 = (bf16[128,1024]{1,0:T(8,128)(2,1)S(1)}, bf16[128,1024]{1,0:T(8,128)(2,1)S(1)}, u32[]{:S(2)}, u32[]{:S(2)}) collective-permute-start(bf16[128,1024]{1,0:T(8,128)(2,1)S(1)} %shard_map.109), channel_id=1, source_target_pairs={{0,2},{1,3},{6,4},{7,5},{8,10},{9,11},{14,12},{15,13},{16,18},{17,... | collective-permute-start | bytes 786440 | tf_op jit(solution)/shard_map/ppermute | solution.py:278
  57.8 0.1 shard_map.110
  57.9 7.4 %collective-permute-start.12 = (bf16[128,1024]{1,0:T(8,128)(2,1)S(1)}, bf16[128,1024]{1,0:T(8,128)(2,1)S(1)}, u32[]{:S(2)}, u32[]{:S(2)}) collective-permute-start(bf16[128,1024]{1,0:T(8,128)(2,1)S(1)} %shard_map.110), channel_id=1, source_target_pairs={{2,0},{3,1},{4,6},{5,7},{10,8},{11,9},{12,14},{13,15},{18,16},{19,... | collective-permute-start | bytes 786440 | tf_op jit(solution)/shard_map/ppermute | solution.py:278
  65.3 3.3 %collective-permute-done.14.one_ref.refs_9_ = bf16[128,1024]{1,0:T(8,128)(2,1)S(1)} collective-permute-done((bf16[128,1024]{1,0:T(8,128)(2,1)S(1)}, bf16[128,1024]{1,0:T(8,128)(2,1)S(1)}, u32[]{:S(2)}, u32[]{:S(2)}) %collective-permute-start.14) | collective-permute-done | bytes 262176 | tf_op jit(solution)/shard_map/ppermute | solution.py:266
  68.6 0.1 shard_map.111
  68.7 1.3 %collective-permute-start.16 = (bf16[128,1024]{1,0:T(8,128)(2,1)S(1)}, bf16[128,1024]{1,0:T(8,128)(2,1)S(1)}, u32[]{:S(2)}, u32[]{:S(2)}) collective-permute-start(bf16[128,1024]{1,0:T(8,128)(2,1)S(1)} %shard_map.111), channel_id=1, source_target_pairs={{0,2},{1,3},{6,4},{7,5},{8,10},{9,11},{14,12},{15,13},{16,18},{17,... | collective-permute-start | bytes 786440 | tf_op jit(solution)/shard_map/ppermute | solution.py:278
  70.0 1.3 %collective-permute-done.12.refs_5_ = bf16[128,1024]{1,0:T(8,128)(2,1)S(1)} collective-permute-done((bf16[128,1024]{1,0:T(8,128)(2,1)S(1)}, bf16[128,1024]{1,0:T(8,128)(2,1)S(1)}, u32[]{:S(2)}, u32[]{:S(2)}) %collective-permute-start.12) | collective-permute-done | bytes 262176 | tf_op jit(solution)/shard_map/ppermute | solution.py:278
  71.3 2.5 %collective-permute-done.13.refs_8_ = bf16[128,1024]{1,0:T(8,128)(2,1)S(1)} collective-permute-done((bf16[128,1024]{1,0:T(8,128)(2,1)S(1)}, bf16[128,1024]{1,0:T(8,128)(2,1)S(1)}, u32[]{:S(2)}, u32[]{:S(2)}) %collective-permute-start.13) | collective-permute-done | bytes 262176 | tf_op jit(solution)/shard_map/ppermute | solution.py:278
  73.8 7.9 %collective-permute-done.16.refs_11_ = bf16[128,1024]{1,0:T(8,128)(2,1)S(1)} collective-permute-done((bf16[128,1024]{1,0:T(8,128)(2,1)S(1)}, bf16[128,1024]{1,0:T(8,128)(2,1)S(1)}, u32[]{:S(2)}, u32[]{:S(2)}) %collective-permute-start.16) | collective-permute-done | bytes 262176 | tf_op jit(solution)/shard_map/ppermute | solution.py:278
  81.6 1.5 %shard_map.112 = bf16[1,256,1024]{2,1,0:T(8,128)(2,1)} custom-call(s32[3]{0:T(128)S(1)} %pad_add_fusion.place, f32[128,1024]{1,0:T(8,128)S(1)} %get-tuple-element.27.one_ref.refs_0_, bf16[128,1024]{1,0:T(8,128)(2,1)S(1)} %collective-permute-done.7.two_ref.refs_1_, bf16[128,1024]{1,0:T(8,128)(2,1)S(1)} %collective-permute-done.8.refs_2_, ...), custom_call_target="tpu_custom_call" | custom-call | flops 786432 | bytes 4194316 | tf_op jit(solution)/shard_map/pallas_call | solution.py:180
  (24 shorter events, 0.1 us)
Async XLA Ops:
  0.0 10.3 %copy-start.4 = (bf16[1,256,1024]{2,1,0:T(8,128)(2,1)S(1)}, bf16[1,256,1024]{2,1,0:T(8,128)(2,1)}, u32[]{:S(2)}) copy-start(bf16[1,256,1024]{2,1,0:T(8,128)(2,1)} %own_ref.1) | copy-start | bytes 1572868
  1.0 15.2 %copy-start.8 = (f32[1,3,3,1024]{3,0,2,1:T(1,128)S(1)}, f32[1,3,3,1024]{3,0,2,1:T(1,128)}, u32[]{:S(2)}) copy-start(f32[1,3,3,1024]{3,0,2,1:T(1,128)} %param.14) | copy-start | bytes 110596
  1.1 9.3 %collective-permute-start.2 = (bf16[256,512]{1,0:T(8,128)(2,1)S(1)}, bf16[256,512]{1,0:T(8,128)(2,1)S(1)}, u32[]{:S(2)}, u32[]{:S(2)}) collective-permute-start(bf16[256,512]{1,0:T(8,128)(2,1)S(1)} %dynamic-slice_bitcast_fusion), channel_id=1, source_target_pairs={{0,4},{4,0},{1,5},{5,1},{2,6},{6,2},{3,7},{7,3},{8,12},{12,8},{9,1... | collective-permute-start | bytes 786440 | tf_op jit(solution)/shard_map/ppermute | solution.py:212
  1.2 1.0 %copy-start.2 = (bf16[1,256,1024]{2,1,0:T(8,128)(2,1)S(1)}, bf16[1,256,1024]{2,1,0:T(8,128)(2,1)}, u32[]{:S(2)}) copy-start(bf16[1,256,1024]{2,1,0:T(8,128)(2,1)} %key_ref.3) | copy-start | bytes 1572868
  2.3 1.0 %copy-start.3 = (bf16[1,256,1024]{2,1,0:T(8,128)(2,1)S(1)}, bf16[1,256,1024]{2,1,0:T(8,128)(2,1)}, u32[]{:S(2)}) copy-start(bf16[1,256,1024]{2,1,0:T(8,128)(2,1)} %value_ref.3) | copy-start | bytes 1572868
  3.3 0.8 copy-start.7
  4.1 12.2 %copy-start.9 = (bf16[512,1024]{1,0:T(8,128)(2,1)S(1)}, bf16[512,1024]{1,0:T(8,128)(2,1)}, u32[]{:S(2)}) copy-start(bf16[512,1024]{1,0:T(8,128)(2,1)} %constant.52.clone.back_low_ref) | copy-start | bytes 3145732
  4.1 12.2 %copy-start.10 = (bf16[512,1024]{1,0:T(8,128)(2,1)S(1)}, bf16[512,1024]{1,0:T(8,128)(2,1)}, u32[]{:S(2)}) copy-start(bf16[512,1024]{1,0:T(8,128)(2,1)} %constant.51.clone.back_high_ref) | copy-start | bytes 3145732
  5.1 11.2 %collective-permute-start.1 = (bf16[272,512]{1,0:T(8,128)(2,1)S(1)}, bf16[272,512]{1,0:T(8,128)(2,1)S(1)}, u32[]{:S(2)}, u32[]{:S(2)}) collective-permute-start(bf16[272,512]{1,0:T(8,128)(2,1)S(1)} %shard_map.101), channel_id=1, source_target_pairs={{0,4},{4,0},{1,5},{5,1},{2,6},{6,2},{3,7},{7,3},{8,12},{12,8},{9,1... | collective-permute-start | bytes 835592 | tf_op jit(solution)/shard_map/ppermute | solution.py:215
  8.1 12.7 %collective-permute-start = (bf16[256,512]{1,0:T(8,128)(2,1)S(1)}, bf16[256,512]{1,0:T(8,128)(2,1)S(1)}, u32[]{:S(2)}, u32[]{:S(2)}) collective-permute-start(bf16[256,512]{1,0:T(8,128)(2,1)S(1)} %dynamic-slice_bitcast_fusion.1), channel_id=1, source_target_pairs={{0,4},{4,0},{1,5},{5,1},{2,6},{6,2},{3,7},{7,3},{8,12},{12,8},{9,1... | collective-permute-start | bytes 786440 | tf_op jit(solution)/shard_map/ppermute | solution.py:216
  10.3 1.2 %copy-start.5 = (bf16[1024,512]{1,0:T(8,128)(2,1)S(1)}, bf16[1024,512]{1,0:T(8,128)(2,1)}, u32[]{:S(2)}) copy-start(bf16[1024,512]{1,0:T(8,128)(2,1)} %constant.50.clone.low_ref) | copy-start | bytes 3145732
  11.5 1.2 %copy-start.6 = (bf16[1024,512]{1,0:T(8,128)(2,1)S(1)}, bf16[1024,512]{1,0:T(8,128)(2,1)}, u32[]{:S(2)}) copy-start(bf16[1024,512]{1,0:T(8,128)(2,1)} %constant.49.clone.high_ref) | copy-start | bytes 3145732
  14.6 6.2 %copy-start.1 = (bf16[1,256,1024]{2,1,0:T(8,128)(2,1)S(1)}, bf16[1,256,1024]{2,1,0:T(8,128)(2,1)}, u32[]{:S(2)}) copy-start(bf16[1,256,1024]{2,1,0:T(8,128)(2,1)} %current_ref.1) | copy-start | bytes 1572868
  20.0 11.0 %copy-start = (bf16[1,1024,2048]{2,1,0:T(8,128)(2,1)S(1)}, bf16[1,1024,2048]{2,1,0:T(8,128)(2,1)}, u32[]{:S(2)}) copy-start(bf16[1,1024,2048]{2,1,0:T(8,128)(2,1)} %weight_ref.3) | copy-start | bytes 12582916
  21.5 9.5 %collective-permute-start.6 = (bf16[256,512]{1,0:T(8,128)(2,1)S(1)}, bf16[256,512]{1,0:T(8,128)(2,1)S(1)}, u32[]{:S(2)}, u32[]{:S(2)}) collective-permute-start(bf16[256,512]{1,0:T(8,128)(2,1)S(1)} %shard_map.104), channel_id=1, source_target_pairs={{0,12},{4,8},{8,20},{12,16},{16,28},{20,24},{24,4},{28,0},{1,13},{... | collective-permute-start | bytes 786440 | tf_op jit(solution)/shard_map/ppermute | solution.py:241
  22.3 8.7 %collective-permute-start.5 = (bf16[256,512]{1,0:T(8,128)(2,1)S(1)}, bf16[256,512]{1,0:T(8,128)(2,1)S(1)}, u32[]{:S(2)}, u32[]{:S(2)}) collective-permute-start(bf16[256,512]{1,0:T(8,128)(2,1)S(1)} %shard_map.105), channel_id=1, source_target_pairs={{0,8},{4,12},{8,16},{12,20},{16,24},{20,28},{24,0},{28,4},{1,9},{5... | collective-permute-start | bytes 786440 | tf_op jit(solution)/shard_map/ppermute | solution.py:241
  24.0 12.6 %collective-permute-start.3 = (bf16[256,512]{1,0:T(8,128)(2,1)S(1)}, bf16[256,512]{1,0:T(8,128)(2,1)S(1)}, u32[]{:S(2)}, u32[]{:S(2)}) collective-permute-start(bf16[256,512]{1,0:T(8,128)(2,1)S(1)} %shard_map.104), channel_id=1, source_target_pairs={{0,8},{4,12},{8,16},{12,20},{16,24},{20,28},{24,0},{28,4},{1,9},{5... | collective-permute-start | bytes 786440 | tf_op jit(solution)/shard_map/ppermute | solution.py:241
  24.0 12.6 %collective-permute-start.4 = (bf16[256,512]{1,0:T(8,128)(2,1)S(1)}, bf16[256,512]{1,0:T(8,128)(2,1)S(1)}, u32[]{:S(2)}, u32[]{:S(2)}) collective-permute-start(bf16[256,512]{1,0:T(8,128)(2,1)S(1)} %shard_map.105), channel_id=1, source_target_pairs={{0,12},{4,8},{8,20},{12,16},{16,28},{20,24},{24,4},{28,0},{1,13},{... | collective-permute-start | bytes 786440 | tf_op jit(solution)/shard_map/ppermute | solution.py:241
  36.6 9.2 %collective-permute-start.7 = (bf16[128,1024]{1,0:T(8,128)(2,1)S(1)}, bf16[128,1024]{1,0:T(8,128)(2,1)S(1)}, u32[]{:S(2)}, u32[]{:S(2)}) collective-permute-start(bf16[128,1024]{1,0:T(8,128)(2,1)S(1)} %get-tuple-element.28), channel_id=1, source_target_pairs={{0,1},{1,0},{2,3},{3,2},{4,5},{5,4},{6,7},{7,6},{8,9},{9,8},{10,11... | collective-permute-start | bytes 786440 | tf_op jit(solution)/shard_map/ppermute | solution.py:265
  40.0 11.7 %collective-permute-start.10 = (bf16[128,1024]{1,0:T(8,128)(2,1)S(1)}, bf16[128,1024]{1,0:T(8,128)(2,1)S(1)}, u32[]{:S(2)}, u32[]{:S(2)}) collective-permute-start(bf16[128,1024]{1,0:T(8,128)(2,1)S(1)} %get-tuple-element.33), channel_id=1, source_target_pairs={{0,5},{1,4},{2,7},{3,6},{4,1},{5,0},{6,3},{7,2},{8,13},{9,12},{10,... | collective-permute-start | bytes 786440 | tf_op jit(solution)/shard_map/ppermute | solution.py:266
  40.7 15.7 %collective-permute-start.11 = (bf16[128,1024]{1,0:T(8,128)(2,1)S(1)}, bf16[128,1024]{1,0:T(8,128)(2,1)S(1)}, u32[]{:S(2)}, u32[]{:S(2)}) collective-permute-start(bf16[128,1024]{1,0:T(8,128)(2,1)S(1)} %get-tuple-element.34), channel_id=1, source_target_pairs={{0,4},{4,0},{1,5},{5,1},{2,6},{6,2},{3,7},{7,3},{8,12},{12,8},{9,1... | collective-permute-start | bytes 786440 | tf_op jit(solution)/shard_map/ppermute | solution.py:267
  42.0 15.9 %collective-permute-start.9 = (bf16[128,1024]{1,0:T(8,128)(2,1)S(1)}, bf16[128,1024]{1,0:T(8,128)(2,1)S(1)}, u32[]{:S(2)}, u32[]{:S(2)}) collective-permute-start(bf16[128,1024]{1,0:T(8,128)(2,1)S(1)} %get-tuple-element.30), channel_id=1, source_target_pairs={{0,1},{1,0},{2,3},{3,2},{4,5},{5,4},{6,7},{7,6},{8,9},{9,8},{10,11... | collective-permute-start | bytes 786440 | tf_op jit(solution)/shard_map/ppermute | solution.py:265
  43.5 25.0 %collective-permute-start.14 = (bf16[128,1024]{1,0:T(8,128)(2,1)S(1)}, bf16[128,1024]{1,0:T(8,128)(2,1)S(1)}, u32[]{:S(2)}, u32[]{:S(2)}) collective-permute-start(bf16[128,1024]{1,0:T(8,128)(2,1)S(1)} %get-tuple-element.37), channel_id=1, source_target_pairs={{0,5},{1,4},{2,7},{3,6},{4,1},{5,0},{6,3},{7,2},{8,13},{9,12},{10,... | collective-permute-start | bytes 786440 | tf_op jit(solution)/shard_map/ppermute | solution.py:266
  45.9 22.7 %collective-permute-start.15 = (bf16[128,1024]{1,0:T(8,128)(2,1)S(1)}, bf16[128,1024]{1,0:T(8,128)(2,1)S(1)}, u32[]{:S(2)}, u32[]{:S(2)}) collective-permute-start(bf16[128,1024]{1,0:T(8,128)(2,1)S(1)} %get-tuple-element.38), channel_id=1, source_target_pairs={{0,4},{4,0},{1,5},{5,1},{2,6},{6,2},{3,7},{7,3},{8,12},{12,8},{9,1... | collective-permute-start | bytes 786440 | tf_op jit(solution)/shard_map/ppermute | solution.py:267
  51.7 18.2 %collective-permute-start.8 = (bf16[128,1024]{1,0:T(8,128)(2,1)S(1)}, bf16[128,1024]{1,0:T(8,128)(2,1)S(1)}, u32[]{:S(2)}, u32[]{:S(2)}) collective-permute-start(bf16[128,1024]{1,0:T(8,128)(2,1)S(1)} %shard_map.107), channel_id=1, source_target_pairs={{2,0},{3,1},{4,6},{5,7},{10,8},{11,9},{12,14},{13,15},{18,16},{19,... | collective-permute-start | bytes 786440 | tf_op jit(solution)/shard_map/ppermute | solution.py:278
  56.5 17.2 %collective-permute-start.13 = (bf16[128,1024]{1,0:T(8,128)(2,1)S(1)}, bf16[128,1024]{1,0:T(8,128)(2,1)S(1)}, u32[]{:S(2)}, u32[]{:S(2)}) collective-permute-start(bf16[128,1024]{1,0:T(8,128)(2,1)S(1)} %shard_map.109), channel_id=1, source_target_pairs={{0,2},{1,3},{6,4},{7,5},{8,10},{9,11},{14,12},{15,13},{16,18},{17,... | collective-permute-start | bytes 786440 | tf_op jit(solution)/shard_map/ppermute | solution.py:278
  57.9 13.4 %collective-permute-start.12 = (bf16[128,1024]{1,0:T(8,128)(2,1)S(1)}, bf16[128,1024]{1,0:T(8,128)(2,1)S(1)}, u32[]{:S(2)}, u32[]{:S(2)}) collective-permute-start(bf16[128,1024]{1,0:T(8,128)(2,1)S(1)} %shard_map.110), channel_id=1, source_target_pairs={{2,0},{3,1},{4,6},{5,7},{10,8},{11,9},{12,14},{13,15},{18,16},{19,... | collective-permute-start | bytes 786440 | tf_op jit(solution)/shard_map/ppermute | solution.py:278
  68.7 13.0 %collective-permute-start.16 = (bf16[128,1024]{1,0:T(8,128)(2,1)S(1)}, bf16[128,1024]{1,0:T(8,128)(2,1)S(1)}, u32[]{:S(2)}, u32[]{:S(2)}) collective-permute-start(bf16[128,1024]{1,0:T(8,128)(2,1)S(1)} %shard_map.111), channel_id=1, source_target_pairs={{0,2},{1,3},{6,4},{7,5},{8,10},{9,11},{14,12},{15,13},{16,18},{17,... | collective-permute-start | bytes 786440 | tf_op jit(solution)/shard_map/ppermute | solution.py:278

commit v6 on v4

--- a/solution.py
+++ b/solution.py
@@ -17,7 +17,7 @@
 LANES = 256
 WIDE = 512
 OWN, CROSS = 2, 2
-ORDER = [(0, 0, None), (1, 0, None), (0, 1, (1, 0)), (1, 1, (0, 1))]
+ORDER = [(0, 0, None), (1, 0, None), (0, 1, (1, 0)), (1, 1, None)]
 
 
 def odd_tables(length):

time: 83.6 us -> 83.6 us (level)
  no operation moved by 1% of the time
where the time goes in v6:
time: 83.6 us; the launch traced here: 83.2 us
  waiting for transfers between devices  34.4 us (41%)
  starting transfers between devices  26.9 us (32%)
  Pallas kernels  14.2 us (17%)
  local copies, waits for them, and re-layouts  7.34 us (9%)
    ppermute x4, starting transfers between devices, two_by_four(): groups += [*pairs[role][c], lax.ppermute(sums[role, c], ('ctx', 'mp'), far)]  14.7 us
    pallas_call x13, Pallas kernels, local(): pl.pallas_call(kernel, out_shape=out_shape, in_specs=[pl.BlockSpec(memory...  14.2 us
    ppermute x4, waiting for transfers between devices, two_by_four(): groups += [*pairs[role][c], lax.ppermute(sums[role, c], ('ctx', 'mp'), far)]  11.7 us
    ppermute x4, waiting for transfers between devices, to_next(): return lax.ppermute(array, ('section', 'ctx'), pairs)  9.11 us
    ppermute x2, waiting for transfers between devices, two_by_four(): lax.ppermute(piece, ('ctx', 'mp'), diagonal)  8.33 us
    unnamed x22, local copies, waits for them, and re-layouts  5.33 us
    ppermute x4, starting transfers between devices, to_next(): return lax.ppermute(array, ('section', 'ctx'), pairs)  3.42 us
    ppermute x2, starting transfers between devices, two_by_four(): own_near = [lax.ppermute(piece, 'mp', near) for piece in owned[:OWN]]  3.15 us
  transfers between devices with their start and end apart: 17, of which 11 were waited for; matrix products, arithmetic and copies ran while one was open for 1% of the time, Pallas kernels for 14%

profile of v6, /device:TPU:2, one launch (start us, length us, event | category | flops | bytes accessed | tf_op | source)
XLA Modules:
  0.0 83.2 jit_solution(8905790975650258213)
XLA Ops:
  0.0 1.0 %dynamic-slice_bitcast_fusion = bf16[256,512]{1,0:T(8,128)(2,1)S(1)} fusion(bf16[1,256,1024]{2,1,0:T(8,128)(2,1)} %own_ref.1, s32[]{:T(128)S(6)} %select_n.17), kind=kLoop, calls=%fused_computation | loop fusion | bytes 524292 | tf_op jit(solution)/shard_map/dynamic_slice | solution.py:210
  1.1 0.1 collective-permute-start.2
  1.2 0.1 pad_add_fusion.place
  1.2 1.0 %copy-done.2 = bf16[1,256,1024]{2,1,0:T(8,128)(2,1)S(1)} copy-done((bf16[1,256,1024]{2,1,0:T(8,128)(2,1)S(1)}, bf16[1,256,1024]{2,1,0:T(8,128)(2,1)}, u32[]{:S(2)}) %copy-start.2) | copy-done | bytes 524312
  2.3 1.0 %copy-done.3 = bf16[1,256,1024]{2,1,0:T(8,128)(2,1)S(1)} copy-done((bf16[1,256,1024]{2,1,0:T(8,128)(2,1)S(1)}, bf16[1,256,1024]{2,1,0:T(8,128)(2,1)}, u32[]{:S(2)}) %copy-start.3) | copy-done | bytes 524312
  3.3 0.8 copy-done.7
  4.1 0.9 %shard_map.101 = bf16[272,512]{1,0:T(8,128)(2,1)S(1)} custom-call(s32[3]{0:T(128)S(1)} %pad_add_fusion.place, bf16[1,256,1024]{2,1,0:T(8,128)(2,1)S(1)} %copy-done.2, bf16[1,256,1024]{2,1,0:T(8,128)(2,1)S(1)} %copy-done.3, f32[3,3,1,1024]{3,2,1,0:T(1,128)S(1)} %bitcast.8), custom_call_target="tpu_custom_call" | custom-call | flops 2621440 | bytes 1363980 | tf_op jit(solution)/shard_map/pallas_call | solution.py:180
  5.0 2.1 %collective-permute-start.1 = (bf16[272,512]{1,0:T(8,128)(2,1)S(1)}, bf16[272,512]{1,0:T(8,128)(2,1)S(1)}, u32[]{:S(2)}, u32[]{:S(2)}) collective-permute-start(bf16[272,512]{1,0:T(8,128)(2,1)S(1)} %shard_map.101), channel_id=1, source_target_pairs={{0,4},{4,0},{1,5},{5,1},{2,6},{6,2},{3,7},{7,3},{8,12},{12,8},{9,1... | collective-permute-start | bytes 835592 | tf_op jit(solution)/shard_map/ppermute | solution.py:215
  7.1 1.0 %dynamic-slice_bitcast_fusion.1 = bf16[256,512]{1,0:T(8,128)(2,1)S(1)} fusion(bf16[1,256,1024]{2,1,0:T(8,128)(2,1)} %current_ref.1, s32[]{:T(128)S(6)} %select_n.17), kind=kLoop, calls=%fused_computation.1 | loop fusion | bytes 524292 | tf_op jit(solution)/shard_map/dynamic_slice | solution.py:210
  8.0 0.1 collective-permute-start
  8.1 0.9 %shard_map.100.own_ref = bf16[272,512]{1,0:T(8,128)(2,1)S(1)} custom-call(s32[3]{0:T(128)S(1)} %pad_add_fusion.place, bf16[1,256,1024]{2,1,0:T(8,128)(2,1)S(1)} %copy-done.2, bf16[1,256,1024]{2,1,0:T(8,128)(2,1)S(1)} %copy-done.3, f32[3,3,1,1024]{3,2,1,0:T(1,128)S(1)} %bitcast.9), custom_call_target="tpu_custom_call" | custom-call | flops 2621440 | bytes 1363980 | tf_op jit(solution)/shard_map/pallas_call | solution.py:180
  9.1 1.3 %collective-permute-done.2.come_ref = bf16[256,512]{1,0:T(8,128)(2,1)S(1)} collective-permute-done((bf16[256,512]{1,0:T(8,128)(2,1)S(1)}, bf16[256,512]{1,0:T(8,128)(2,1)S(1)}, u32[]{:S(2)}, u32[]{:S(2)}) %collective-permute-start.2) | collective-permute-done | bytes 262176 | tf_op jit(solution)/shard_map/ppermute | solution.py:212
  10.3 1.2 %copy-done.5 = bf16[1024,512]{1,0:T(8,128)(2,1)S(1)} copy-done((bf16[1024,512]{1,0:T(8,128)(2,1)S(1)}, bf16[1024,512]{1,0:T(8,128)(2,1)}, u32[]{:S(2)}) %copy-start.5) | copy-done | bytes 1048600
  11.5 1.2 %copy-done.6 = bf16[1024,512]{1,0:T(8,128)(2,1)S(1)} copy-done((bf16[1024,512]{1,0:T(8,128)(2,1)S(1)}, bf16[1024,512]{1,0:T(8,128)(2,1)}, u32[]{:S(2)}) %copy-start.6) | copy-done | bytes 1048600
  12.8 1.8 %shard_map.102.spec_ref = f32[1024,512]{1,0:T(8,128)S(1)} custom-call(s32[3]{0:T(128)S(1)} %pad_add_fusion.place, bf16[1,256,1024]{2,1,0:T(8,128)(2,1)S(1)} %copy-done.4, bf16[256,512]{1,0:T(8,128)(2,1)S(1)} %collective-permute-done.2.come_ref, bf16[1024,512]{1,0:T(8,128)(2,1)S(1)} %copy-done.6, bf16[1024,512]{1,0:T(8,128)(2,1)S(1)} %copy-done.5), custom_call_target="tpu_custom_call" | custom-call | flops 1073741824 | bytes 4980748 | tf_op jit(solution)/shard_map/pallas_call | solution.py:180
  14.6 1.7 %collective-permute-done.1.come_ref = bf16[272,512]{1,0:T(8,128)(2,1)S(1)} collective-permute-done((bf16[272,512]{1,0:T(8,128)(2,1)S(1)}, bf16[272,512]{1,0:T(8,128)(2,1)S(1)}, u32[]{:S(2)}, u32[]{:S(2)}) %collective-permute-start.1) | collective-permute-done | bytes 278560 | tf_op jit(solution)/shard_map/ppermute | solution.py:215
  16.3 3.7 %shard_map.103.conv_ref = f32[512,512]{1,0:T(8,128)S(1)} custom-call(s32[3]{0:T(128)S(1)} %pad_add_fusion.place, bf16[272,512]{1,0:T(8,128)(2,1)S(1)} %shard_map.100.own_ref, bf16[272,512]{1,0:T(8,128)(2,1)S(1)} %collective-permute-done.1.come_ref, f32[3,3,1,1024]{3,2,1,0:T(1,128)S(1)} %bitcast.10, f32[1024,512]{1,0:T(8,128)S(1)} %shard_map.102.spec_ref, ...), custom_call_target="tpu_custom_call" | custom-call | flops 2684354560 | bytes 7933964 | tf_op jit(solution)/shard_map/pallas_call | solution.py:180
  20.0 0.7 collective-permute-done.current_ref.previous_ref
  20.8 0.7 shard_map.104
  21.5 0.1 collective-permute-start.6
  21.6 0.8 shard_map.105
  22.3 1.6 %collective-permute-start.5 = (bf16[256,512]{1,0:T(8,128)(2,1)S(1)}, bf16[256,512]{1,0:T(8,128)(2,1)S(1)}, u32[]{:S(2)}, u32[]{:S(2)}) collective-permute-start(bf16[256,512]{1,0:T(8,128)(2,1)S(1)} %shard_map.105), channel_id=1, source_target_pairs={{0,8},{4,12},{8,16},{12,20},{16,24},{20,28},{24,0},{28,4},{1,9},{5... | collective-permute-start | bytes 786440 | tf_op jit(solution)/shard_map/ppermute | solution.py:241
  24.0 0.1 collective-permute-start.3
  24.0 1.7 %collective-permute-start.4 = (bf16[256,512]{1,0:T(8,128)(2,1)S(1)}, bf16[256,512]{1,0:T(8,128)(2,1)S(1)}, u32[]{:S(2)}, u32[]{:S(2)}) collective-permute-start(bf16[256,512]{1,0:T(8,128)(2,1)S(1)} %shard_map.105), channel_id=1, source_target_pairs={{0,12},{4,8},{8,20},{12,16},{16,28},{20,24},{24,4},{28,0},{1,13},{... | collective-permute-start | bytes 786440 | tf_op jit(solution)/shard_map/ppermute | solution.py:241
  25.7 5.3 %collective-permute-done.6.cross_ref = bf16[256,512]{1,0:T(8,128)(2,1)S(1)} collective-permute-done((bf16[256,512]{1,0:T(8,128)(2,1)S(1)}, bf16[256,512]{1,0:T(8,128)(2,1)S(1)}, u32[]{:S(2)}, u32[]{:S(2)}) %collective-permute-start.6) | collective-permute-done | bytes 262176 | tf_op jit(solution)/shard_map/ppermute | solution.py:241
  31.0 1.8 %shard_map.106 = (bf16[128,1024]{1,0:T(8,128)(2,1)S(1)}, bf16[128,1024]{1,0:T(8,128)(2,1)S(1)}, f32[128,1024]{1,0:T(8,128)S(1)}, f32[128,1024]{1,0:T(8,128)S(1)}) custom-call(s32[3]{0:T(128)S(1)} %pad_add_fusion.place, bf16[256,512]{1,0:T(8,128)(2,1)S(1)} %collective-permute-done.5.same_ref, bf16[256,512]{1,0:T(8,128)(2,1)S(1)} %collective-permute-done.6.cross_ref, ...), custom_call_target="tpu_custom_call" | custom-call | flops 1073741824 | bytes 6291468 | tf_op jit(solution)/shard_map/pallas_call | solution.py:180
  32.8 3.8 %collective-permute-done.3.same_ref = bf16[256,512]{1,0:T(8,128)(2,1)S(1)} collective-permute-done((bf16[256,512]{1,0:T(8,128)(2,1)S(1)}, bf16[256,512]{1,0:T(8,128)(2,1)S(1)}, u32[]{:S(2)}, u32[]{:S(2)}) %collective-permute-start.3) | collective-permute-done | bytes 262176 | tf_op jit(solution)/shard_map/ppermute | solution.py:241
  36.6 1.6 %collective-permute-start.7 = (bf16[128,1024]{1,0:T(8,128)(2,1)S(1)}, bf16[128,1024]{1,0:T(8,128)(2,1)S(1)}, u32[]{:S(2)}, u32[]{:S(2)}) collective-permute-start(bf16[128,1024]{1,0:T(8,128)(2,1)S(1)} %get-tuple-element.26), channel_id=1, source_target_pairs={{0,1},{1,0},{2,3},{3,2},{4,5},{5,4},{6,7},{7,6},{8,9},{9,8},{10,11... | collective-permute-start | bytes 786440 | tf_op jit(solution)/shard_map/ppermute | solution.py:265
  38.2 1.8 %shard_map.108 = (bf16[128,1024]{1,0:T(8,128)(2,1)S(1)}, bf16[128,1024]{1,0:T(8,128)(2,1)S(1)}, bf16[128,1024]{1,0:T(8,128)(2,1)S(1)}, bf16[128,1024]{1,0:T(8,128)(2,1)S(1)}) custom-call(s32[3]{0:T(128)S(1)} %pad_add_fusion.place, bf16[256,512]{1,0:T(8,128)(2,1)S(1)} %collective-permute-done.3.same_ref, ...), custom_call_target="tpu_custom_call" | custom-call | flops 1073741824 | bytes 5767180 | tf_op jit(solution)/shard_map/pallas_call | solution.py:180
  40.0 0.7 collective-permute-start.10
  40.7 1.2 %collective-permute-start.11 = (bf16[128,1024]{1,0:T(8,128)(2,1)S(1)}, bf16[128,1024]{1,0:T(8,128)(2,1)S(1)}, u32[]{:S(2)}, u32[]{:S(2)}) collective-permute-start(bf16[128,1024]{1,0:T(8,128)(2,1)S(1)} %get-tuple-element.32), channel_id=1, source_target_pairs={{0,4},{4,0},{1,5},{5,1},{2,6},{6,2},{3,7},{7,3},{8,12},{12,8},{9,1... | collective-permute-start | bytes 786440 | tf_op jit(solution)/shard_map/ppermute | solution.py:267
  42.0 1.6 %collective-permute-start.9 = (bf16[128,1024]{1,0:T(8,128)(2,1)S(1)}, bf16[128,1024]{1,0:T(8,128)(2,1)S(1)}, u32[]{:S(2)}, u32[]{:S(2)}) collective-permute-start(bf16[128,1024]{1,0:T(8,128)(2,1)S(1)} %get-tuple-element.28), channel_id=1, source_target_pairs={{0,1},{1,0},{2,3},{3,2},{4,5},{5,4},{6,7},{7,6},{8,9},{9,8},{10,11... | collective-permute-start | bytes 786440 | tf_op jit(solution)/shard_map/ppermute | solution.py:265
  43.5 0.7 collective-permute-start.14
  44.2 1.6 %collective-permute-done.7.two_ref.refs_1_ = bf16[128,1024]{1,0:T(8,128)(2,1)S(1)} collective-permute-done((bf16[128,1024]{1,0:T(8,128)(2,1)S(1)}, bf16[128,1024]{1,0:T(8,128)(2,1)S(1)}, u32[]{:S(2)}, u32[]{:S(2)}) %collective-permute-start.7) | collective-permute-done | bytes 262176 | tf_op jit(solution)/shard_map/ppermute | solution.py:265
  45.9 0.8 collective-permute-start.15
  46.7 5.1 %collective-permute-done.10.one_ref.refs_6_ = bf16[128,1024]{1,0:T(8,128)(2,1)S(1)} collective-permute-done((bf16[128,1024]{1,0:T(8,128)(2,1)S(1)}, bf16[128,1024]{1,0:T(8,128)(2,1)S(1)}, u32[]{:S(2)}, u32[]{:S(2)}) %collective-permute-start.10) | collective-permute-done | bytes 262176 | tf_op jit(solution)/shard_map/ppermute | solution.py:266
  51.7 4.7 %collective-permute-start.8 = (bf16[128,1024]{1,0:T(8,128)(2,1)S(1)}, bf16[128,1024]{1,0:T(8,128)(2,1)S(1)}, u32[]{:S(2)}, u32[]{:S(2)}) collective-permute-start(bf16[128,1024]{1,0:T(8,128)(2,1)S(1)} %shard_map.107), channel_id=1, source_target_pairs={{2,0},{3,1},{4,6},{5,7},{10,8},{11,9},{12,14},{13,15},{18,16},{19,... | collective-permute-start | bytes 786440 | tf_op jit(solution)/shard_map/ppermute | solution.py:278
  56.5 0.1 shard_map.109
  56.5 1.3 %collective-permute-start.13 = (bf16[128,1024]{1,0:T(8,128)(2,1)S(1)}, bf16[128,1024]{1,0:T(8,128)(2,1)S(1)}, u32[]{:S(2)}, u32[]{:S(2)}) collective-permute-start(bf16[128,1024]{1,0:T(8,128)(2,1)S(1)} %shard_map.109), channel_id=1, source_target_pairs={{0,2},{1,3},{6,4},{7,5},{8,10},{9,11},{14,12},{15,13},{16,18},{17,... | collective-permute-start | bytes 786440 | tf_op jit(solution)/shard_map/ppermute | solution.py:278
  57.8 0.1 shard_map.110
  57.9 7.4 %collective-permute-start.12 = (bf16[128,1024]{1,0:T(8,128)(2,1)S(1)}, bf16[128,1024]{1,0:T(8,128)(2,1)S(1)}, u32[]{:S(2)}, u32[]{:S(2)}) collective-permute-start(bf16[128,1024]{1,0:T(8,128)(2,1)S(1)} %shard_map.110), channel_id=1, source_target_pairs={{2,0},{3,1},{4,6},{5,7},{10,8},{11,9},{12,14},{13,15},{18,16},{19,... | collective-permute-start | bytes 786440 | tf_op jit(solution)/shard_map/ppermute | solution.py:278
  65.3 3.3 %collective-permute-done.14.one_ref.refs_9_ = bf16[128,1024]{1,0:T(8,128)(2,1)S(1)} collective-permute-done((bf16[128,1024]{1,0:T(8,128)(2,1)S(1)}, bf16[128,1024]{1,0:T(8,128)(2,1)S(1)}, u32[]{:S(2)}, u32[]{:S(2)}) %collective-permute-start.14) | collective-permute-done | bytes 262176 | tf_op jit(solution)/shard_map/ppermute | solution.py:266
  68.6 0.1 shard_map.111
  68.7 1.3 %collective-permute-start.16 = (bf16[128,1024]{1,0:T(8,128)(2,1)S(1)}, bf16[128,1024]{1,0:T(8,128)(2,1)S(1)}, u32[]{:S(2)}, u32[]{:S(2)}) collective-permute-start(bf16[128,1024]{1,0:T(8,128)(2,1)S(1)} %shard_map.111), channel_id=1, source_target_pairs={{0,2},{1,3},{6,4},{7,5},{8,10},{9,11},{14,12},{15,13},{16,18},{17,... | collective-permute-start | bytes 786440 | tf_op jit(solution)/shard_map/ppermute | solution.py:278
  70.0 1.3 %collective-permute-done.12.refs_5_ = bf16[128,1024]{1,0:T(8,128)(2,1)S(1)} collective-permute-done((bf16[128,1024]{1,0:T(8,128)(2,1)S(1)}, bf16[128,1024]{1,0:T(8,128)(2,1)S(1)}, u32[]{:S(2)}, u32[]{:S(2)}) %collective-permute-start.12) | collective-permute-done | bytes 262176 | tf_op jit(solution)/shard_map/ppermute | solution.py:278
  71.3 2.5 %collective-permute-done.13.refs_8_ = bf16[128,1024]{1,0:T(8,128)(2,1)S(1)} collective-permute-done((bf16[128,1024]{1,0:T(8,128)(2,1)S(1)}, bf16[128,1024]{1,0:T(8,128)(2,1)S(1)}, u32[]{:S(2)}, u32[]{:S(2)}) %collective-permute-start.13) | collective-permute-done | bytes 262176 | tf_op jit(solution)/shard_map/ppermute | solution.py:278
  73.8 7.9 %collective-permute-done.16.refs_11_ = bf16[128,1024]{1,0:T(8,128)(2,1)S(1)} collective-permute-done((bf16[128,1024]{1,0:T(8,128)(2,1)S(1)}, bf16[128,1024]{1,0:T(8,128)(2,1)S(1)}, u32[]{:S(2)}, u32[]{:S(2)}) %collective-permute-start.16) | collective-permute-done | bytes 262176 | tf_op jit(solution)/shard_map/ppermute | solution.py:278
  81.6 1.5 %shard_map.112 = bf16[1,256,1024]{2,1,0:T(8,128)(2,1)} custom-call(s32[3]{0:T(128)S(1)} %pad_add_fusion.place, f32[128,1024]{1,0:T(8,128)S(1)} %get-tuple-element.25.one_ref.refs_0_, bf16[128,1024]{1,0:T(8,128)(2,1)S(1)} %collective-permute-done.7.two_ref.refs_1_, bf16[128,1024]{1,0:T(8,128)(2,1)S(1)} %collective-permute-done.8.refs_2_, ...), custom_call_target="tpu_custom_call" | custom-call | flops 786432 | bytes 4194316 | tf_op jit(solution)/shard_map/pallas_call | solution.py:180
  (24 shorter events, 0.1 us)
Async XLA Ops:
  0.0 10.3 %copy-start.4 = (bf16[1,256,1024]{2,1,0:T(8,128)(2,1)S(1)}, bf16[1,256,1024]{2,1,0:T(8,128)(2,1)}, u32[]{:S(2)}) copy-start(bf16[1,256,1024]{2,1,0:T(8,128)(2,1)} %own_ref.1) | copy-start | bytes 1572868
  1.0 15.2 %copy-start.8 = (f32[1,3,3,1024]{3,0,2,1:T(1,128)S(1)}, f32[1,3,3,1024]{3,0,2,1:T(1,128)}, u32[]{:S(2)}) copy-start(f32[1,3,3,1024]{3,0,2,1:T(1,128)} %param.14) | copy-start | bytes 110596
  1.1 9.3 %collective-permute-start.2 = (bf16[256,512]{1,0:T(8,128)(2,1)S(1)}, bf16[256,512]{1,0:T(8,128)(2,1)S(1)}, u32[]{:S(2)}, u32[]{:S(2)}) collective-permute-start(bf16[256,512]{1,0:T(8,128)(2,1)S(1)} %dynamic-slice_bitcast_fusion), channel_id=1, source_target_pairs={{0,4},{4,0},{1,5},{5,1},{2,6},{6,2},{3,7},{7,3},{8,12},{12,8},{9,1... | collective-permute-start | bytes 786440 | tf_op jit(solution)/shard_map/ppermute | solution.py:212
  1.2 1.0 %copy-start.2 = (bf16[1,256,1024]{2,1,0:T(8,128)(2,1)S(1)}, bf16[1,256,1024]{2,1,0:T(8,128)(2,1)}, u32[]{:S(2)}) copy-start(bf16[1,256,1024]{2,1,0:T(8,128)(2,1)} %key_ref.3) | copy-start | bytes 1572868
  2.3 1.0 %copy-start.3 = (bf16[1,256,1024]{2,1,0:T(8,128)(2,1)S(1)}, bf16[1,256,1024]{2,1,0:T(8,128)(2,1)}, u32[]{:S(2)}) copy-start(bf16[1,256,1024]{2,1,0:T(8,128)(2,1)} %value_ref.3) | copy-start | bytes 1572868
  3.3 0.8 copy-start.7
  4.1 12.2 %copy-start.9 = (bf16[512,1024]{1,0:T(8,128)(2,1)S(1)}, bf16[512,1024]{1,0:T(8,128)(2,1)}, u32[]{:S(2)}) copy-start(bf16[512,1024]{1,0:T(8,128)(2,1)} %constant.52.clone.back_low_ref) | copy-start | bytes 3145732
  4.1 12.2 %copy-start.10 = (bf16[512,1024]{1,0:T(8,128)(2,1)S(1)}, bf16[512,1024]{1,0:T(8,128)(2,1)}, u32[]{:S(2)}) copy-start(bf16[512,1024]{1,0:T(8,128)(2,1)} %constant.51.clone.back_high_ref) | copy-start | bytes 3145732
  5.0 11.3 %collective-permute-start.1 = (bf16[272,512]{1,0:T(8,128)(2,1)S(1)}, bf16[272,512]{1,0:T(8,128)(2,1)S(1)}, u32[]{:S(2)}, u32[]{:S(2)}) collective-permute-start(bf16[272,512]{1,0:T(8,128)(2,1)S(1)} %shard_map.101), channel_id=1, source_target_pairs={{0,4},{4,0},{1,5},{5,1},{2,6},{6,2},{3,7},{7,3},{8,12},{12,8},{9,1... | collective-permute-start | bytes 835592 | tf_op jit(solution)/shard_map/ppermute | solution.py:215
  8.0 12.7 %collective-permute-start = (bf16[256,512]{1,0:T(8,128)(2,1)S(1)}, bf16[256,512]{1,0:T(8,128)(2,1)S(1)}, u32[]{:S(2)}, u32[]{:S(2)}) collective-permute-start(bf16[256,512]{1,0:T(8,128)(2,1)S(1)} %dynamic-slice_bitcast_fusion.1), channel_id=1, source_target_pairs={{0,4},{4,0},{1,5},{5,1},{2,6},{6,2},{3,7},{7,3},{8,12},{12,8},{9,1... | collective-permute-start | bytes 786440 | tf_op jit(solution)/shard_map/ppermute | solution.py:216
  10.3 1.2 %copy-start.5 = (bf16[1024,512]{1,0:T(8,128)(2,1)S(1)}, bf16[1024,512]{1,0:T(8,128)(2,1)}, u32[]{:S(2)}) copy-start(bf16[1024,512]{1,0:T(8,128)(2,1)} %constant.50.clone.low_ref) | copy-start | bytes 3145732
  11.5 1.2 %copy-start.6 = (bf16[1024,512]{1,0:T(8,128)(2,1)S(1)}, bf16[1024,512]{1,0:T(8,128)(2,1)}, u32[]{:S(2)}) copy-start(bf16[1024,512]{1,0:T(8,128)(2,1)} %constant.49.clone.high_ref) | copy-start | bytes 3145732
  14.6 6.2 %copy-start.1 = (bf16[1,256,1024]{2,1,0:T(8,128)(2,1)S(1)}, bf16[1,256,1024]{2,1,0:T(8,128)(2,1)}, u32[]{:S(2)}) copy-start(bf16[1,256,1024]{2,1,0:T(8,128)(2,1)} %current_ref.1) | copy-start | bytes 1572868
  20.0 11.0 %copy-start = (bf16[1,1024,2048]{2,1,0:T(8,128)(2,1)S(1)}, bf16[1,1024,2048]{2,1,0:T(8,128)(2,1)}, u32[]{:S(2)}) copy-start(bf16[1,1024,2048]{2,1,0:T(8,128)(2,1)} %weight_ref.3) | copy-start | bytes 12582916
  21.5 9.5 %collective-permute-start.6 = (bf16[256,512]{1,0:T(8,128)(2,1)S(1)}, bf16[256,512]{1,0:T(8,128)(2,1)S(1)}, u32[]{:S(2)}, u32[]{:S(2)}) collective-permute-start(bf16[256,512]{1,0:T(8,128)(2,1)S(1)} %shard_map.104), channel_id=1, source_target_pairs={{0,12},{4,8},{8,20},{12,16},{16,28},{20,24},{24,4},{28,0},{1,13},{... | collective-permute-start | bytes 786440 | tf_op jit(solution)/shard_map/ppermute | solution.py:241
  22.3 8.7 %collective-permute-start.5 = (bf16[256,512]{1,0:T(8,128)(2,1)S(1)}, bf16[256,512]{1,0:T(8,128)(2,1)S(1)}, u32[]{:S(2)}, u32[]{:S(2)}) collective-permute-start(bf16[256,512]{1,0:T(8,128)(2,1)S(1)} %shard_map.105), channel_id=1, source_target_pairs={{0,8},{4,12},{8,16},{12,20},{16,24},{20,28},{24,0},{28,4},{1,9},{5... | collective-permute-start | bytes 786440 | tf_op jit(solution)/shard_map/ppermute | solution.py:241
  24.0 12.6 %collective-permute-start.3 = (bf16[256,512]{1,0:T(8,128)(2,1)S(1)}, bf16[256,512]{1,0:T(8,128)(2,1)S(1)}, u32[]{:S(2)}, u32[]{:S(2)}) collective-permute-start(bf16[256,512]{1,0:T(8,128)(2,1)S(1)} %shard_map.104), channel_id=1, source_target_pairs={{0,8},{4,12},{8,16},{12,20},{16,24},{20,28},{24,0},{28,4},{1,9},{5... | collective-permute-start | bytes 786440 | tf_op jit(solution)/shard_map/ppermute | solution.py:241
  24.0 12.6 %collective-permute-start.4 = (bf16[256,512]{1,0:T(8,128)(2,1)S(1)}, bf16[256,512]{1,0:T(8,128)(2,1)S(1)}, u32[]{:S(2)}, u32[]{:S(2)}) collective-permute-start(bf16[256,512]{1,0:T(8,128)(2,1)S(1)} %shard_map.105), channel_id=1, source_target_pairs={{0,12},{4,8},{8,20},{12,16},{16,28},{20,24},{24,4},{28,0},{1,13},{... | collective-permute-start | bytes 786440 | tf_op jit(solution)/shard_map/ppermute | solution.py:241
  36.6 9.2 %collective-permute-start.7 = (bf16[128,1024]{1,0:T(8,128)(2,1)S(1)}, bf16[128,1024]{1,0:T(8,128)(2,1)S(1)}, u32[]{:S(2)}, u32[]{:S(2)}) collective-permute-start(bf16[128,1024]{1,0:T(8,128)(2,1)S(1)} %get-tuple-element.26), channel_id=1, source_target_pairs={{0,1},{1,0},{2,3},{3,2},{4,5},{5,4},{6,7},{7,6},{8,9},{9,8},{10,11... | collective-permute-start | bytes 786440 | tf_op jit(solution)/shard_map/ppermute | solution.py:265
  40.0 11.7 %collective-permute-start.10 = (bf16[128,1024]{1,0:T(8,128)(2,1)S(1)}, bf16[128,1024]{1,0:T(8,128)(2,1)S(1)}, u32[]{:S(2)}, u32[]{:S(2)}) collective-permute-start(bf16[128,1024]{1,0:T(8,128)(2,1)S(1)} %get-tuple-element.31), channel_id=1, source_target_pairs={{0,5},{1,4},{2,7},{3,6},{4,1},{5,0},{6,3},{7,2},{8,13},{9,12},{10,... | collective-permute-start | bytes 786440 | tf_op jit(solution)/shard_map/ppermute | solution.py:266
  40.7 15.7 %collective-permute-start.11 = (bf16[128,1024]{1,0:T(8,128)(2,1)S(1)}, bf16[128,1024]{1,0:T(8,128)(2,1)S(1)}, u32[]{:S(2)}, u32[]{:S(2)}) collective-permute-start(bf16[128,1024]{1,0:T(8,128)(2,1)S(1)} %get-tuple-element.32), channel_id=1, source_target_pairs={{0,4},{4,0},{1,5},{5,1},{2,6},{6,2},{3,7},{7,3},{8,12},{12,8},{9,1... | collective-permute-start | bytes 786440 | tf_op jit(solution)/shard_map/ppermute | solution.py:267
  42.0 15.9 %collective-permute-start.9 = (bf16[128,1024]{1,0:T(8,128)(2,1)S(1)}, bf16[128,1024]{1,0:T(8,128)(2,1)S(1)}, u32[]{:S(2)}, u32[]{:S(2)}) collective-permute-start(bf16[128,1024]{1,0:T(8,128)(2,1)S(1)} %get-tuple-element.28), channel_id=1, source_target_pairs={{0,1},{1,0},{2,3},{3,2},{4,5},{5,4},{6,7},{7,6},{8,9},{9,8},{10,11... | collective-permute-start | bytes 786440 | tf_op jit(solution)/shard_map/ppermute | solution.py:265
  43.5 25.0 %collective-permute-start.14 = (bf16[128,1024]{1,0:T(8,128)(2,1)S(1)}, bf16[128,1024]{1,0:T(8,128)(2,1)S(1)}, u32[]{:S(2)}, u32[]{:S(2)}) collective-permute-start(bf16[128,1024]{1,0:T(8,128)(2,1)S(1)} %get-tuple-element.35), channel_id=1, source_target_pairs={{0,5},{1,4},{2,7},{3,6},{4,1},{5,0},{6,3},{7,2},{8,13},{9,12},{10,... | collective-permute-start | bytes 786440 | tf_op jit(solution)/shard_map/ppermute | solution.py:266
  45.9 22.7 %collective-permute-start.15 = (bf16[128,1024]{1,0:T(8,128)(2,1)S(1)}, bf16[128,1024]{1,0:T(8,128)(2,1)S(1)}, u32[]{:S(2)}, u32[]{:S(2)}) collective-permute-start(bf16[128,1024]{1,0:T(8,128)(2,1)S(1)} %get-tuple-element.36), channel_id=1, source_target_pairs={{0,4},{4,0},{1,5},{5,1},{2,6},{6,2},{3,7},{7,3},{8,12},{12,8},{9,1... | collective-permute-start | bytes 786440 | tf_op jit(solution)/shard_map/ppermute | solution.py:267
  51.7 18.2 %collective-permute-start.8 = (bf16[128,1024]{1,0:T(8,128)(2,1)S(1)}, bf16[128,1024]{1,0:T(8,128)(2,1)S(1)}, u32[]{:S(2)}, u32[]{:S(2)}) collective-permute-start(bf16[128,1024]{1,0:T(8,128)(2,1)S(1)} %shard_map.107), channel_id=1, source_target_pairs={{2,0},{3,1},{4,6},{5,7},{10,8},{11,9},{12,14},{13,15},{18,16},{19,... | collective-permute-start | bytes 786440 | tf_op jit(solution)/shard_map/ppermute | solution.py:278
  56.5 17.2 %collective-permute-start.13 = (bf16[128,1024]{1,0:T(8,128)(2,1)S(1)}, bf16[128,1024]{1,0:T(8,128)(2,1)S(1)}, u32[]{:S(2)}, u32[]{:S(2)}) collective-permute-start(bf16[128,1024]{1,0:T(8,128)(2,1)S(1)} %shard_map.109), channel_id=1, source_target_pairs={{0,2},{1,3},{6,4},{7,5},{8,10},{9,11},{14,12},{15,13},{16,18},{17,... | collective-permute-start | bytes 786440 | tf_op jit(solution)/shard_map/ppermute | solution.py:278
  57.9 13.4 %collective-permute-start.12 = (bf16[128,1024]{1,0:T(8,128)(2,1)S(1)}, bf16[128,1024]{1,0:T(8,128)(2,1)S(1)}, u32[]{:S(2)}, u32[]{:S(2)}) collective-permute-start(bf16[128,1024]{1,0:T(8,128)(2,1)S(1)} %shard_map.110), channel_id=1, source_target_pairs={{2,0},{3,1},{4,6},{5,7},{10,8},{11,9},{12,14},{13,15},{18,16},{19,... | collective-permute-start | bytes 786440 | tf_op jit(solution)/shard_map/ppermute | solution.py:278
  68.7 13.0 %collective-permute-start.16 = (bf16[128,1024]{1,0:T(8,128)(2,1)S(1)}, bf16[128,1024]{1,0:T(8,128)(2,1)S(1)}, u32[]{:S(2)}, u32[]{:S(2)}) collective-permute-start(bf16[128,1024]{1,0:T(8,128)(2,1)S(1)} %shard_map.111), channel_id=1, source_target_pairs={{0,2},{1,3},{6,4},{7,5},{8,10},{9,11},{14,12},{15,13},{16,18},{17,... | collective-permute-start | bytes 786440 | tf_op jit(solution)/shard_map/ppermute | solution.py:278
